TPU v7x, 32 devices: a whole 2x2x4 slice. The times are simulated.
32 devices in a mesh: space: 8 (over z, y), chaos: 4 (over x, core).
Axes of the slice: x: 2, y: 2, z: 4, core: 2. Of those that a mesh axis runs over, the one named last changes fastest.
Arguments:
- load_vectors: bfloat16 [256, 2, 16, 3072], P('chaos', None, None, 'space'), may hold values from -6 to 6
- stiff_tiles: bfloat16 [32, 3, 8, 2, 96, 96], P('space'), may hold values from -0.09375 to 0.09375
- tile_columns: int32 [32, 3], P('space'), may hold values from 0 to 5, as said below
- chaos_index: int32 [8, 256, 32], replicated, may hold values from 0 to 255, as said below
- chaos_value: bfloat16 [8, 256, 32], replicated, may hold values from -1 to 1
Outputs:
- response: float32 [256, 2, 16, 3072], P('chaos', None, None, 'space')
Inputs may be any that keep to these rules, and one draw needn't show every extreme that they name: `tile_columns`: in row b of one subdomain with local index l = b % 4, the three numbers are l + 1, one of 0 to l, and one of l + 2 to 5. `chaos_index`: for every k and i the 32 numbers are distinct and the first is i.
All inputs are finite; a program needn't handle non-finite values.
Results may differ from a plain program's by a relative error of at most 0.0029.
Values may be sent and summed in bfloat16 or wider, within the bound.
No kernel may reach another device: no remote copies, remote signals or barrier semaphores. Data moves between devices by JAX's collectives and lax.ppermute only.
A program may use at most 128 MiB of HBM per device.

v0:
```python
import jax
import jax.numpy as jnp
from jax import lax
from jax.sharding import PartitionSpec as P

TILE = 96
NKL = 8
P_SIZE = 256


def with_halo(cells, sides, width):
    for axis, dim in sides:
        count = lax.axis_size(axis)
        ends = count - 1
        head = lax.slice_in_dim(cells, 0, width, axis=dim)
        tail = lax.slice_in_dim(cells, cells.shape[dim] - width, cells.shape[dim], axis=dim)
        cells = jnp.concatenate(
            [
                lax.ppermute(tail, axis, [(i, (i + 1) % count) for i in range(ends)]),
                cells,
                lax.ppermute(head, axis, [((i + 1) % count, i) for i in range(ends)]),
            ],
            axis=dim,
        )
    return cells


def dense_coupling(chaos_index, chaos_value):
    columns = jnp.arange(P_SIZE, dtype=jnp.int32)

    def one_term(index_pair):
        row_index, row_value = index_pair
        matches = row_index[:, :, None] == columns[None, None, :]
        summed = jnp.where(matches, row_value[:, :, None], jnp.zeros((), jnp.bfloat16)).sum(axis=1)
        return summed

    return lax.map(one_term, (chaos_index, chaos_value))


def body(load_vectors, stiff_tiles, tile_columns, chaos_index, chaos_value):
    extended = with_halo(load_vectors, (("space", 3),), TILE)
    blocks = stiff_tiles.shape[0]
    all_terms = lax.all_to_all(extended, "chaos", split_axis=2, concat_axis=0, tiled=True)
    coupling = dense_coupling(chaos_index, chaos_value)
    coupled_field = jnp.einsum(
        "kij,jcrd->kicrd", coupling, all_terms, preferred_element_type=jnp.float32
    ).astype(jnp.bfloat16)
    terms = coupled_field.shape[1]
    cases = coupled_field.shape[3]
    coupled_field = coupled_field.reshape(NKL, terms, 2, cases, blocks + 2, TILE)
    real_part = stiff_tiles[:, :, :, 0]
    imag_part = stiff_tiles[:, :, :, 1]
    upper_row = jnp.stack([real_part, -imag_part], axis=3)
    lower_row = jnp.stack([imag_part, real_part], axis=3)
    complex_tiles = jnp.stack([upper_row, lower_row], axis=3)
    accum_sum = jnp.zeros((terms, 2, cases, blocks, TILE), jnp.float32)
    for tile_slot in range(stiff_tiles.shape[1]):
        columns = jnp.take(coupled_field, tile_columns[:, tile_slot], axis=4)
        accum_sum = accum_sum + jnp.einsum(
            "bkcdxy,kidrby->icrbx",
            complex_tiles[:, tile_slot],
            columns,
            preferred_element_type=jnp.float32,
        )
    result = accum_sum.reshape(terms, 2, cases, blocks * TILE)
    result = lax.all_to_all(result, "chaos", split_axis=0, concat_axis=2, tiled=True)
    return result


def solution(mesh):
    in_specs = (
        P("chaos", None, None, "space"),
        P("space", None, None, None, None, None),
        P("space", None),
        P(),
        P(),
    )
    out_specs = P("chaos", None, None, "space")
    return jax.shard_map(body, mesh=mesh, in_specs=in_specs, out_specs=out_specs, check_vma=False)
```

profile of v0, /device:TPU:0, one launch (start us, length us, event | category | flops | bytes accessed | tf_op | source)
XLA Modules:
  0.0 234.9 jit_solution(17241861360851474832)
XLA Ops:
  0.0 2.3 fusion.33
  2.3 1.3 collective-permute-start.1
  3.6 5.5 %collective-permute-start = (bf16[64,2,16,96]{3,2,1,0:T(8,128)(2,1)S(1)}, bf16[64,2,16,96]{3,2,1,0:T(8,128)(2,1)S(1)}, u32[]{:S(2)}, u32[]{:S(2)}) collective-permute-start(bf16[64,2,16,96]{3,2,1,0:T(8,128)(2,1)S(1)} %get-tuple-element.97), channel_id=1, source_target_pairs={{0,4},{4,8},{8,12},{12,16},{16,20},{20,24},{24,28},{1,5},{5,9},{9,... | collective-permute-start | bytes 1179656 | tf_op jit(solution)/shard_map/ppermute | solution.py:19
  9.1 41.8 %while.13 = (s32[]{:T(128)}, bf16[8,256,256]{2,1,0:T(8,128)(2,1)}, s32[8,256,32]{1,2,0:T(8,128)}, bf16[8,256,32]{1,2,0:T(8,128)(2,1)}, s32[]{:T(128)}) while((s32[]{:T(128)}, bf16[8,256,256]{2,1,0:T(8,128)(2,1)}, s32[8,256,32]{1,2,0:T(8,128)}, bf16[8,256,32]{1,2,0:T(8,128)(2,1)}, s32[]{:T(128)}) %tuple.38), condition=%wide.region_2.3_spmd.clone, body=%wide.region_0.2_spmd.clone.sunk | while | flops 6225922 | bytes 639057 | solution.py:37
  9.2 0.8 dynamic-slice_bitcast_fusion.4
  10.0 0.7 dynamic-slice_bitcast_fusion.5
  10.9 2.8 %fusion.43 = bf16[256,256]{1,0:T(8,128)(2,1)S(1)} fusion(s32[256,32]{1,0:T(8,128)S(1)} %copy.121, bf16[256,32]{1,0:T(8,128)(2,1)S(1)} %copy.122), kind=kLoop, calls=%fused_computation.9.clone.1 | loop fusion | flops 6225920 | bytes 180224 | tf_op jit(solution)/shard_map/while/body/eval_jaxpr/reduce_sum | solution.py:34
  13.7 0.7 bitcast_dynamic-update-slice_fusion.2
  14.4 0.8 dynamic-slice_bitcast_fusion.4
  15.2 0.7 dynamic-slice_bitcast_fusion.5
  16.0 0.1 copy.122
  16.1 2.8 %fusion.43 = bf16[256,256]{1,0:T(8,128)(2,1)S(1)} fusion(s32[256,32]{1,0:T(8,128)S(1)} %copy.121, bf16[256,32]{1,0:T(8,128)(2,1)S(1)} %copy.122), kind=kLoop, calls=%fused_computation.9.clone.1 | loop fusion | flops 6225920 | bytes 180224 | tf_op jit(solution)/shard_map/while/body/eval_jaxpr/reduce_sum | solution.py:34
  18.9 0.7 bitcast_dynamic-update-slice_fusion.2
  19.6 0.8 dynamic-slice_bitcast_fusion.4
  20.5 0.7 dynamic-slice_bitcast_fusion.5
  21.3 2.8 %fusion.43 = bf16[256,256]{1,0:T(8,128)(2,1)S(1)} fusion(s32[256,32]{1,0:T(8,128)S(1)} %copy.121, bf16[256,32]{1,0:T(8,128)(2,1)S(1)} %copy.122), kind=kLoop, calls=%fused_computation.9.clone.1 | loop fusion | flops 6225920 | bytes 180224 | tf_op jit(solution)/shard_map/while/body/eval_jaxpr/reduce_sum | solution.py:34
  24.2 0.7 bitcast_dynamic-update-slice_fusion.2
  24.8 0.8 dynamic-slice_bitcast_fusion.4
  25.7 0.7 dynamic-slice_bitcast_fusion.5
  26.5 2.8 %fusion.43 = bf16[256,256]{1,0:T(8,128)(2,1)S(1)} fusion(s32[256,32]{1,0:T(8,128)S(1)} %copy.121, bf16[256,32]{1,0:T(8,128)(2,1)S(1)} %copy.122), kind=kLoop, calls=%fused_computation.9.clone.1 | loop fusion | flops 6225920 | bytes 180224 | tf_op jit(solution)/shard_map/while/body/eval_jaxpr/reduce_sum | solution.py:34
  29.4 0.7 bitcast_dynamic-update-slice_fusion.2
  30.1 0.8 dynamic-slice_bitcast_fusion.4
  30.9 0.7 dynamic-slice_bitcast_fusion.5
  31.8 2.8 %fusion.43 = bf16[256,256]{1,0:T(8,128)(2,1)S(1)} fusion(s32[256,32]{1,0:T(8,128)S(1)} %copy.121, bf16[256,32]{1,0:T(8,128)(2,1)S(1)} %copy.122), kind=kLoop, calls=%fused_computation.9.clone.1 | loop fusion | flops 6225920 | bytes 180224 | tf_op jit(solution)/shard_map/while/body/eval_jaxpr/reduce_sum | solution.py:34
  34.6 0.7 bitcast_dynamic-update-slice_fusion.2
  35.3 0.8 dynamic-slice_bitcast_fusion.4
  36.2 0.7 dynamic-slice_bitcast_fusion.5
  37.0 2.8 %fusion.43 = bf16[256,256]{1,0:T(8,128)(2,1)S(1)} fusion(s32[256,32]{1,0:T(8,128)S(1)} %copy.121, bf16[256,32]{1,0:T(8,128)(2,1)S(1)} %copy.122), kind=kLoop, calls=%fused_computation.9.clone.1 | loop fusion | flops 6225920 | bytes 180224 | tf_op jit(solution)/shard_map/while/body/eval_jaxpr/reduce_sum | solution.py:34
  39.9 0.7 bitcast_dynamic-update-slice_fusion.2
  40.5 0.8 dynamic-slice_bitcast_fusion.4
  41.4 0.7 dynamic-slice_bitcast_fusion.5
  42.1 0.1 copy.122
  42.2 2.8 %fusion.43 = bf16[256,256]{1,0:T(8,128)(2,1)S(1)} fusion(s32[256,32]{1,0:T(8,128)S(1)} %copy.121, bf16[256,32]{1,0:T(8,128)(2,1)S(1)} %copy.122), kind=kLoop, calls=%fused_computation.9.clone.1 | loop fusion | flops 6225920 | bytes 180224 | tf_op jit(solution)/shard_map/while/body/eval_jaxpr/reduce_sum | solution.py:34
  45.1 0.7 bitcast_dynamic-update-slice_fusion.2
  45.8 0.8 dynamic-slice_bitcast_fusion.4
  46.6 0.7 dynamic-slice_bitcast_fusion.5
  47.5 2.8 %fusion.43 = bf16[256,256]{1,0:T(8,128)(2,1)S(1)} fusion(s32[256,32]{1,0:T(8,128)S(1)} %copy.121, bf16[256,32]{1,0:T(8,128)(2,1)S(1)} %copy.122), kind=kLoop, calls=%fused_computation.9.clone.1 | loop fusion | flops 6225920 | bytes 180224 | tf_op jit(solution)/shard_map/while/body/eval_jaxpr/reduce_sum | solution.py:34
  50.3 0.7 bitcast_dynamic-update-slice_fusion.2
  51.0 0.2 slice_reduce_fusion.2
  51.2 1.5 pad_maximum_fusion.2
  52.7 2.4 %copy.72 = bf16[64,2,16,576]{3,0,1,2:T(8,128)(2,1)} copy(bf16[64,2,16,576]{3,2,1,0:T(8,128)(2,1)S(1)} %pad_maximum_fusion.2) | data formatting | bytes 4718592 | tf_op jit(solution)/shard_map/concatenate | solution.py:17
  55.1 3.8 %all-to-all-start = ((bf16[64,2,16,576]{3,0,1,2:T(8,128)(2,1)}), bf16[64,2,16,576]{3,0,1,2:T(8,128)(2,1)S(1)}, u32[]{:S(2)}, u32[]{:S(2)}) async-start(bf16[64,2,16,576]{3,0,1,2:T(8,128)(2,1)} %copy.72), calls=%async_computation | async-start | bytes 5242880 | tf_op jit(solution)/shard_map/all_to_all | solution.py:43
  59.0 3.3 %fusion.32 = (bf16[4,3,8,1,96,96]{5,4,3,2,1,0:T(8,128)(2,1)S(1)}, bf16[4,3,8,1,96,96]{5,4,3,2,1,0:T(8,128)(2,1)S(1)}) fusion(bf16[4,3,8,2,96,96]{5,4,3,2,1,0:T(8,128)(2,1)} %param.10), kind=kLoop, calls=%fused_computation.62 | loop fusion | bytes 7077888 | tf_op jit(solution)/shard_map/slice | solution.py:52
  62.3 0.3 copy_negate_fusion
  62.6 4.9 %maximum_bitcast_fusion = (bf16[4,3,8,1,2,96,96]{6,5,2,4,3,0,1:T(8,128)(2,1)}, bf16[4,3,8,1,2,96,96]{6,5,2,4,3,0,1:T(8,128)(2,1)}) fusion(bf16[4,3,8,1,96,96]{5,4,2,3,0,1:T(8,128)(2,1)S(1)} %copy_negate_fusion, bf16[4,3,8,1,96,96]{5,4,3,2,1,0:T(8,128)(2,1)S(1)} %get-tuple-element.96, bf16[4,3,8,1,96,96]{5,4,3,2,1,0:T(8,128)(2,1)S(1)} %get-tuple-element.95), kind=kLoop, calls=%fused_computation.30 | loop fusion | flops 8847360 | bytes 12386304 | tf_op jit(solution)/shard_map/stack | solution.py:55
  67.4 22.6 %all-to-all-done = bf16[64,2,16,576]{3,0,1,2:T(8,128)(2,1)S(1)} async-done(((bf16[64,2,16,576]{3,0,1,2:T(8,128)(2,1)}), bf16[64,2,16,576]{3,0,1,2:T(8,128)(2,1)S(1)}, u32[]{:S(2)}, u32[]{:S(2)}) %all-to-all-start) | async-done | bytes 2359328 | tf_op jit(solution)/shard_map/all_to_all | solution.py:43
  90.1 0.3 copy.73
  90.3 10.4 %convolution_convert_fusion = bf16[8,256,2,4,576]{1,4,3,2,0:T(8,128)(2,1)} fusion(bf16[256,2,4,576,1]{3,0,2,1,4:T(8,128)(2,1)S(1)} %bitcast.107, bf16[8,256,256]{2,1,0:T(8,128)(2,1)} %get-tuple-element.71), kind=kOutput, calls=%fused_computation.25 | convolution fusion | flops 4841275392 | bytes 22282240 | tf_op jit(solution)/shard_map/kij,jcrd->kicrd/dot_general | solution.py:45
  100.8 13.6 %fusion.31 = (bf16[8,128,2,4,6,96]{1,5,4,3,2,0:T(8,128)(2,1)}, bf16[8,128,2,4,6,96]{1,5,4,3,2,0:T(8,128)(2,1)}) fusion(bf16[8,256,2,4,6,96]{1,5,4,3,2,0:T(8,128)(2,1)} %bitcast.92), kind=kLoop, calls=%fused_computation.61 | loop fusion | bytes 37748736 | tf_op jit(solution)/shard_map/jit(_take)/gather | solution.py:58
  114.3 7.7 %gather_fusion.5 = bf16[4,8,128,2,4,96]{2,5,4,3,1,0:T(8,128)(2,1)} fusion(bf16[8,128,2,4,6,96]{1,5,4,3,2,0:T(8,128)(2,1)} %get-tuple-element.94, s32[1024]{0:T(1024)S(1)} %pad_clamp_fusion), kind=kCustom, calls=%fused_computation.5.clone | custom fusion | bytes 12582928 | tf_op jit(solution)/shard_map/jit(_take)/gather | solution.py:58
  122.0 7.7 %gather_fusion.4 = bf16[4,8,128,2,4,96]{2,5,4,3,1,0:T(8,128)(2,1)} fusion(bf16[8,128,2,4,6,96]{1,5,4,3,2,0:T(8,128)(2,1)} %get-tuple-element.93, s32[1024]{0:T(1024)S(1)} %pad_clamp_fusion), kind=kCustom, calls=%fused_computation.4.clone | custom fusion | bytes 12582928 | tf_op jit(solution)/shard_map/jit(_take)/gather | solution.py:58
  129.7 7.7 %gather_fusion.3 = bf16[4,8,128,2,4,96]{2,5,4,3,1,0:T(8,128)(2,1)} fusion(bf16[8,128,2,4,6,96]{1,5,4,3,2,0:T(8,128)(2,1)} %get-tuple-element.94, s32[1024]{0:T(1024)S(1)} %pad_clamp_fusion.1), kind=kCustom, calls=%fused_computation.3.clone | custom fusion | bytes 12582928 | tf_op jit(solution)/shard_map/jit(_take)/gather | solution.py:58
  137.5 7.8 %gather_fusion.2 = bf16[4,8,128,2,4,96]{2,5,4,3,1,0:T(8,128)(2,1)} fusion(bf16[8,128,2,4,6,96]{1,5,4,3,2,0:T(8,128)(2,1)} %get-tuple-element.93, s32[1024]{0:T(1024)S(1)} %pad_clamp_fusion.1), kind=kCustom, calls=%fused_computation.2.clone | custom fusion | bytes 12582928 | tf_op jit(solution)/shard_map/jit(_take)/gather | solution.py:58
  145.2 7.7 %gather_fusion.1 = bf16[4,8,128,2,4,96]{2,5,4,3,1,0:T(8,128)(2,1)} fusion(bf16[8,128,2,4,6,96]{1,5,4,3,2,0:T(8,128)(2,1)} %get-tuple-element.94, s32[1024]{0:T(1024)S(1)} %pad_clamp_fusion.2), kind=kCustom, calls=%fused_computation.1.clone | custom fusion | bytes 12582928 | tf_op jit(solution)/shard_map/jit(_take)/gather | solution.py:58
  152.9 7.7 %gather_fusion = bf16[4,8,128,2,4,96]{2,5,4,3,1,0:T(8,128)(2,1)} fusion(bf16[8,128,2,4,6,96]{1,5,4,3,2,0:T(8,128)(2,1)} %get-tuple-element.93, s32[1024]{0:T(1024)S(1)} %pad_clamp_fusion.2), kind=kCustom, calls=%fused_computation.clone | custom fusion | bytes 12582928 | tf_op jit(solution)/shard_map/jit(_take)/gather | solution.py:58
  160.6 8.6 %fusion.7 = f32[4,256,4,2,96,1,1]{1,4,6,5,3,2,0:T(8,128)} fusion(bf16[4,3,8,1,2,96,96]{6,5,2,4,3,0,1:T(8,128)(2,1)} %get-tuple-element.104, bf16[4,3,8,1,2,96,96]{6,5,2,4,3,0,1:T(8,128)(2,1)} %get-tuple-element.103, bf16[8,128,2,4,4,96]{1,5,3,2,0,4:T(8,128)(2,1)} %bitcast.104, bf16[8,128,2,4,4,96]{1,5,3,2,0,4:T(8,128)(2,1)} %bitcast.105, ...), kind=kOutput, calls=%fused_computation.19 | convolution fusion | flops 2452094976 | bytes 22806532 | tf_op jit(solution)/shard_map/bkcdxy,kidrby->icrbx/dot_general | solution.py:59
  169.3 8.4 %fusion.9 = f32[4,256,4,2,96,1,1]{1,4,6,5,3,2,0:T(8,128)} fusion(bf16[4,3,8,1,2,96,96]{6,5,2,4,3,0,1:T(8,128)(2,1)} %get-tuple-element.103, bf16[4,3,8,1,2,96,96]{6,5,2,4,3,0,1:T(8,128)(2,1)} %get-tuple-element.104, bf16[8,128,2,4,4,96]{1,5,3,2,0,4:T(8,128)(2,1)} %bitcast.102, bf16[8,128,2,4,4,96]{1,5,3,2,0,4:T(8,128)(2,1)} %bitcast.103, ...), kind=kOutput, calls=%fused_computation.21 | convolution fusion | flops 2452094976 | bytes 22806532 | tf_op jit(solution)/shard_map/bkcdxy,kidrby->icrbx/dot_general | solution.py:59
  177.7 7.2 %fusion.22 = f32[256,2,4,4,96]{0,4,1,2,3:T(8,128)} fusion(f32[4,256,4,2,96,1,1]{1,4,6,5,3,2,0:T(8,128)} %fusion.7, f32[4,256,4,2,96,1,1]{1,4,6,5,3,2,0:T(8,128)} %fusion.9, bf16[4,3,8,1,2,96,96]{6,5,2,4,3,0,1:T(8,128)(2,1)} %get-tuple-element.103, bf16[4,3,8,1,2,96,96]{6,5,2,4,3,0,1:T(8,128)(2,1)} %get-tuple-element.104, ...), kind=kOutput, calls=%fused_computation.41 | convolution fusion | flops 2453667840 | bytes 29097988 | tf_op jit(solution)/shard_map/bkcdxy,kidrby->icrbx/dot_general | solution.py:59
  184.9 2.1 copy.81
  187.1 2.8 %copy.82 = f32[256,2,4,384]{3,2,1,0:T(4,128)} copy(f32[256,2,4,384]{0,3,2,1:T(8,128)S(1)} %bitcast.93) | data formatting | bytes 6291456 | tf_op jit(solution)/shard_map/reshape | solution.py:65
  189.9 40.6 %all_to_all.36 = f32[256,2,4,384]{3,2,1,0:T(4,128)S(1)} all-to-all(f32[256,2,4,384]{3,2,1,0:T(4,128)} %copy.82), channel_id=1, replica_groups=mesh['space'=8,'chaos'=4] {'chaos'}, dimensions={0} | all-to-all | bytes 6291456 | tf_op jit(solution)/shard_map/all_to_all | solution.py:66
  230.5 0.6 copy.83
  231.1 0.3 copy.84
  231.4 3.5 %copy.85 = f32[64,2,16,384]{3,2,1,0:T(8,128)} copy(f32[64,2,16,384]{3,0,2,1:T(8,128)S(1)} %bitcast.95) | data formatting | bytes 6291456 | tf_op jit(solution)/shard_map/all_to_all | solution.py:66
  (38 shorter events, 1.6 us)
Async XLA Ops:
  0.0 51.2 %copy-start = (bf16[64,2,16,384]{3,2,1,0:T(8,128)(2,1)S(1)}, bf16[64,2,16,384]{3,2,1,0:T(8,128)(2,1)}, u32[]{:S(2)}) copy-start(bf16[64,2,16,384]{3,2,1,0:T(8,128)(2,1)} %param.9) | copy-start | bytes 4718596
  0.0 51.0 %copy-start.1 = (s32[4,3]{1,0:T(4,128)S(1)}, s32[4,3]{1,0:T(4,128)}, u32[]{:S(2)}) copy-start(s32[4,3]{1,0:T(4,128)} %param.11) | copy-start | bytes 148
  2.3 48.9 %collective-permute-start.1 = (bf16[64,2,16,96]{3,2,1,0:T(8,128)(2,1)}, bf16[64,2,16,96]{3,2,1,0:T(8,128)(2,1)S(1)}, u32[]{:S(2)}, u32[]{:S(2)}) collective-permute-start(bf16[64,2,16,96]{3,2,1,0:T(8,128)(2,1)} %get-tuple-element.98), channel_id=1, source_target_pairs={{4,0},{8,4},{12,8},{16,12},{20,16},{24,20},{28,24},{5,1},{9,5},{13... | collective-permute-start | bytes 1179656 | tf_op jit(solution)/shard_map/ppermute | solution.py:21
  3.6 47.6 %collective-permute-start = (bf16[64,2,16,96]{3,2,1,0:T(8,128)(2,1)S(1)}, bf16[64,2,16,96]{3,2,1,0:T(8,128)(2,1)S(1)}, u32[]{:S(2)}, u32[]{:S(2)}) collective-permute-start(bf16[64,2,16,96]{3,2,1,0:T(8,128)(2,1)S(1)} %get-tuple-element.97), channel_id=1, source_target_pairs={{0,4},{4,8},{8,12},{12,16},{16,20},{20,24},{24,28},{1,5},{5,9},{9,... | collective-permute-start | bytes 1179656 | tf_op jit(solution)/shard_map/ppermute | solution.py:19
  55.1 34.9 %all-to-all-start = ((bf16[64,2,16,576]{3,0,1,2:T(8,128)(2,1)}), bf16[64,2,16,576]{3,0,1,2:T(8,128)(2,1)S(1)}, u32[]{:S(2)}, u32[]{:S(2)}) async-start(bf16[64,2,16,576]{3,0,1,2:T(8,128)(2,1)} %copy.72), calls=%async_computation | async-start | bytes 5242880 | tf_op jit(solution)/shard_map/all_to_all | solution.py:43
  160.6 17.1 %slice-start = ((s8[6291456]{0:T(1024)(128)(4,1)}), s8[4194304]{0:T(1024)(128)(4,1)S(1)}, s32[]{:S(2)}) async-start(s8[6291456]{0:T(1024)(128)(4,1)} %bitcast.96), calls=%async_computation.2 | async-start | bytes 8388608
  160.6 17.1 %slice-start.2 = ((s8[6291456]{0:T(1024)(128)(4,1)}), s8[4194304]{0:T(1024)(128)(4,1)S(1)}, s32[]{:S(2)}) async-start(s8[6291456]{0:T(1024)(128)(4,1)} %bitcast.99), calls=%async_computation.4 | async-start | bytes 8388608
  169.3 8.4 %slice-start.1 = ((s8[6291456]{0:T(1024)(128)(4,1)}), s8[2097152]{0:T(1024)(128)(4,1)S(1)}, s32[]{:S(2)}) async-start(s8[6291456]{0:T(1024)(128)(4,1)} %bitcast.96), calls=%async_computation.3 | async-start | bytes 4194304
  169.3 8.4 %slice-start.3 = ((s8[6291456]{0:T(1024)(128)(4,1)}), s8[2097152]{0:T(1024)(128)(4,1)S(1)}, s32[]{:S(2)}) async-start(s8[6291456]{0:T(1024)(128)(4,1)} %bitcast.99), calls=%async_computation.5 | async-start | bytes 4194304
where the time goes:
time: 237 us; the launch traced here: 235 us
  local copies, waits for them, and re-layouts  96.5 us (41%)
  blocking collectives  40.6 us (17%)
  matrix products  34.7 us (15%)
  other arithmetic  29.5 us (12%)
  waiting for transfers between devices  22.6 us (10%)
  starting transfers between devices  10.6 us (4%)
    gather x7, local copies, waits for them, and re-layouts, body(): columns = jnp.take(coupled_field, tile_columns[:, tile_slot], axis=4)  59.8 us
    all_to_all x1, blocking collectives, body(): lax.all_to_all(result, 'chaos', split_axis=0, concat_axis=2, tiled=True)  40.6 us
    dot_general x3, matrix products, body(): jnp.einsum('bkcdxy,kidrby->icrbx', complex_tiles[:, tile_slot], columns,...  24.3 us
    reduce_sum x8, other arithmetic, one_term(): jnp.where(matches, row_value[:, :, None], jnp.zeros((), jnp.bfloat16))  22.8 us
    all_to_all x1, waiting for transfers between devices, body(): lax.all_to_all(extended, 'chaos', split_axis=2, concat_axis=0, tiled=True)  22.6 us
    dot_general x1, matrix products, body(): jnp.einsum('kij,jcrd->kicrd', coupling, all_terms, preferred_element_type...  10.4 us
    eq x16, local copies, waits for them, and re-layouts, one_term(): matches = row_index[:, :, None] == columns[None, None, :]  6.88 us
    broadcast_in_dim x16, local copies, waits for them, and re-layouts, one_term(): jnp.where(matches, row_value[:, :, None], jnp.zeros((), jnp.bfloat16))  6.75 us
  transfers between devices with their start and end apart: 3, of which 1 were waited for; matrix products, arithmetic and copies ran while one was open for 21% of the time, Pallas kernels for 0%

commit v1 on v0

v1 whole, which is shorter than its diff:
```python
import functools

import jax
import jax.numpy as jnp
from jax import lax
from jax.experimental import pallas as pl
from jax.experimental.pallas import tpu as pltpu
from jax.sharding import PartitionSpec as P

TILE = 96


def coupling_kernel(place_ref, index_ref, value_ref, out_ref):
    me = place_ref[0]
    terms = out_ref.shape[1]
    share = terms // 4
    half = terms // 2

    def arrange(v):
        low, high = v[:, :half], v[:, half:]
        flip = (me >> 1) == 1
        first, second = jnp.where(flip, high, low), jnp.where(flip, low, high)
        shift = (me & 1) * share
        return jnp.concatenate([pltpu.roll(first, shift, 1), pltpu.roll(second, shift, 1)], axis=1)

    index = arrange(index_ref[0] ^ (me * share)).astype(jnp.float32).astype(jnp.bfloat16)
    value = arrange(value_ref[0].astype(jnp.float32)).astype(jnp.bfloat16)
    chunk = terms // 4
    for part in range(terms // chunk):
        j = lax.broadcasted_iota(jnp.int32, (chunk, terms), 0) + part * chunk
        j = j.astype(jnp.float32).astype(jnp.bfloat16)
        dense = jnp.zeros((chunk, terms), jnp.bfloat16)
        for n in range(index.shape[0]):
            dense = jnp.where(index[n : n + 1, :] == j, value[n : n + 1, :], dense)
        out_ref[0, part * chunk : (part + 1) * chunk, :] = dense


def dense_coupling(place, chaos_index, chaos_value):
    nkl, terms, nzc = chaos_index.shape
    return pl.pallas_call(
        coupling_kernel,
        grid_spec=pltpu.PrefetchScalarGridSpec(
            num_scalar_prefetch=1,
            grid=(nkl,),
            in_specs=[pl.BlockSpec((1, nzc, terms), lambda k, w: (k, 0, 0))] * 2,
            out_specs=pl.BlockSpec((1, terms, terms), lambda k, w: (k, 0, 0)),
        ),
        out_shape=jax.ShapeDtypeStruct((nkl, terms, terms), jnp.bfloat16),
        cost_estimate=pl.CostEstimate(flops=10_000_000, bytes_accessed=2_000_000, transcendentals=0),
    )(place, jnp.swapaxes(chaos_index, 1, 2), jnp.swapaxes(chaos_value, 1, 2))


def tiles_kernel(tiles_ref, out_ref):
    _, nnz, nkl = tiles_ref.shape[:3]
    for s in range(nnz):
        for part in range(2):
            out_ref[0, s, part * TILE : (part + 1) * TILE, :] = jnp.concatenate(
                [tiles_ref[0, s, k, part] for k in range(nkl)], axis=1
            )


def wide_tiles(stiff_tiles):
    blocks, nnz, nkl = stiff_tiles.shape[:3]
    return pl.pallas_call(
        tiles_kernel,
        grid=(blocks,),
        in_specs=[pl.BlockSpec((1, nnz, nkl, 2, TILE, TILE), lambda b: (b, 0, 0, 0, 0, 0))],
        out_specs=pl.BlockSpec((1, nnz, 2 * TILE, nkl * TILE), lambda b: (b, 0, 0, 0)),
        out_shape=jax.ShapeDtypeStruct((blocks, nnz, 2 * TILE, nkl * TILE), jnp.bfloat16),
        cost_estimate=pl.CostEstimate(flops=10_000_000, bytes_accessed=4_000_000, transcendentals=0),
    )(stiff_tiles)


def pack_kernel(chunk, place_ref, own_ref, near_ref, keep_ref, send_ref, rows):
    me = place_ref[0]
    terms, _, loads, width = own_ref.shape
    lanes = rows.shape[3]
    for which, ref in enumerate((own_ref, near_ref)):
        for t in range(width // lanes):
            part = ref[:, 0, :, t * lanes : (t + 1) * lanes].astype(jnp.float32)
            rows[which, t] = part.reshape(terms * loads, lanes)
    for m in range(keep_ref.shape[0]):
        for out_ref, x in ((send_ref, 1 - (me >> 1)), (keep_ref, me >> 1)):
            r = 8 * chunk + 4 * m + 2 * (me & 1) + x
            for t in range(width // lanes):
                both = [rows[which, t, pl.ds(r, terms, stride=loads), :] for which in range(2)]
                flipped = jnp.concatenate(both, axis=0).astype(jnp.bfloat16).T
                out_ref[m, 0, t * lanes : (t + 1) * lanes, :] = flipped


def pack(place, own, near, chunk):
    terms, parts, loads, width = own.shape
    cases = loads // 8
    out = jax.ShapeDtypeStruct((cases, parts, width, 2 * terms), jnp.bfloat16)
    return pl.pallas_call(
        functools.partial(pack_kernel, chunk),
        grid_spec=pltpu.PrefetchScalarGridSpec(
            num_scalar_prefetch=1,
            grid=(parts,),
            in_specs=[pl.BlockSpec((terms, 1, loads, width), lambda c, w: (0, c, 0, 0))] * 2,
            out_specs=[pl.BlockSpec((cases, 1, width, 2 * terms), lambda c, w: (0, c, 0, 0))] * 2,
            scratch_shapes=[pltpu.VMEM((2, width // 128, terms * loads, 128), jnp.float32)],
        ),
        out_shape=[out, out],
        compiler_params=pltpu.CompilerParams(vmem_limit_bytes=24 << 20),
        cost_estimate=pl.CostEstimate(flops=1_000_000, bytes_accessed=4_000_000, transcendentals=0),
    )(place, own, near)


def operator_kernel(slots_ref, own_ref, far_ref, even_ref, odd_ref, coupling_ref, tiles_ref, keep_ref, send_ref, mixed):
    nkl, terms, _ = coupling_ref.shape
    blocks, nnz = tiles_ref.shape[:2]
    half = terms // 2
    for c in range(2):
        pieces = [jnp.concatenate([own_ref[0, c], far_ref[0, c]], axis=1)]
        for halo_ref in (even_ref, odd_ref):
            pieces.append(jnp.concatenate([halo_ref[0, 0, c], halo_ref[0, 1, c]], axis=1))
        field = jnp.concatenate(pieces, axis=0)
        for k in range(nkl):
            mix = jnp.dot(field, coupling_ref[k], preferred_element_type=jnp.float32).astype(jnp.bfloat16)
            for g in range(blocks + 2):
                mixed[g, k * TILE : (k + 1) * TILE, c * terms : (c + 1) * terms] = mix[g * TILE : (g + 1) * TILE]
    for b in range(blocks):
        acc = None
        for s in range(nnz):
            term = jnp.dot(tiles_ref[b, s], mixed[slots_ref[b * nnz + s]], preferred_element_type=jnp.float32)
            acc = term if acc is None else acc + term
        real = (acc[:TILE, :terms] - acc[TILE:, terms:]).T.astype(jnp.bfloat16)
        imag = (acc[:TILE, terms:] + acc[TILE:, :terms]).T.astype(jnp.bfloat16)
        for c, part in enumerate((real, imag)):
            keep_ref[0, c, :, b * TILE : (b + 1) * TILE] = part[:half]
            send_ref[0, c, :, b * TILE : (b + 1) * TILE] = part[half:]


def apply_operator(slots, own, far, even, odd, coupling, tiles):
    cases, _, width, half = own.shape
    blocks, _, _, depth = tiles.shape
    terms = coupling.shape[1]
    inner = pl.BlockSpec((1, 2, width, half), lambda r, s: (r, 0, 0, 0))
    outer = pl.BlockSpec((1, 2, 2, TILE, half), lambda r, s: (r, 0, 0, 0, 0))
    out = jax.ShapeDtypeStruct((cases, 2, half, width), jnp.bfloat16)
    return pl.pallas_call(
        operator_kernel,
        grid_spec=pltpu.PrefetchScalarGridSpec(
            num_scalar_prefetch=1,
            grid=(cases,),
            in_specs=[
                inner,
                inner,
                outer,
                outer,
                pl.BlockSpec(coupling.shape, lambda r, s: (0, 0, 0)),
                pl.BlockSpec(tiles.shape, lambda r, s: (0, 0, 0, 0)),
            ],
            out_specs=[pl.BlockSpec((1, 2, half, width), lambda r, s: (r, 0, 0, 0))] * 2,
            scratch_shapes=[pltpu.VMEM((blocks + 2, depth, 2 * terms), jnp.bfloat16)],
        ),
        out_shape=[out, out],
        compiler_params=pltpu.CompilerParams(vmem_limit_bytes=32 << 20),
        cost_estimate=pl.CostEstimate(flops=6_000_000_000, bytes_accessed=5_000_000, transcendentals=0),
    )(slots, own, far, even, odd, coupling, tiles)


def unpack_kernel(place_ref, *refs):
    me = place_ref[0]
    *piece_refs, out_ref, rows = refs
    cases, parts, terms, width = piece_refs[0].shape
    lanes = rows.shape[2]
    loads = out_ref.shape[0] // (terms * parts)
    for position, ref in enumerate(piece_refs):
        chunk, source = position // 4, me ^ (position % 4)
        for m in range(cases):
            r = 8 * chunk + 4 * m + 2 * (source & 1) + (source >> 1)
            for c in range(parts):
                for t in range(width // lanes):
                    part = ref[m, c, :, t * lanes : (t + 1) * lanes].astype(jnp.float32)
                    rows[t, pl.ds(c * loads + r, terms, stride=parts * loads), :] = part
    for t in range(width // lanes):
        out_ref[:, t * lanes : (t + 1) * lanes] = rows[t]


def unpack(place, chunks):
    cases, parts, half, width = chunks[0][0].shape
    terms = half // 2
    loads = 4 * cases * len(chunks)
    step = 16
    steps = terms // step
    first = pl.BlockSpec((cases, parts, step, width), lambda t, w: (0, 0, t, 0))
    second = pl.BlockSpec((cases, parts, step, width), lambda t, w: (0, 0, t + steps, 0))
    pieces, specs = [], []
    for keep, near_keep, back, near_back in chunks:
        pieces += [keep, near_keep, back, near_back]
        specs += [first, second, first, second]
    out = pl.pallas_call(
        unpack_kernel,
        grid_spec=pltpu.PrefetchScalarGridSpec(
            num_scalar_prefetch=1,
            grid=(steps,),
            in_specs=specs,
            out_specs=pl.BlockSpec((step * parts * loads, width), lambda t, w: (t, 0)),
            scratch_shapes=[pltpu.VMEM((width // 128, step * parts * loads, 128), jnp.float32)],
        ),
        out_shape=jax.ShapeDtypeStruct((terms * parts * loads, width), jnp.float32),
        cost_estimate=pl.CostEstimate(flops=1_000_000, bytes_accessed=6_000_000, transcendentals=0),
    )(place, *pieces)
    return out.reshape(terms, parts, loads, width)


def swap_edges(own, far):
    count = lax.axis_size("space")
    odd_place = lax.axis_index("space") % 2
    last = own.shape[2] - TILE

    def edge(start):
        return jnp.stack([lax.dynamic_slice_in_dim(v, start, TILE, axis=2) for v in (own, far)], axis=1)

    even_pairs = [(i, i ^ 1) for i in range(count)]
    odd_pairs = [(i, ((i - 1) ^ 1) + 1) for i in range(1, count - 1)]
    even = lax.ppermute(edge(last * (1 - odd_place)), "space", even_pairs)
    odd = lax.ppermute(edge(last * odd_place), "space", odd_pairs)
    return even, odd


def body(load_vectors, stiff_tiles, tile_columns, chaos_index, chaos_value):
    count = lax.axis_size("chaos")
    blocks = stiff_tiles.shape[0]
    odd_place = lax.axis_index("space") % 2
    slots = jnp.where(
        tile_columns == 0,
        blocks + 1 - odd_place,
        jnp.where(tile_columns == blocks + 1, blocks + odd_place, tile_columns - 1),
    ).reshape(-1)

    if count != 4:
        coupling = dense_coupling(jnp.zeros((1,), jnp.int32), chaos_index, chaos_value)
        tiles = wide_tiles(stiff_tiles)
        mine = lax.all_to_all(load_vectors, "chaos", split_axis=2, concat_axis=0, tiled=True)
        mine = mine.transpose(2, 1, 3, 0)
        half = mine.shape[3] // 2
        own, far = mine[..., :half], mine[..., half:]
        even, odd = swap_edges(own, far)
        keep, send = apply_operator(slots, own, far, even, odd, coupling, tiles)
        result = jnp.concatenate([keep, send], axis=2)
        result = lax.all_to_all(result, "chaos", split_axis=2, concat_axis=0, tiled=True)
        return result.transpose(2, 1, 0, 3).astype(jnp.float32)

    place = lax.axis_index("chaos").reshape(1)
    near = lambda v: lax.ppermute(v, "chaos", [(i, i ^ 1) for i in range(4)])
    across = lambda v: lax.ppermute(v, "chaos", [(i, i ^ 2) for i in range(4)])
    near_loads = near(load_vectors)
    tiles = wide_tiles(stiff_tiles)
    packed = [pack(place, load_vectors, near_loads, chunk) for chunk in range(2)]
    far = [across(send) for _, send in packed]
    coupling = dense_coupling(place, chaos_index, chaos_value)
    chunks = []
    for (own, _), other in zip(packed, far):
        even, odd = swap_edges(own, other)
        keep, send = apply_operator(slots, own, other, even, odd, coupling, tiles)
        back = across(send)
        chunks.append((keep, near(keep), back, near(back)))
    return unpack(place, chunks)


def solution(mesh):
    in_specs = (
        P("chaos", None, None, "space"),
        P("space", None, None, None, None, None),
        P("space", None),
        P(),
        P(),
    )
    out_specs = P("chaos", None, None, "space")
    return jax.shard_map(body, mesh=mesh, in_specs=in_specs, out_specs=out_specs, check_vma=False)
```

time: 237 us -> 82.5 us (0.35)
  local copies, waits for them, and re-layouts: 96.5 us -> 7.83 us
  blocking collectives: 40.6 us -> 0 us
  Pallas kernels: 0 us -> 39.3 us
  matrix products: 34.7 us -> 0 us
  other arithmetic: 29.5 us -> 0.09 us
  starting transfers between devices: 10.6 us -> 15 us
  waiting for transfers between devices: 22.6 us -> 19.1 us
    gather x7 -> x0, local copies, waits for them, and re-layouts: 59.8 us -> none  [body(): columns = jnp.take(coupled_field, tile_columns[:, tile_slot], axis=4)]
    all_to_all x1 -> x0, blocking collectives: 40.6 us -> none  [body(): lax.all_to_all(result, 'chaos', split_axis=0, concat_axis=2, tiled=True)]
    pallas_call x0 -> x7, Pallas kernels: none -> 39.3 us  [the longest x2 17.6 us: apply_operator(): pl.pallas_call(operator_kernel, grid_spec=pltpu.PrefetchScalarGridSpec(nu...]
    dot_general x4 -> x0, matrix products: 34.7 us -> none  [the longest x3 24.3 us: body(): jnp.einsum('bkcdxy,kidrby->icrbx', complex_tiles[:, tile_slot], columns,...]
    reduce_sum x8 -> x0, other arithmetic: 22.8 us -> none  [one_term(): jnp.where(matches, row_value[:, :, None], jnp.zeros((), jnp.bfloat16))]
    all_to_all x1 -> x0, waiting for transfers between devices: 22.6 us -> none  [body(): lax.all_to_all(extended, 'chaos', split_axis=2, concat_axis=0, tiled=True)]
    ppermute x2 -> x13, waiting for transfers between devices: 0.01 us -> 19.1 us  [the longest x4 8.36 us: body(): across = lambda v: lax.ppermute(v, 'chaos', [(i, i ^ 2) for i in range(4)])]
    ppermute x2 -> x13, starting transfers between devices: 6.81 us -> 15 us  [the longest x2 7.55 us: swap_edges(): even = lax.ppermute(edge(last * (1 - odd_place)), 'space', even_pairs)]
  transfers between devices with their start and end apart: 3 -> 13, of which waited for: 1 -> 5; matrix products, arithmetic and copies ran while one was open for 21% -> 3% of each run, Pallas kernels for 0% -> 38%
where the time goes in v1:
time: 82.5 us; the launch traced here: 81.5 us
  Pallas kernels  39.3 us (48%)
  waiting for transfers between devices  19.1 us (23%)
  starting transfers between devices  15 us (18%)
  local copies, waits for them, and re-layouts  7.83 us (9%)
    pallas_call x2, Pallas kernels, apply_operator(): pl.pallas_call(operator_kernel, grid_spec=pltpu.PrefetchScalarGridSpec(nu...  17.6 us
    ppermute x4, waiting for transfers between devices, body(): across = lambda v: lax.ppermute(v, 'chaos', [(i, i ^ 2) for i in range(4)])  8.36 us
    ppermute x2, starting transfers between devices, swap_edges(): even = lax.ppermute(edge(last * (1 - odd_place)), 'space', even_pairs)  7.55 us
    pallas_call x1, Pallas kernels, dense_coupling(): pl.pallas_call(coupling_kernel, grid_spec=pltpu.PrefetchScalarGridSpec(nu...  6.13 us
    ppermute x2, waiting for transfers between devices, swap_edges(): even = lax.ppermute(edge(last * (1 - odd_place)), 'space', even_pairs)  5.83 us
    pallas_call x1, Pallas kernels, unpack(): pl.pallas_call(unpack_kernel, grid_spec=pltpu.PrefetchScalarGridSpec(num_...  5.66 us
    pallas_call x1, Pallas kernels, wide_tiles(): pl.pallas_call(tiles_kernel, grid=(blocks,), in_specs=[pl.BlockSpec((1, n...  5.12 us
    ppermute x4, starting transfers between devices, body(): across = lambda v: lax.ppermute(v, 'chaos', [(i, i ^ 2) for i in range(4)])  5.02 us
  transfers between devices with their start and end apart: 13, of which 5 were waited for; matrix products, arithmetic and copies ran while one was open for 3% of the time, Pallas kernels for 38%

profile of v1, /device:TPU:0, one launch (start us, length us, event | category | flops | bytes accessed | tf_op | source)
XLA Modules:
  0.0 81.5 jit_solution(17841340531069200928)
XLA Ops:
  0.0 0.5 collective-permute-start
  0.5 3.2 %collective-permute-done.near_ref = bf16[64,2,16,384]{3,2,1,0:T(8,128)(2,1)S(1)} collective-permute-done((bf16[64,2,16,384]{3,2,1,0:T(8,128)(2,1)}, bf16[64,2,16,384]{3,2,1,0:T(8,128)(2,1)S(1)}, u32[]{:S(2)}, u32[]{:S(2)}) %collective-permute-start) | collective-permute-done | bytes 1572896 | tf_op jit(solution)/shard_map/ppermute | solution.py:248
  3.7 0.0 copy-start
  3.7 1.4 %copy-done = bf16[64,2,16,384]{3,2,1,0:T(8,128)(2,1)S(1)} copy-done((bf16[64,2,16,384]{3,2,1,0:T(8,128)(2,1)S(1)}, bf16[64,2,16,384]{3,2,1,0:T(8,128)(2,1)}, u32[]{:S(2)}) %copy-start) | copy-done | bytes 1572888
  5.1 0.0 copy-start.15
  5.1 2.4 %shard_map.59 = (bf16[2,2,384,128]{3,2,1,0:T(8,128)(2,1)S(1)}, bf16[2,2,384,128]{3,2,1,0:T(8,128)(2,1)}) custom-call(s32[1]{0:T(128)} %bitcast.place_ref, bf16[64,2,16,384]{3,2,1,0:T(8,128)(2,1)S(1)} %copy-done, bf16[64,2,16,384]{3,2,1,0:T(8,128)(2,1)S(1)} %collective-permute-done.near_ref), custom_call_target="tpu_custom_call" | custom-call | flops 1000000 | bytes 4000000 | tf_op jit(solution)/shard_map/pallas_call | solution.py:95
  7.5 0.0 copy-start.7
  7.5 0.7 copy-done.7
  8.2 2.9 %collective-permute-start.7 = (bf16[2,2,384,128]{3,2,1,0:T(8,128)(2,1)}, bf16[2,2,384,128]{3,2,1,0:T(8,128)(2,1)}, u32[]{:S(2)}, u32[]{:S(2)}) collective-permute-start(bf16[2,2,384,128]{3,2,1,0:T(8,128)(2,1)} %get-tuple-element.18), channel_id=1, source_target_pairs={{0,2},{1,3},{2,0},{3,1},{4,6},{5,7},{6,4},{7,5},{8,10},{9,11},{10,... | collective-permute-start | bytes 1179656 | tf_op jit(solution)/shard_map/ppermute | solution.py:249
  11.1 2.4 %shard_map.55 = (bf16[2,2,384,128]{3,2,1,0:T(8,128)(2,1)S(1)}, bf16[2,2,384,128]{3,2,1,0:T(8,128)(2,1)}) custom-call(s32[1]{0:T(128)} %bitcast.place_ref, bf16[64,2,16,384]{3,2,1,0:T(8,128)(2,1)S(1)} %copy-done, bf16[64,2,16,384]{3,2,1,0:T(8,128)(2,1)S(1)} %collective-permute-done.near_ref), custom_call_target="tpu_custom_call" | custom-call | flops 1000000 | bytes 4000000 | tf_op jit(solution)/shard_map/pallas_call | solution.py:95
  13.5 0.0 copy-start.5
  13.5 0.7 copy-done.5
  14.2 0.0 collective-permute-start.1
  14.2 0.0 copy-done.15
  14.2 0.1 reshape.10.slots_ref
  14.3 5.1 %shard_map.57.tiles_ref = bf16[4,3,192,768]{3,2,1,0:T(8,128)(2,1)} custom-call(bf16[4,3,8,2,96,96]{5,4,3,2,1,0:T(8,128)(2,1)} %tiles_ref.1), custom_call_target="tpu_custom_call" | custom-call | flops 10000000 | bytes 4000000 | tf_op jit(solution)/shard_map/pallas_call | solution.py:64
  19.4 6.1 %shard_map.56.coupling_ref = bf16[8,256,256]{2,1,0:T(8,128)(2,1)} custom-call(s32[1]{0:T(128)} %bitcast.place_ref, s32[8,32,256]{2,1,0:T(8,128)} %bitcast.20, bf16[8,32,256]{2,1,0:T(8,128)(2,1)} %bitcast.21), custom_call_target="tpu_custom_call" | custom-call | flops 10000000 | bytes 2000000 | tf_op jit(solution)/shard_map/pallas_call | solution.py:40
  25.6 1.0 %dynamic-slice_bitcast_fusion.1 = (bf16[2,1,2,96,128]{4,3,2,1,0:T(8,128)(2,1)S(1)}, bf16[2,1,2,96,128]{4,3,2,1,0:T(8,128)(2,1)S(1)}) fusion(bf16[2,2,384,128]{3,2,1,0:T(8,128)(2,1)} %copy-done.7, s32[]{:T(128)S(6)} %select_n.34, s32[]{:T(128)S(6)} %select_n.33), kind=kLoop, calls=%fused_computation.5 | loop fusion | bytes 393224 | tf_op jit(solution)/shard_map/stack | solution.py:215
  26.6 1.0 %dynamic-slice_bitcast_fusion.5 = (bf16[2,1,2,96,128]{4,3,2,1,0:T(8,128)(2,1)S(1)}, bf16[2,1,2,96,128]{4,3,2,1,0:T(8,128)(2,1)S(1)}) fusion(bf16[2,2,384,128]{3,2,1,0:T(8,128)(2,1)} %copy-done.5, s32[]{:T(128)S(6)} %select_n.34, s32[]{:T(128)S(6)} %select_n.33), kind=kLoop, calls=%fused_computation.9 | loop fusion | bytes 393224 | tf_op jit(solution)/shard_map/stack | solution.py:215
  27.6 0.0 collective-permute-done.7.far_ref
  27.6 1.6 %collective-permute-done.1.far_ref = bf16[2,2,384,128]{3,2,1,0:T(8,128)(2,1)} collective-permute-done((bf16[2,2,384,128]{3,2,1,0:T(8,128)(2,1)}, bf16[2,2,384,128]{3,2,1,0:T(8,128)(2,1)}, u32[]{:S(2)}, u32[]{:S(2)}) %collective-permute-start.1) | collective-permute-done | bytes 393248 | tf_op jit(solution)/shard_map/ppermute | solution.py:249
  29.2 1.1 %dynamic-slice_bitcast_fusion = (bf16[2,1,2,96,128]{4,3,2,1,0:T(8,128)(2,1)S(1)}, bf16[2,1,2,96,128]{4,3,2,1,0:T(8,128)(2,1)S(1)}, bf16[2,1,2,96,128]{4,3,2,1,0:T(8,128)(2,1)S(1)}, bf16[2,1,2,96,128]{4,3,2,1,0:T(8,128)(2,1)S(1)}) fusion(bf16[2,2,384,128]{3,2,1,0:T(8,128)(2,1)} %collective-permute-done.7.far_ref, s32[]{:T(128)S(6)} %select_n.34, ...), kind=kLoop, calls=%fused_computation.4 | loop fusion | bytes 786440 | tf_op jit(solution)/shard_map/stack | solution.py:215
  30.3 1.8 %collective-permute-start.8 = (bf16[2,2,2,96,128]{4,3,2,1,0:T(8,128)(2,1)S(1)}, bf16[2,2,2,96,128]{4,3,2,1,0:T(8,128)(2,1)S(1)}, u32[]{:S(2)}, u32[]{:S(2)}) collective-permute-start(bf16[2,2,2,96,128]{4,3,2,1,0:T(8,128)(2,1)S(1)} %pad_maximum_fusion.2), channel_id=1, source_target_pairs={{0,4},{4,0},{8,12},{12,8},{16,20},{20,16},{24,28},{28,24},{1,5},{5... | collective-permute-start | bytes 589832 | tf_op jit(solution)/shard_map/ppermute | solution.py:219
  32.2 0.7 collective-permute-start.9
  32.9 0.7 collective-permute-start.3
  33.6 0.0 copy-start.6
  33.6 5.7 %collective-permute-start.2 = (bf16[2,2,2,96,128]{4,3,2,1,0:T(8,128)(2,1)S(1)}, bf16[2,2,2,96,128]{4,3,2,1,0:T(8,128)(2,1)S(1)}, u32[]{:S(2)}, u32[]{:S(2)}) collective-permute-start(bf16[2,2,2,96,128]{4,3,2,1,0:T(8,128)(2,1)S(1)} %pad_maximum_fusion), channel_id=1, source_target_pairs={{0,4},{4,0},{8,12},{12,8},{16,20},{20,16},{24,28},{28,24},{1,5},{5... | collective-permute-start | bytes 589832 | tf_op jit(solution)/shard_map/ppermute | solution.py:219
  39.4 5.8 %collective-permute-done.8.even_ref = bf16[2,2,2,96,128]{4,3,2,1,0:T(8,128)(2,1)S(1)} collective-permute-done((bf16[2,2,2,96,128]{4,3,2,1,0:T(8,128)(2,1)S(1)}, bf16[2,2,2,96,128]{4,3,2,1,0:T(8,128)(2,1)S(1)}, u32[]{:S(2)}, u32[]{:S(2)}) %collective-permute-start.8) | collective-permute-done | bytes 196640 | tf_op jit(solution)/shard_map/ppermute | solution.py:219
  45.2 0.0 collective-permute-done.9.odd_ref
  45.2 0.0 copy-done.1
  45.2 0.0 copy-done.2
  45.2 1.0 %copy-done.8 = bf16[2,2,384,128]{3,2,1,0:T(8,128)(2,1)S(1)} copy-done((bf16[2,2,384,128]{3,2,1,0:T(8,128)(2,1)S(1)}, bf16[2,2,384,128]{3,2,1,0:T(8,128)(2,1)}, u32[]{:S(2)}) %copy-start.8) | copy-done | bytes 393240
  46.2 8.8 %shard_map.60 = (bf16[2,2,128,384]{3,2,1,0:T(8,128)(2,1)S(1)}, bf16[2,2,128,384]{3,2,1,0:T(8,128)(2,1)S(1)}) custom-call(s32[12]{0:T(128)S(1)} %reshape.10.slots_ref, bf16[2,2,384,128]{3,2,1,0:T(8,128)(2,1)S(1)} %copy-done.8, bf16[2,2,384,128]{3,2,1,0:T(8,128)(2,1)} %collective-permute-done.7.far_ref, ...), custom_call_target="tpu_custom_call" | custom-call | flops 6000000000 | bytes 5000000 | tf_op jit(solution)/shard_map/pallas_call | solution.py:142
  55.0 0.0 copy-start.3
  55.0 1.6 %collective-permute-start.11 = (bf16[2,2,128,384]{3,2,1,0:T(8,128)(2,1)S(1)}, bf16[2,2,128,384]{3,2,1,0:T(8,128)(2,1)S(1)}, u32[]{:S(2)}, u32[]{:S(2)}) collective-permute-start(bf16[2,2,128,384]{3,2,1,0:T(8,128)(2,1)S(1)} %get-tuple-element.20), channel_id=1, source_target_pairs={{0,2},{1,3},{2,0},{3,1},{4,6},{5,7},{6,4},{7,5},{8,10},{9,11},{10,... | collective-permute-start | bytes 1179656 | tf_op jit(solution)/shard_map/ppermute | solution.py:249
  56.6 0.0 collective-permute-done.3.odd_ref
  56.7 0.0 collective-permute-done.2.even_ref
  56.7 0.0 copy-done.6
  56.7 8.8 %shard_map.58 = (bf16[2,2,128,384]{3,2,1,0:T(8,128)(2,1)S(1)}, bf16[2,2,128,384]{3,2,1,0:T(8,128)(2,1)S(1)}) custom-call(s32[12]{0:T(128)S(1)} %reshape.10.slots_ref, bf16[2,2,384,128]{3,2,1,0:T(8,128)(2,1)S(1)} %copy-done.6, bf16[2,2,384,128]{3,2,1,0:T(8,128)(2,1)} %collective-permute-done.1.far_ref, ...), custom_call_target="tpu_custom_call" | custom-call | flops 6000000000 | bytes 5000000 | tf_op jit(solution)/shard_map/pallas_call | solution.py:142
  65.5 0.0 copy-start.4
  65.5 0.5 collective-permute-start.5
  66.0 0.0 copy-done.3
  66.0 0.0 collective-permute-start.10
  66.0 0.5 collective-permute-start.4
  66.6 0.0 collective-permute-done.11.refs_6_
  66.6 0.1 collective-permute-start.12
  66.6 6.7 %collective-permute-done.5.refs_2_ = bf16[2,2,128,384]{3,2,1,0:T(8,128)(2,1)S(1)} collective-permute-done((bf16[2,2,128,384]{3,2,1,0:T(8,128)(2,1)S(1)}, bf16[2,2,128,384]{3,2,1,0:T(8,128)(2,1)S(1)}, u32[]{:S(2)}, u32[]{:S(2)}) %collective-permute-start.5) | collective-permute-done | bytes 393248 | tf_op jit(solution)/shard_map/ppermute | solution.py:249
  73.3 0.0 collective-permute-start.6
  73.4 0.0 collective-permute-done.10.refs_5_
  73.4 0.0 copy-done.4
  73.4 0.0 copy-start.11
  73.4 0.0 collective-permute-done.4.refs_1_
  73.4 0.0 copy-done.9
  73.4 0.0 copy-start.12
  73.4 0.0 collective-permute-done.12.refs_7_
  73.4 0.0 copy-start.13
  73.4 1.6 %collective-permute-done.6.refs_3_ = bf16[2,2,128,384]{3,2,1,0:T(8,128)(2,1)S(1)} collective-permute-done((bf16[2,2,128,384]{3,2,1,0:T(8,128)(2,1)S(1)}, bf16[2,2,128,384]{3,2,1,0:T(8,128)(2,1)S(1)}, u32[]{:S(2)}, u32[]{:S(2)}) %collective-permute-start.6) | collective-permute-done | bytes 393248 | tf_op jit(solution)/shard_map/ppermute | solution.py:248
  75.1 0.0 copy-done.10
  75.1 0.0 copy-done.11
  75.1 0.0 copy-done.12
  75.1 0.0 copy-done.13
  75.1 0.0 copy-start.14
  75.1 0.7 copy-done.14
  75.8 5.7 %shard_map.61 = f32[2048,384]{1,0:T(8,128)} custom-call(s32[1]{0:T(128)} %bitcast.place_ref, bf16[2,2,128,384]{3,2,1,0:T(8,128)(2,1)} %copy-done.4, bf16[2,2,128,384]{3,2,1,0:T(8,128)(2,1)} %copy-done.12, bf16[2,2,128,384]{3,2,1,0:T(8,128)(2,1)} %copy-done.10, bf16[2,2,128,384]{3,2,1,0:T(8,128)(2,1)} %copy-done.14, bf16[2,2,128,384]{3,2,1,0:T(8,128)(2,1)} %copy-done.3, ...), custom_call_target="tpu_custom_call" | custom-call | flops 1000000 | bytes 6000000 | tf_op jit(solution)/shard_map/pallas_call | solution.py:194
  (10 shorter events, 0.1 us)
Async XLA Ops:
  0.0 3.7 %collective-permute-start = (bf16[64,2,16,384]{3,2,1,0:T(8,128)(2,1)}, bf16[64,2,16,384]{3,2,1,0:T(8,128)(2,1)S(1)}, u32[]{:S(2)}, u32[]{:S(2)}) collective-permute-start(bf16[64,2,16,384]{3,2,1,0:T(8,128)(2,1)} %own_ref.3), channel_id=1, source_target_pairs={{0,1},{1,0},{2,3},{3,2},{4,5},{5,4},{6,7},{7,6},{8,9},{9,8},{10,11... | collective-permute-start | bytes 4718600 | tf_op jit(solution)/shard_map/ppermute | solution.py:248
  3.7 1.4 %copy-start = (bf16[64,2,16,384]{3,2,1,0:T(8,128)(2,1)S(1)}, bf16[64,2,16,384]{3,2,1,0:T(8,128)(2,1)}, u32[]{:S(2)}) copy-start(bf16[64,2,16,384]{3,2,1,0:T(8,128)(2,1)} %own_ref.3) | copy-start | bytes 4718596
  5.1 9.1 %copy-start.15 = (s32[4,3]{1,0:T(4,128)S(1)}, s32[4,3]{1,0:T(4,128)}, u32[]{:S(2)}) copy-start(s32[4,3]{1,0:T(4,128)} %param.7) | copy-start | bytes 148
  7.5 0.8 copy-start.7
  8.2 19.4 %collective-permute-start.7 = (bf16[2,2,384,128]{3,2,1,0:T(8,128)(2,1)}, bf16[2,2,384,128]{3,2,1,0:T(8,128)(2,1)}, u32[]{:S(2)}, u32[]{:S(2)}) collective-permute-start(bf16[2,2,384,128]{3,2,1,0:T(8,128)(2,1)} %get-tuple-element.18), channel_id=1, source_target_pairs={{0,2},{1,3},{2,0},{3,1},{4,6},{5,7},{6,4},{7,5},{8,10},{9,11},{10,... | collective-permute-start | bytes 1179656 | tf_op jit(solution)/shard_map/ppermute | solution.py:249
  13.5 0.7 copy-start.5
  14.2 15.0 %collective-permute-start.1 = (bf16[2,2,384,128]{3,2,1,0:T(8,128)(2,1)}, bf16[2,2,384,128]{3,2,1,0:T(8,128)(2,1)}, u32[]{:S(2)}, u32[]{:S(2)}) collective-permute-start(bf16[2,2,384,128]{3,2,1,0:T(8,128)(2,1)} %get-tuple-element.14), channel_id=1, source_target_pairs={{0,2},{1,3},{2,0},{3,1},{4,6},{5,7},{6,4},{7,5},{8,10},{9,11},{10,... | collective-permute-start | bytes 1179656 | tf_op jit(solution)/shard_map/ppermute | solution.py:249
  19.4 25.7 %copy-start.1 = (bf16[4,3,192,768]{3,2,1,0:T(8,128)(2,1)S(1)}, bf16[4,3,192,768]{3,2,1,0:T(8,128)(2,1)}, u32[]{:S(2)}) copy-start(bf16[4,3,192,768]{3,2,1,0:T(8,128)(2,1)} %shard_map.57.tiles_ref) | copy-start | bytes 10616836
  25.6 19.6 %copy-start.2 = (bf16[8,256,256]{2,1,0:T(8,128)(2,1)S(1)}, bf16[8,256,256]{2,1,0:T(8,128)(2,1)}, u32[]{:S(2)}) copy-start(bf16[8,256,256]{2,1,0:T(8,128)(2,1)} %shard_map.56.coupling_ref) | copy-start | bytes 3145732
  30.3 14.8 %collective-permute-start.8 = (bf16[2,2,2,96,128]{4,3,2,1,0:T(8,128)(2,1)S(1)}, bf16[2,2,2,96,128]{4,3,2,1,0:T(8,128)(2,1)S(1)}, u32[]{:S(2)}, u32[]{:S(2)}) collective-permute-start(bf16[2,2,2,96,128]{4,3,2,1,0:T(8,128)(2,1)S(1)} %pad_maximum_fusion.2), channel_id=1, source_target_pairs={{0,4},{4,0},{8,12},{12,8},{16,20},{20,16},{24,28},{28,24},{1,5},{5... | collective-permute-start | bytes 589832 | tf_op jit(solution)/shard_map/ppermute | solution.py:219
  32.2 13.0 %collective-permute-start.9 = (bf16[2,2,2,96,128]{4,3,2,1,0:T(8,128)(2,1)S(1)}, bf16[2,2,2,96,128]{4,3,2,1,0:T(8,128)(2,1)S(1)}, u32[]{:S(2)}, u32[]{:S(2)}) collective-permute-start(bf16[2,2,2,96,128]{4,3,2,1,0:T(8,128)(2,1)S(1)} %pad_maximum_fusion.3), channel_id=1, source_target_pairs={{4,8},{8,4},{12,16},{16,12},{20,24},{24,20},{5,9},{9,5},{13,17},{1... | collective-permute-start | bytes 589832 | tf_op jit(solution)/shard_map/ppermute | solution.py:220
  32.9 23.7 %collective-permute-start.3 = (bf16[2,2,2,96,128]{4,3,2,1,0:T(8,128)(2,1)S(1)}, bf16[2,2,2,96,128]{4,3,2,1,0:T(8,128)(2,1)S(1)}, u32[]{:S(2)}, u32[]{:S(2)}) collective-permute-start(bf16[2,2,2,96,128]{4,3,2,1,0:T(8,128)(2,1)S(1)} %pad_maximum_fusion.1), channel_id=1, source_target_pairs={{4,8},{8,4},{12,16},{16,12},{20,24},{24,20},{5,9},{9,5},{13,17},{1... | collective-permute-start | bytes 589832 | tf_op jit(solution)/shard_map/ppermute | solution.py:220
  33.6 23.0 %copy-start.6 = (bf16[2,2,384,128]{3,2,1,0:T(8,128)(2,1)S(1)}, bf16[2,2,384,128]{3,2,1,0:T(8,128)(2,1)}, u32[]{:S(2)}) copy-start(bf16[2,2,384,128]{3,2,1,0:T(8,128)(2,1)} %copy-done.5) | copy-start | bytes 1179652
  33.6 23.0 %collective-permute-start.2 = (bf16[2,2,2,96,128]{4,3,2,1,0:T(8,128)(2,1)S(1)}, bf16[2,2,2,96,128]{4,3,2,1,0:T(8,128)(2,1)S(1)}, u32[]{:S(2)}, u32[]{:S(2)}) collective-permute-start(bf16[2,2,2,96,128]{4,3,2,1,0:T(8,128)(2,1)S(1)} %pad_maximum_fusion), channel_id=1, source_target_pairs={{0,4},{4,0},{8,12},{12,8},{16,20},{20,16},{24,28},{28,24},{1,5},{5... | collective-permute-start | bytes 589832 | tf_op jit(solution)/shard_map/ppermute | solution.py:219
  45.2 1.0 %copy-start.8 = (bf16[2,2,384,128]{3,2,1,0:T(8,128)(2,1)S(1)}, bf16[2,2,384,128]{3,2,1,0:T(8,128)(2,1)}, u32[]{:S(2)}) copy-start(bf16[2,2,384,128]{3,2,1,0:T(8,128)(2,1)} %copy-done.7) | copy-start | bytes 1179652
  55.0 11.0 %copy-start.3 = (bf16[2,2,128,384]{3,2,1,0:T(8,128)(2,1)}, bf16[2,2,128,384]{3,2,1,0:T(8,128)(2,1)S(1)}, u32[]{:S(2)}) copy-start(bf16[2,2,128,384]{3,2,1,0:T(8,128)(2,1)S(1)} %get-tuple-element.19.refs_4_) | copy-start | bytes 1179652
  55.0 11.5 %collective-permute-start.11 = (bf16[2,2,128,384]{3,2,1,0:T(8,128)(2,1)S(1)}, bf16[2,2,128,384]{3,2,1,0:T(8,128)(2,1)S(1)}, u32[]{:S(2)}, u32[]{:S(2)}) collective-permute-start(bf16[2,2,128,384]{3,2,1,0:T(8,128)(2,1)S(1)} %get-tuple-element.20), channel_id=1, source_target_pairs={{0,2},{1,3},{2,0},{3,1},{4,6},{5,7},{6,4},{7,5},{8,10},{9,11},{10,... | collective-permute-start | bytes 1179656 | tf_op jit(solution)/shard_map/ppermute | solution.py:249
  65.5 7.9 %copy-start.4 = (bf16[2,2,128,384]{3,2,1,0:T(8,128)(2,1)}, bf16[2,2,128,384]{3,2,1,0:T(8,128)(2,1)S(1)}, u32[]{:S(2)}) copy-start(bf16[2,2,128,384]{3,2,1,0:T(8,128)(2,1)S(1)} %get-tuple-element.15.refs_0_) | copy-start | bytes 1179652
  65.5 7.8 %collective-permute-start.5 = (bf16[2,2,128,384]{3,2,1,0:T(8,128)(2,1)S(1)}, bf16[2,2,128,384]{3,2,1,0:T(8,128)(2,1)S(1)}, u32[]{:S(2)}, u32[]{:S(2)}) collective-permute-start(bf16[2,2,128,384]{3,2,1,0:T(8,128)(2,1)S(1)} %get-tuple-element.16), channel_id=1, source_target_pairs={{0,2},{1,3},{2,0},{3,1},{4,6},{5,7},{6,4},{7,5},{8,10},{9,11},{10,... | collective-permute-start | bytes 1179656 | tf_op jit(solution)/shard_map/ppermute | solution.py:249
  66.0 7.3 %collective-permute-start.10 = (bf16[2,2,128,384]{3,2,1,0:T(8,128)(2,1)S(1)}, bf16[2,2,128,384]{3,2,1,0:T(8,128)(2,1)S(1)}, u32[]{:S(2)}, u32[]{:S(2)}) collective-permute-start(bf16[2,2,128,384]{3,2,1,0:T(8,128)(2,1)S(1)} %get-tuple-element.19.refs_4_), channel_id=1, source_target_pairs={{0,1},{1,0},{2,3},{3,2},{4,5},{5,4},{6,7},{7,6},{8,9},{9,8},{10,11... | collective-permute-start | bytes 1179656 | tf_op jit(solution)/shard_map/ppermute | solution.py:248
  66.0 7.3 %collective-permute-start.4 = (bf16[2,2,128,384]{3,2,1,0:T(8,128)(2,1)S(1)}, bf16[2,2,128,384]{3,2,1,0:T(8,128)(2,1)S(1)}, u32[]{:S(2)}, u32[]{:S(2)}) collective-permute-start(bf16[2,2,128,384]{3,2,1,0:T(8,128)(2,1)S(1)} %get-tuple-element.15.refs_0_), channel_id=1, source_target_pairs={{0,1},{1,0},{2,3},{3,2},{4,5},{5,4},{6,7},{7,6},{8,9},{9,8},{10,11... | collective-permute-start | bytes 1179656 | tf_op jit(solution)/shard_map/ppermute | solution.py:248
  66.6 6.8 %copy-start.9 = (bf16[2,2,128,384]{3,2,1,0:T(8,128)(2,1)}, bf16[2,2,128,384]{3,2,1,0:T(8,128)(2,1)S(1)}, u32[]{:S(2)}) copy-start(bf16[2,2,128,384]{3,2,1,0:T(8,128)(2,1)S(1)} %collective-permute-done.11.refs_6_) | copy-start | bytes 1179652
  66.6 6.9 %collective-permute-start.12 = (bf16[2,2,128,384]{3,2,1,0:T(8,128)(2,1)S(1)}, bf16[2,2,128,384]{3,2,1,0:T(8,128)(2,1)S(1)}, u32[]{:S(2)}, u32[]{:S(2)}) collective-permute-start(bf16[2,2,128,384]{3,2,1,0:T(8,128)(2,1)S(1)} %collective-permute-done.11.refs_6_), channel_id=1, source_target_pairs={{0,1},{1,0},{2,3},{3,2},{4,5},{5,4},{6,7},{7,6},{8,9},{9,8},{10,11... | collective-permute-start | bytes 1179656 | tf_op jit(solution)/shard_map/ppermute | solution.py:248
  73.3 1.7 %copy-start.10 = (bf16[2,2,128,384]{3,2,1,0:T(8,128)(2,1)}, bf16[2,2,128,384]{3,2,1,0:T(8,128)(2,1)S(1)}, u32[]{:S(2)}) copy-start(bf16[2,2,128,384]{3,2,1,0:T(8,128)(2,1)S(1)} %collective-permute-done.5.refs_2_) | copy-start | bytes 1179652
  73.3 1.7 %collective-permute-start.6 = (bf16[2,2,128,384]{3,2,1,0:T(8,128)(2,1)S(1)}, bf16[2,2,128,384]{3,2,1,0:T(8,128)(2,1)S(1)}, u32[]{:S(2)}, u32[]{:S(2)}) collective-permute-start(bf16[2,2,128,384]{3,2,1,0:T(8,128)(2,1)S(1)} %collective-permute-done.5.refs_2_), channel_id=1, source_target_pairs={{0,1},{1,0},{2,3},{3,2},{4,5},{5,4},{6,7},{7,6},{8,9},{9,8},{10,11... | collective-permute-start | bytes 1179656 | tf_op jit(solution)/shard_map/ppermute | solution.py:248
  73.4 1.7 %copy-start.11 = (bf16[2,2,128,384]{3,2,1,0:T(8,128)(2,1)}, bf16[2,2,128,384]{3,2,1,0:T(8,128)(2,1)S(1)}, u32[]{:S(2)}) copy-start(bf16[2,2,128,384]{3,2,1,0:T(8,128)(2,1)S(1)} %collective-permute-done.10.refs_5_) | copy-start | bytes 1179652
  73.4 1.7 %copy-start.12 = (bf16[2,2,128,384]{3,2,1,0:T(8,128)(2,1)}, bf16[2,2,128,384]{3,2,1,0:T(8,128)(2,1)S(1)}, u32[]{:S(2)}) copy-start(bf16[2,2,128,384]{3,2,1,0:T(8,128)(2,1)S(1)} %collective-permute-done.4.refs_1_) | copy-start | bytes 1179652
  73.4 1.7 %copy-start.13 = (bf16[2,2,128,384]{3,2,1,0:T(8,128)(2,1)}, bf16[2,2,128,384]{3,2,1,0:T(8,128)(2,1)S(1)}, u32[]{:S(2)}) copy-start(bf16[2,2,128,384]{3,2,1,0:T(8,128)(2,1)S(1)} %collective-permute-done.12.refs_7_) | copy-start | bytes 1179652
  75.1 0.7 copy-start.14

commit v2 on v0

v2 whole, which is shorter than its diff:
```python
import functools

import jax
import jax.numpy as jnp
from jax import lax
from jax.experimental import pallas as pl
from jax.experimental.pallas import tpu as pltpu
from jax.sharding import PartitionSpec as P

TILE = 96
VMEM = pl.BlockSpec(memory_space=pltpu.VMEM)
SMEM = pl.BlockSpec(memory_space=pltpu.SMEM)
ANY = pl.BlockSpec(memory_space=pl.ANY)
HBM = pl.BlockSpec(memory_space=pltpu.HBM)
SHORT = pl.CostEstimate(flops=1000, bytes_accessed=1000, transcendentals=0)


def near_core(*values):
    return [pltpu.with_memory_space_constraint(v, pltpu.VMEM) for v in values]


def in_hbm(value):
    return pltpu.with_memory_space_constraint(value, pltpu.HBM)


def params(mebibytes):
    return pltpu.CompilerParams(vmem_limit_bytes=mebibytes << 20)


def coupling_kernel(place_ref, index_hbm_ref, value_hbm_ref, out_ref, index_ref, value_ref, done):
    copies = [
        pltpu.make_async_copy(index_hbm_ref, index_ref, done.at[0]),
        pltpu.make_async_copy(value_hbm_ref, value_ref, done.at[1]),
    ]
    for copy in copies:
        copy.start()
    for copy in copies:
        copy.wait()
    me = place_ref[0]
    nkl, terms, _ = out_ref.shape
    share = terms // 4
    half = terms // 2

    def arrange(v):
        low, high = v[:, :half], v[:, half:]
        flip = (me >> 1) == 1
        first, second = jnp.where(flip, high, low), jnp.where(flip, low, high)
        shift = (me & 1) * share
        return jnp.concatenate([pltpu.roll(first, shift, 1), pltpu.roll(second, shift, 1)], axis=1)

    def one_term(k, carry):
        index = arrange(index_ref[k] ^ (me * share)).astype(jnp.float32).astype(jnp.bfloat16)
        value = arrange(value_ref[k].astype(jnp.float32)).astype(jnp.bfloat16)
        chunk = terms // 4
        for part in range(terms // chunk):
            j = lax.broadcasted_iota(jnp.int32, (chunk, terms), 0) + part * chunk
            j = j.astype(jnp.float32).astype(jnp.bfloat16)
            dense = jnp.zeros((chunk, terms), jnp.bfloat16)
            for n in range(index.shape[0]):
                dense = jnp.where(index[n : n + 1, :] == j, value[n : n + 1, :], dense)
            out_ref[k, part * chunk : (part + 1) * chunk, :] = dense
        return carry

    lax.fori_loop(0, nkl, one_term, 0)


def dense_coupling(place, chaos_index, chaos_value):
    nkl, terms, nzc = chaos_index.shape
    return pl.pallas_call(
        coupling_kernel,
        in_specs=[SMEM, ANY, ANY],
        out_specs=VMEM,
        scratch_shapes=[
            pltpu.VMEM((nkl, nzc, terms), chaos_index.dtype),
            pltpu.VMEM((nkl, nzc, terms), chaos_value.dtype),
            pltpu.SemaphoreType.DMA((2,)),
        ],
        out_shape=pltpu.VMEM((nkl, terms, terms), jnp.bfloat16),
        compiler_params=params(8),
        cost_estimate=SHORT,
    )(place, in_hbm(jnp.swapaxes(chaos_index, 1, 2)), in_hbm(jnp.swapaxes(chaos_value, 1, 2)))


def tiles_kernel(_, tiles_hbm_ref, out_ref, tiles_ref, done):
    blocks, nnz, nkl = tiles_ref.shape[:3]
    copies = [pltpu.make_async_copy(tiles_hbm_ref.at[b], tiles_ref.at[b], done.at[b]) for b in range(blocks)]
    for copy in copies:
        copy.start()
    for b in range(blocks):
        copies[b].wait()
        for s in range(nnz):
            for part in range(2):
                out_ref[b, s, part * TILE : (part + 1) * TILE, :] = jnp.concatenate(
                    [tiles_ref[b, s, k, part] for k in range(nkl)], axis=1
                )


def wide_tiles(place, stiff_tiles):
    blocks, nnz, nkl = stiff_tiles.shape[:3]
    return pl.pallas_call(
        tiles_kernel,
        in_specs=[SMEM, ANY],
        out_specs=VMEM,
        scratch_shapes=[pltpu.VMEM(stiff_tiles.shape, stiff_tiles.dtype), pltpu.SemaphoreType.DMA((blocks,))],
        out_shape=pltpu.VMEM((blocks, nnz, 2 * TILE, nkl * TILE), jnp.bfloat16),
        compiler_params=params(8),
        cost_estimate=SHORT,
    )(place, in_hbm(stiff_tiles))


def pack_kernel(place_ref, own_ref, near_ref, *refs):
    out_refs, (staged, rows, done), packed = refs[:6], refs[6:9], refs[9:]
    (send_outer, send_inner, keep_outer, keep_inner), pair_refs = packed[:4], packed[4:]
    me, odd_place = place_ref[0], place_ref[1] == 1
    terms, parts, loads, width = own_ref.shape
    copies = [
        [pltpu.make_async_copy(ref.at[:, c], staged.at[q, :, c], done.at[2 * c + q]) for q, ref in enumerate((own_ref, near_ref))]
        for c in range(parts)
    ]
    for pair in copies:
        for copy in pair:
            copy.start()
    out_copies = []
    cases = loads // 4
    lanes = rows.shape[3]
    for c in range(parts):
        for copy in copies[c]:
            copy.wait()
        for t in range(width // lanes):
            for q in range(2):
                piece = staged[q, :, c, :, t * lanes : (t + 1) * lanes].astype(jnp.float32)
                rows[c, t, q * terms * loads : (q + 1) * terms * loads] = piece.reshape(terms * loads, lanes)
            first, last = t * lanes, (t + 1) * lanes
            for m in range(cases):
                for outer, inner, x in ((send_outer, send_inner, 1 - (me >> 1)), (keep_outer, keep_inner, me >> 1)):
                    r = 4 * m + 2 * (me & 1) + x
                    both = rows[c, t, pl.ds(r, 2 * terms, stride=loads), :].astype(jnp.bfloat16).T
                    for ref, low, high, base in (
                        (outer, 0, TILE, 0),
                        (inner, TILE, width - TILE, 0),
                        (outer, width - TILE, width, TILE),
                    ):
                        low_row, high_row = max(low, first), min(high, last)
                        if low_row < high_row:
                            ref[m, c, base + low_row - low : base + high_row - low] = both[low_row - first : high_row - first]
        for m in range(cases):
            low, high = keep_outer[m, c, :TILE], keep_outer[m, c, TILE:]
            pair_refs[0][m, c] = jnp.where(odd_place, low, high)
            pair_refs[1][m, c] = jnp.where(odd_place, high, low)
        for i, (source, target) in enumerate(zip(packed, out_refs)):
            out_copies.append(pltpu.make_async_copy(source.at[:, c], target.at[:, c], done.at[2 * parts + 6 * c + i]))
            out_copies[-1].start()
    for copy in out_copies:
        copy.wait()


def pack(place, own, near):
    terms, parts, loads, width = own.shape
    cases = loads // 4
    shapes = [(cases, parts, 2 * TILE, 2 * terms), (cases, parts, width - 2 * TILE, 2 * terms)] * 2
    shapes += [(cases, parts, TILE, 2 * terms)] * 2
    return pl.pallas_call(
        pack_kernel,
        in_specs=[SMEM, ANY, ANY],
        out_specs=[HBM] * 6,
        scratch_shapes=[
            pltpu.VMEM((2, *near.shape), near.dtype),
            pltpu.VMEM((parts, width // 128, 2 * terms * loads, 128), jnp.float32),
            pltpu.SemaphoreType.DMA((8 * parts,)),
            *[pltpu.VMEM(shape, near.dtype) for shape in shapes],
        ],
        out_shape=[pltpu.HBM(shape, near.dtype) for shape in shapes],
        compiler_params=params(20),
        cost_estimate=SHORT,
    )(place, in_hbm(own), near)


def outer_kernel(place_ref, own_ref, far_ref, field_ref, even_ref, odd_ref, done):
    odd_place = place_ref[1] == 1
    cases, parts, _, half = own_ref.shape
    copies = [
        pltpu.make_async_copy(ref, field_ref.at[:, :, :, pl.ds(q * half, half)], done.at[q])
        for q, ref in ((1, far_ref), (0, own_ref))
    ]
    for copy in copies:
        copy.start()
    copies[0].wait()
    for m in range(cases):
        for c in range(parts):
            low, high = field_ref[m, c, :TILE, half:], field_ref[m, c, TILE:, half:]
            even_ref[m, c] = jnp.where(odd_place, low, high)
            odd_ref[m, c] = jnp.where(odd_place, high, low)
    copies[1].wait()


def gather_outer(place, own, far):
    cases, parts, height, half = own.shape
    edge = pltpu.VMEM((cases, parts, TILE, half), jnp.bfloat16)
    return pl.pallas_call(
        outer_kernel,
        in_specs=[SMEM, ANY, ANY],
        out_specs=[VMEM] * 3,
        scratch_shapes=[pltpu.SemaphoreType.DMA((2,))],
        out_shape=[pltpu.VMEM((cases, parts, height, 2 * half), jnp.bfloat16), edge, edge],
        compiler_params=params(4),
        cost_estimate=SHORT,
    )(place, in_hbm(own), far)


def swap(even, odd):
    count = lax.axis_size("space")
    even_pairs = [(i, i ^ 1) for i in range(count)]
    odd_pairs = [(i, ((i - 1) ^ 1) + 1) for i in range(1, count - 1)]
    return lax.ppermute(even, "space", even_pairs), lax.ppermute(odd, "space", odd_pairs)


def mix(fields, coupling_ref, slots, mixed):
    nkl, terms, _ = coupling_ref.shape
    for k in range(nkl):
        rows = slice(k * TILE, (k + 1) * TILE)
        for c, field in enumerate(fields):
            sums = jnp.dot(field, coupling_ref[k], preferred_element_type=jnp.float32).astype(jnp.bfloat16)
            for g, slot in enumerate(slots):
                mixed[slot, rows, c * terms : (c + 1) * terms] = sums[g * TILE : (g + 1) * TILE]


def mix_outer_kernel(field_ref, coupling_ref, mixed):
    def one_case(m, carry):
        mix([field_ref[m, c] for c in range(2)], coupling_ref, (0, mixed.shape[1] - 3), mixed.at[m])
        return carry

    lax.fori_loop(0, field_ref.shape[0], one_case, 0)


def mix_outer(field, coupling, blocks):
    cases, _, height, terms = field.shape
    nkl = coupling.shape[0]
    return pl.pallas_call(
        mix_outer_kernel,
        in_specs=[VMEM] * 2,
        out_specs=VMEM,
        out_shape=pltpu.VMEM((cases, blocks + 2, nkl * TILE, 2 * terms), jnp.bfloat16),
        compiler_params=params(4),
        cost_estimate=SHORT,
    )(*near_core(field, coupling))


def mix_inner_kernel(own_ref, far_ref, *refs):
    edge_refs = refs[: (len(refs) - 5) // 2]
    coupling_ref, _, mixed, *staged_refs, field_ref, done = refs[len(edge_refs) :]
    half = own_ref.shape[3]
    pairs = [
        (far_ref, field_ref.at[:, :, :, pl.ds(half, half)]),
        (own_ref, field_ref.at[:, :, :, pl.ds(0, half)]),
        *zip(edge_refs, staged_refs),
    ]
    copies = [pltpu.make_async_copy(source, target, done.at[i]) for i, (source, target) in enumerate(pairs)]
    for copy in copies:
        copy.start()
    for copy in copies[:2]:
        copy.wait()

    def one_case(m, carry):
        mix([field_ref[m, c] for c in range(2)], coupling_ref, range(1, mixed.shape[1] - 3), mixed.at[m])
        return carry

    lax.fori_loop(0, field_ref.shape[0], one_case, 0)
    for copy in copies[2:]:
        copy.wait()


def mix_inner(own, far, edges, coupling, mixed):
    cases, parts, height, half = own.shape
    nkl, terms, _ = coupling.shape
    count = len(edges)
    return pl.pallas_call(
        mix_inner_kernel,
        in_specs=[ANY] * (2 + count) + [VMEM] * 2,
        out_specs=[VMEM] * (1 + count),
        scratch_shapes=[
            pltpu.VMEM((cases, parts, height, terms), jnp.bfloat16),
            pltpu.SemaphoreType.DMA((2 + count,)),
        ],
        out_shape=[pltpu.VMEM(mixed.shape, mixed.dtype)] + [pltpu.VMEM(v.shape, v.dtype) for v in edges],
        input_output_aliases={3 + count: 0},
        compiler_params=params(8),
        cost_estimate=SHORT,
    )(in_hbm(own), far, *edges, *near_core(coupling, mixed))


def tiles_apply_kernel(m, quarters, place_ref, columns_ref, *refs):
    *edge_refs, coupling_ref, tiles_ref, _ = refs[:7]
    *out_refs, whole, flipped = refs[7:]
    terms = coupling_ref.shape[1]
    blocks, nnz = tiles_ref.shape[:2]
    half = terms // 2
    low, high = half * quarters[0], half * (quarters[-1] + 1)
    mixed = whole.at[m]

    def outer(c):
        even, odd, far_even, far_odd = (ref[m, c] for ref in edge_refs)
        return jnp.concatenate(
            [jnp.concatenate([even, far_even], axis=1), jnp.concatenate([odd, far_odd], axis=1)], axis=0
        )

    def slot_of(column):
        odd_place = place_ref[1]
        outside = jnp.where(column == 0, blocks + 1 - odd_place, blocks + odd_place)
        return jnp.where((column == 0) | (column == blocks + 1), outside, column - 1)

    if quarters[-1] == 1:
        mix([outer(c) for c in range(2)], coupling_ref, (blocks, blocks + 1), mixed)
    count = high - low
    for b in range(blocks):
        acc = None
        for s in range(nnz):
            slot = slot_of(columns_ref[b, s])
            field = jnp.concatenate([mixed[slot, :, c * terms + low : c * terms + high] for c in range(2)], axis=1)
            term = jnp.dot(tiles_ref[b, s], field, preferred_element_type=jnp.float32)
            acc = term if acc is None else acc + term
        rows = slice(b * TILE, (b + 1) * TILE)
        flipped[0, rows, :count] = (acc[:TILE, :count] - acc[TILE:, count:]).astype(jnp.bfloat16)
        flipped[1, rows, :count] = (acc[:TILE, count:] + acc[TILE:, :count]).astype(jnp.bfloat16)
    for c in range(2):
        part = flipped[c, :, :count].T
        for i, ref in enumerate(out_refs):
            ref[c] = part[i * half : (i + 1) * half]


def apply_tiles(m, place, columns, edges, coupling, tiles, mixed, quarters=(0, 1)):
    blocks, nnz, rows, depth = tiles.shape
    terms = coupling.shape[1]
    out = pltpu.VMEM((2, terms // 2, blocks * TILE), jnp.bfloat16)
    count = len(quarters)
    return pl.pallas_call(
        functools.partial(tiles_apply_kernel, m, quarters),
        in_specs=[SMEM] * 2 + [VMEM] * 7,
        out_specs=[VMEM] * (count + 1),
        scratch_shapes=[pltpu.VMEM((2, blocks * TILE, terms), jnp.bfloat16)],
        out_shape=[out] * count + [pltpu.VMEM(mixed.shape, mixed.dtype)],
        input_output_aliases={8: count},
        compiler_params=params(8),
        cost_estimate=SHORT,
    )(place, columns, *near_core(*edges, coupling, tiles, mixed))


def unpack_kernel(chunk, place_ref, *refs):
    me = place_ref[0]
    *piece_refs, out_ref, rows, done = refs
    parts, half, width = piece_refs[0].shape
    terms = half // 2
    loads = out_ref.shape[1] // 2
    lanes = rows.shape[2]
    copies = []
    for t in range(width // lanes):
        for position in range(loads):
            m, source = position // 4, me ^ (position % 4)
            r = 4 * m + 2 * (source & 1) + (source >> 1)
            first = terms * (position % 2)
            for c in range(parts):
                part = piece_refs[position][c, first : first + terms, t * lanes : (t + 1) * lanes]
                rows[t, pl.ds(c * loads + r, terms, stride=parts * loads), :] = part.astype(jnp.float32)
        source = rows.at[t].reshape(terms * parts, loads, lanes)
        target = out_ref.at[:, loads * chunk : loads * (chunk + 1), t * lanes : (t + 1) * lanes]
        copies.append(pltpu.make_async_copy(source, target, done.at[t]))
        copies[-1].start()
    for copy in copies:
        copy.wait()


def unpack(place, chunk, pieces, whole=None):
    parts, half, width = pieces[0].shape
    terms = half // 2
    loads = len(pieces)
    specs = [SMEM] + [VMEM] * loads
    aliases = {}
    if whole is not None:
        aliases = {len(pieces) + 1: 0}
        pieces = [*pieces, whole]
        specs = [*specs, ANY]

    def kernel(place_ref, *refs):
        refs = list(refs)
        if aliases:
            refs.pop(loads)
        unpack_kernel(chunk, place_ref, *refs)

    return pl.pallas_call(
        kernel,
        in_specs=specs,
        out_specs=ANY,
        scratch_shapes=[
            pltpu.VMEM((width // 128, terms * parts * loads, 128), jnp.float32),
            pltpu.SemaphoreType.DMA((width // 128,)),
        ],
        out_shape=jax.ShapeDtypeStruct((terms * parts, 2 * loads, width), jnp.float32),
        input_output_aliases=aliases,
        compiler_params=params(8),
        cost_estimate=SHORT,
    )(place, *pieces)


def after(value, *others):
    return lax.optimization_barrier((value, others))[0]


def body(load_vectors, stiff_tiles, tile_columns, chaos_index, chaos_value):
    count = lax.axis_size("chaos")
    blocks = stiff_tiles.shape[0]
    odd_place = lax.axis_index("space") % 2

    if count != 4:
        place = jnp.stack([jnp.zeros((), jnp.int32), odd_place])
        coupling = dense_coupling(place, chaos_index, chaos_value)
        tiles = wide_tiles(place, stiff_tiles)
        mine = lax.all_to_all(load_vectors, "chaos", split_axis=2, concat_axis=0, tiled=True)
        field = mine.transpose(2, 1, 3, 0)
        half = field.shape[3] // 2
        low, high = field[:, :, :TILE], field[:, :, -TILE:]
        swapped = swap(jnp.where(odd_place == 1, low, high), jnp.where(odd_place == 1, high, low))
        edges = [v[..., :half] for v in swapped] + [v[..., half:] for v in swapped]
        inner = field[:, :, TILE:-TILE]
        mixed = mix_outer(jnp.concatenate([low, high], axis=2), coupling, blocks)
        mixed = mix_inner(inner[..., :half], inner[..., half:], [], coupling, mixed)[0]
        cases = []
        for m in range(field.shape[0]):
            keep, send, mixed = apply_tiles(m, place, tile_columns, edges, coupling, tiles, mixed)
            cases.append(jnp.concatenate([keep, send], axis=1))
        result = jnp.stack(cases, axis=0)
        result = lax.all_to_all(result, "chaos", split_axis=2, concat_axis=0, tiled=True)
        return result.transpose(2, 1, 0, 3).astype(jnp.float32)

    place = jnp.stack([lax.axis_index("chaos"), odd_place])
    near = lambda v: lax.ppermute(v, "chaos", [(i, i ^ 1) for i in range(4)])
    across = lambda v: lax.ppermute(v, "chaos", [(i, i ^ 2) for i in range(4)])
    near_loads = near(load_vectors)
    coupling = dense_coupling(place, chaos_index, chaos_value)
    place = after(place, coupling)
    send_outer, send_inner, outer, inner, even, odd = pack(place, load_vectors, near_loads)
    far_outer = across(send_outer)
    own_edges = swap(even, odd)
    tiles = wide_tiles(after(place, even), stiff_tiles)
    far_inner = across(after(send_inner, tiles))
    field, even, odd = gather_outer(after(place, tiles), outer, far_outer)
    far_edges = swap(even, odd)
    mixed = mix_outer(field, coupling, blocks)
    mixed, *own_edges = mix_inner(inner, far_inner, own_edges, coupling, mixed)
    cases = field.shape[0]
    edges = [*own_edges, *far_edges]
    kept, near_kept, sent = [], [], []
    for m in range(cases):
        ready = after(place, *near_kept[m - 2 : m - 1], *sent[m - 3 : m - 2]) if m >= 2 else place
        given = ready, tile_columns, edges, coupling, tiles
        if m < cases - 1:
            keep, send, mixed = apply_tiles(m, *given, mixed)
        else:
            send, mixed = apply_tiles(m, *given, mixed, (1,))
            keep, mixed = apply_tiles(m, after(place, near_kept[m - 1], sent[m - 2]), *given[1:], mixed, (0,))
        kept.append(keep)
        near_kept.append(near(keep))
        sent.append(across(send))
    result = None
    for chunk in range(2):
        pieces = []
        for m in (2 * chunk, 2 * chunk + 1):
            back = after(sent[m], kept[-1] if result is None else result)
            pieces += [kept[m], near_kept[m], back, near(back)]
        result = unpack(after(place, sent[2]), chunk, pieces, result)
    return result.reshape(load_vectors.shape)


def solution(mesh):
    in_specs = (
        P("chaos", None, None, "space"),
        P("space", None, None, None, None, None),
        P("space", None),
        P(),
        P(),
    )
    out_specs = P("chaos", None, None, "space")
    return jax.shard_map(body, mesh=mesh, in_specs=in_specs, out_specs=out_specs, check_vma=False)
```

time: 237 us -> 64.6 us (0.27)
  local copies, waits for them, and re-layouts: 96.5 us -> 0.01 us
  blocking collectives: 40.6 us -> 0 us
  Pallas kernels: 0 us -> 38 us
  matrix products: 34.7 us -> 0 us
  other arithmetic: 29.5 us -> 0.07 us
  waiting for transfers between devices: 22.6 us -> 11.6 us
  starting transfers between devices: 10.6 us -> 14.3 us
    gather x7 -> x0, local copies, waits for them, and re-layouts: 59.8 us -> none  [body(): columns = jnp.take(coupled_field, tile_columns[:, tile_slot], axis=4)]
    all_to_all x1 -> x0, blocking collectives: 40.6 us -> none  [body(): lax.all_to_all(result, 'chaos', split_axis=0, concat_axis=2, tiled=True)]
    pallas_call x0 -> x13, Pallas kernels: none -> 38 us  [the longest x5 13.9 us: apply_tiles(): pl.pallas_call(functools.partial(tiles_apply_kernel, m, quarters), in_spe...]
    dot_general x4 -> x0, matrix products: 34.7 us -> none  [the longest x3 24.3 us: body(): jnp.einsum('bkcdxy,kidrby->icrbx', complex_tiles[:, tile_slot], columns,...]
    reduce_sum x8 -> x0, other arithmetic: 22.8 us -> none  [one_term(): jnp.where(matches, row_value[:, :, None], jnp.zeros((), jnp.bfloat16))]
    all_to_all x1 -> x0, waiting for transfers between devices: 22.6 us -> none  [body(): lax.all_to_all(extended, 'chaos', split_axis=2, concat_axis=0, tiled=True)]
    ppermute x2 -> x19, waiting for transfers between devices: 0.01 us -> 11.6 us  [the longest x6 9.75 us: body(): across = lambda v: lax.ppermute(v, 'chaos', [(i, i ^ 2) for i in range(4)])]
    ppermute x2 -> x19, starting transfers between devices: 6.81 us -> 14.3 us  [the longest x6 6.77 us: body(): across = lambda v: lax.ppermute(v, 'chaos', [(i, i ^ 2) for i in range(4)])]
  transfers between devices with their start and end apart: 3 -> 19, of which waited for: 1 -> 8; matrix products, arithmetic and copies ran while one was open for 21% -> 0% of each run, Pallas kernels for 0% -> 43%
where the time goes in v2:
time: 64.6 us; the launch traced here: 64.3 us
  Pallas kernels  38 us (59%)
  starting transfers between devices  14.3 us (22%)
  waiting for transfers between devices  11.6 us (18%)
    pallas_call x5, Pallas kernels, apply_tiles(): pl.pallas_call(functools.partial(tiles_apply_kernel, m, quarters), in_spe...  13.9 us
    ppermute x6, waiting for transfers between devices, body(): across = lambda v: lax.ppermute(v, 'chaos', [(i, i ^ 2) for i in range(4)])  9.75 us
    ppermute x6, starting transfers between devices, body(): across = lambda v: lax.ppermute(v, 'chaos', [(i, i ^ 2) for i in range(4)])  6.77 us
    pallas_call x1, Pallas kernels, pack(): pl.pallas_call(pack_kernel, in_specs=[SMEM, ANY, ANY], out_specs=[HBM] *...  4.62 us
    pallas_call x1, Pallas kernels, dense_coupling(): pl.pallas_call(coupling_kernel, in_specs=[SMEM, ANY, ANY], out_specs=VMEM...  4.59 us
    pallas_call x2, Pallas kernels, unpack(): pl.pallas_call(kernel, in_specs=specs, out_specs=ANY, scratch_shapes=[plt...  4.26 us
    ppermute x2, starting transfers between devices, swap(): lax.ppermute(even, 'space', even_pairs)  4.08 us
    pallas_call x1, Pallas kernels, mix_inner(): pl.pallas_call(mix_inner_kernel, in_specs=[ANY] * (2 + count) + [VMEM] *...  3.43 us
  transfers between devices with their start and end apart: 19, of which 8 were waited for; matrix products, arithmetic and copies ran while one was open for 0% of the time, Pallas kernels for 43%

profile of v2, /device:TPU:0, one launch (start us, length us, event | category | flops | bytes accessed | tf_op | source)
XLA Modules:
  0.0 64.3 jit_solution(11271954273247191455)
XLA Ops:
  0.0 0.5 collective-permute-start
  0.5 0.1 pad_add_fusion.place_ref._
  0.5 4.6 %shard_map.55.coupling_ref.refs_2_.refs_4_ = bf16[8,256,256]{2,1,0:T(8,128)(2,1)S(1)} custom-call(s32[2]{0:T(128)S(1)} %pad_add_fusion.place_ref._, s32[8,32,256]{2,1,0:T(8,128)} %bitcast.5, bf16[8,32,256]{2,1,0:T(8,128)(2,1)} %bitcast.6), custom_call_target="tpu_custom_call" | custom-call | flops 1000 | bytes 1000 | tf_op jit(solution)/shard_map/pallas_call | solution.py:69
  5.1 0.0 collective-permute-done.near_ref
  5.1 4.6 %shard_map.56 = (bf16[4,2,192,128]{3,2,1,0:T(8,128)(2,1)}, bf16[4,2,192,128]{3,2,1,0:T(8,128)(2,1)}, bf16[4,2,192,128]{3,2,1,0:T(8,128)(2,1)}, bf16[4,2,192,128]...) custom-call(s32[2]{0:T(128)S(1)} %pad_add_fusion.place_ref._, ...), custom_call_target="tpu_custom_call" | custom-call | flops 1000 | bytes 1000 | tf_op jit(solution)/shard_map/pallas_call | solution.py:162
  9.8 2.6 %collective-permute-start.4 = (bf16[4,2,192,128]{3,2,1,0:T(8,128)(2,1)}, bf16[4,2,192,128]{3,2,1,0:T(8,128)(2,1)S(1)}, u32[]{:S(2)}, u32[]{:S(2)}) collective-permute-start(bf16[4,2,192,128]{3,2,1,0:T(8,128)(2,1)} %get-tuple-element.50), channel_id=1, source_target_pairs={{0,2},{1,3},{2,0},{3,1},{4,6},{5,7},{6,4},{7,5},{8,10},{9,11},{10,... | collective-permute-start | bytes 1179656 | tf_op jit(solution)/shard_map/ppermute | solution.py:435
  12.3 3.2 %shard_map.57.refs_5_ = bf16[4,3,192,768]{3,2,1,0:T(8,128)(2,1)S(1)} custom-call(s32[2]{0:T(128)S(1)} %pad_add_fusion.place_ref._, bf16[4,3,8,2,96,96]{5,4,3,2,1,0:T(8,128)(2,1)} %tiles_hbm_ref.1), custom_call_target="tpu_custom_call" | custom-call | flops 1000 | bytes 1000 | tf_op jit(solution)/shard_map/pallas_call | solution.py:100
  15.5 0.1 collective-permute-start.1
  15.6 2.0 %collective-permute-start.2 = (bf16[4,2,96,128]{3,2,1,0:T(8,128)(2,1)}, bf16[4,2,96,128]{3,2,1,0:T(8,128)(2,1)S(1)}, u32[]{:S(2)}, u32[]{:S(2)}) collective-permute-start(bf16[4,2,96,128]{3,2,1,0:T(8,128)(2,1)} %get-tuple-element.44), channel_id=1, source_target_pairs={{0,4},{4,0},{8,12},{12,8},{16,20},{20,16},{24,28},{28,24},{1,5},{5... | collective-permute-start | bytes 589832 | tf_op jit(solution)/shard_map/ppermute | solution.py:214
  17.7 0.7 %collective-permute-start.3 = (bf16[4,2,96,128]{3,2,1,0:T(8,128)(2,1)}, bf16[4,2,96,128]{3,2,1,0:T(8,128)(2,1)S(1)}, u32[]{:S(2)}, u32[]{:S(2)}) collective-permute-start(bf16[4,2,96,128]{3,2,1,0:T(8,128)(2,1)} %get-tuple-element.47), channel_id=1, source_target_pairs={{4,8},{8,4},{12,16},{16,12},{20,24},{24,20},{5,9},{9,5},{13,17},{1... | collective-permute-start | bytes 589832 | tf_op jit(solution)/shard_map/ppermute | solution.py:214
  18.3 4.2 %collective-permute-done.4.far_ref = bf16[4,2,192,128]{3,2,1,0:T(8,128)(2,1)S(1)} collective-permute-done((bf16[4,2,192,128]{3,2,1,0:T(8,128)(2,1)}, bf16[4,2,192,128]{3,2,1,0:T(8,128)(2,1)S(1)}, u32[]{:S(2)}, u32[]{:S(2)}) %collective-permute-start.4) | collective-permute-done | bytes 393248 | tf_op jit(solution)/shard_map/ppermute | solution.py:435
  22.5 1.6 %shard_map.58 = (bf16[4,2,192,256]{3,2,1,0:T(8,128)(2,1)S(1)}, bf16[4,2,96,128]{3,2,1,0:T(8,128)(2,1)S(1)}, bf16[4,2,96,128]{3,2,1,0:T(8,128)(2,1)S(1)}) custom-call(s32[2]{0:T(128)S(1)} %pad_add_fusion.place_ref._, bf16[4,2,192,128]{3,2,1,0:T(8,128)(2,1)} %get-tuple-element.49.own_ref, bf16[4,2,192,128]{3,2,1,0:T(8,128)(2,1)S(1)} %collective-permute-done.4.far_ref), custom_call_target="tpu_custom_call" | custom-call | flops 1000 | bytes 1000 | tf_op jit(solution)/shard_map/pallas_call | solution.py:199
  24.1 2.0 %collective-permute-start.5 = (bf16[4,2,96,128]{3,2,1,0:T(8,128)(2,1)S(1)}, bf16[4,2,96,128]{3,2,1,0:T(8,128)(2,1)S(1)}, u32[]{:S(2)}, u32[]{:S(2)}) collective-permute-start(bf16[4,2,96,128]{3,2,1,0:T(8,128)(2,1)S(1)} %get-tuple-element.54), channel_id=1, source_target_pairs={{0,4},{4,0},{8,12},{12,8},{16,20},{20,16},{24,28},{28,24},{1,5},{5... | collective-permute-start | bytes 589832 | tf_op jit(solution)/shard_map/ppermute | solution.py:214
  26.2 0.8 %collective-permute-start.6 = (bf16[4,2,96,128]{3,2,1,0:T(8,128)(2,1)S(1)}, bf16[4,2,96,128]{3,2,1,0:T(8,128)(2,1)S(1)}, u32[]{:S(2)}, u32[]{:S(2)}) collective-permute-start(bf16[4,2,96,128]{3,2,1,0:T(8,128)(2,1)S(1)} %get-tuple-element.55), channel_id=1, source_target_pairs={{4,8},{8,4},{12,16},{16,12},{20,24},{24,20},{5,9},{9,5},{13,17},{1... | collective-permute-start | bytes 589832 | tf_op jit(solution)/shard_map/ppermute | solution.py:214
  27.0 0.0 copy-start
  27.0 2.4 %shard_map.59.refs_3_ = bf16[4,6,768,512]{3,2,1,0:T(8,128)(2,1)S(1)} custom-call(bf16[4,2,192,256]{3,2,1,0:T(8,128)(2,1)S(1)} %get-tuple-element.51.field_ref, bf16[8,256,256]{2,1,0:T(8,128)(2,1)S(1)} %shard_map.55.coupling_ref.refs_2_.refs_4_), custom_call_target="tpu_custom_call" | custom-call | flops 1000 | bytes 1000 | tf_op jit(solution)/shard_map/pallas_call | solution.py:238
  29.4 0.0 collective-permute-done.3.refs_1_
  29.4 0.0 collective-permute-done.2.refs_0_
  29.4 1.3 %collective-permute-done.1.far_ref = bf16[4,2,192,128]{3,2,1,0:T(8,128)(2,1)S(1)} collective-permute-done((bf16[4,2,192,128]{3,2,1,0:T(8,128)(2,1)}, bf16[4,2,192,128]{3,2,1,0:T(8,128)(2,1)S(1)}, u32[]{:S(2)}, u32[]{:S(2)}) %collective-permute-start.1) | collective-permute-done | bytes 393248 | tf_op jit(solution)/shard_map/ppermute | solution.py:435
  30.7 3.4 %shard_map.60 = (bf16[4,6,768,512]{3,2,1,0:T(8,128)(2,1)S(1)}, bf16[4,2,96,128]{3,2,1,0:T(8,128)(2,1)S(1)}, bf16[4,2,96,128]{3,2,1,0:T(8,128)(2,1)S(1)}) custom-call(bf16[4,2,192,128]{3,2,1,0:T(8,128)(2,1)} %get-tuple-element.42.own_ref, bf16[4,2,192,128]{3,2,1,0:T(8,128)(2,1)S(1)} %collective-permute-done.1.far_ref, ...), custom_call_target="tpu_custom_call", output_to_operand_aliasing={{0}: (5, {})} | custom-call | flops 1000 | bytes 1000 | tf_op jit(solution)/shard_map/pallas_call | solution.py:276
  34.2 0.6 collective-permute-done.5.refs_2_
  34.8 0.0 collective-permute-done.6.refs_3_
  34.8 0.0 copy-done
  34.8 3.2 %shard_map.61 = (bf16[2,128,384]{2,1,0:T(8,128)(2,1)S(1)}, bf16[2,128,384]{2,1,0:T(8,128)(2,1)S(1)}, bf16[4,6,768,512]{3,2,1,0:T(8,128)(2,1)S(1)}) custom-call(s32[2]{0:T(128)S(1)} %pad_add_fusion.place_ref._, s32[4,3]{1,0:T(4,128)S(1)} %copy-done, bf16[4,2,96,128]{3,2,1,0:T(8,128)(2,1)S(1)} %get-tuple-element.52.refs_0_, ...), custom_call_target="tpu_custom_call", output_to_operand_aliasing={{2}: (8, {})} | custom-call | flops 1000 | bytes 1000 | tf_op jit(solution)/shard_map/pallas_call | solution.py:335
  38.0 0.1 collective-permute-start.7
  38.1 1.5 %collective-permute-start.10 = (bf16[2,128,384]{2,1,0:T(8,128)(2,1)S(1)}, bf16[2,128,384]{2,1,0:T(8,128)(2,1)S(1)}, u32[]{:S(2)}, u32[]{:S(2)}) collective-permute-start(bf16[2,128,384]{2,1,0:T(8,128)(2,1)S(1)} %get-tuple-element.64), channel_id=1, source_target_pairs={{0,2},{1,3},{2,0},{3,1},{4,6},{5,7},{6,4},{7,5},{8,10},{9,11},{10,... | collective-permute-start | bytes 589832 | tf_op jit(solution)/shard_map/ppermute | solution.py:435
  39.7 3.3 %shard_map.62 = (bf16[2,128,384]{2,1,0:T(8,128)(2,1)S(1)}, bf16[2,128,384]{2,1,0:T(8,128)(2,1)S(1)}, bf16[4,6,768,512]{3,2,1,0:T(8,128)(2,1)S(1)}) custom-call(s32[2]{0:T(128)S(1)} %pad_add_fusion.place_ref._, s32[4,3]{1,0:T(4,128)S(1)} %copy-done, bf16[4,2,96,128]{3,2,1,0:T(8,128)(2,1)S(1)} %get-tuple-element.52.refs_0_, ...), custom_call_target="tpu_custom_call", output_to_operand_aliasing={{2}: (8, {})} | custom-call | flops 1000 | bytes 1000 | tf_op jit(solution)/shard_map/pallas_call | solution.py:335
  42.9 0.2 collective-permute-start.12
  43.2 0.5 collective-permute-start.11
  43.7 0.0 collective-permute-done.7.refs_1_
  43.7 3.2 %shard_map.63 = (bf16[2,128,384]{2,1,0:T(8,128)(2,1)S(1)}, bf16[2,128,384]{2,1,0:T(8,128)(2,1)S(1)}, bf16[4,6,768,512]{3,2,1,0:T(8,128)(2,1)S(1)}) custom-call(s32[2]{0:T(128)S(1)} %pad_add_fusion.place_ref._, s32[4,3]{1,0:T(4,128)S(1)} %copy-done, bf16[4,2,96,128]{3,2,1,0:T(8,128)(2,1)S(1)} %get-tuple-element.52.refs_0_, ...), custom_call_target="tpu_custom_call", output_to_operand_aliasing={{2}: (8, {})} | custom-call | flops 1000 | bytes 1000 | tf_op jit(solution)/shard_map/pallas_call | solution.py:335
  47.0 0.1 collective-permute-start.9
  47.1 0.0 collective-permute-done.10.refs_2_
  47.1 0.0 collective-permute-done.12.refs_5_
  47.1 1.5 %collective-permute-start.8 = (bf16[2,128,384]{2,1,0:T(8,128)(2,1)S(1)}, bf16[2,128,384]{2,1,0:T(8,128)(2,1)S(1)}, u32[]{:S(2)}, u32[]{:S(2)}) collective-permute-start(bf16[2,128,384]{2,1,0:T(8,128)(2,1)S(1)} %get-tuple-element.61), channel_id=1, source_target_pairs={{0,2},{1,3},{2,0},{3,1},{4,6},{5,7},{6,4},{7,5},{8,10},{9,11},{10,... | collective-permute-start | bytes 589832 | tf_op jit(solution)/shard_map/ppermute | solution.py:435
  48.6 2.4 %shard_map.64 = (bf16[2,128,384]{2,1,0:T(8,128)(2,1)S(1)}, bf16[4,6,768,512]{3,2,1,0:T(8,128)(2,1)S(1)}) custom-call(s32[2]{0:T(128)S(1)} %pad_add_fusion.place_ref._, s32[4,3]{1,0:T(4,128)S(1)} %copy-done, bf16[4,2,96,128]{3,2,1,0:T(8,128)(2,1)S(1)} %get-tuple-element.52.refs_0_, ...), custom_call_target="tpu_custom_call", output_to_operand_aliasing={{1}: (8, {})} | custom-call | flops 1000 | bytes 1000 | tf_op jit(solution)/shard_map/pallas_call | solution.py:335
  51.0 0.0 collective-permute-done.11.refs_6_
  51.0 0.0 collective-permute-done.9.refs_1_
  51.0 1.8 %shard_map.65 = (bf16[2,128,384]{2,1,0:T(8,128)(2,1)S(1)}, bf16[4,6,768,512]{3,2,1,0:T(8,128)(2,1)S(1)}) custom-call(s32[2]{0:T(128)S(1)} %pad_add_fusion.place_ref._, s32[4,3]{1,0:T(4,128)S(1)} %copy-done, bf16[4,2,96,128]{3,2,1,0:T(8,128)(2,1)S(1)} %get-tuple-element.52.refs_0_, ...), custom_call_target="tpu_custom_call", output_to_operand_aliasing={{1}: (8, {})} | custom-call | flops 1000 | bytes 1000 | tf_op jit(solution)/shard_map/pallas_call | solution.py:335
  52.8 0.2 collective-permute-start.13
  53.0 0.4 collective-permute-start.14
  53.4 0.5 collective-permute-start.17
  53.9 0.0 collective-permute-start.16
  53.9 0.6 collective-permute-done.8.refs_2_
  54.5 0.0 collective-permute-done.13.refs_3_
  54.5 0.1 collective-permute-done.14.refs_7_
  54.6 2.1 %shard_map.66.refs_8_ = f32[128,16,384]{2,1,0:T(8,128)} custom-call(s32[2]{0:T(128)S(1)} %pad_add_fusion.place_ref._, bf16[2,128,384]{2,1,0:T(8,128)(2,1)S(1)} %get-tuple-element.57.refs_0_, bf16[2,128,384]{2,1,0:T(8,128)(2,1)S(1)} %collective-permute-done.7.refs_1_, bf16[2,128,384]{2,1,0:T(8,128)(2,1)S(1)} %collective-permute-done.10.refs_2_, ...), custom_call_target="tpu_custom_call" | custom-call | flops 1000 | bytes 1000 | tf_op jit(solution)/shard_map/pallas_call | solution.py:388
  56.7 3.6 %collective-permute-done.17.refs_6_ = bf16[2,128,384]{2,1,0:T(8,128)(2,1)S(1)} collective-permute-done((bf16[2,128,384]{2,1,0:T(8,128)(2,1)S(1)}, bf16[2,128,384]{2,1,0:T(8,128)(2,1)S(1)}, u32[]{:S(2)}, u32[]{:S(2)}) %collective-permute-start.17) | collective-permute-done | bytes 196640 | tf_op jit(solution)/shard_map/ppermute | solution.py:435
  60.3 0.0 collective-permute-start.15
  60.3 0.5 collective-permute-start.18
  60.8 0.0 collective-permute-done.16.refs_5_
  60.8 0.9 %collective-permute-done.15.refs_3_ = bf16[2,128,384]{2,1,0:T(8,128)(2,1)S(1)} collective-permute-done((bf16[2,128,384]{2,1,0:T(8,128)(2,1)S(1)}, bf16[2,128,384]{2,1,0:T(8,128)(2,1)S(1)}, u32[]{:S(2)}, u32[]{:S(2)}) %collective-permute-start.15) | collective-permute-done | bytes 196640 | tf_op jit(solution)/shard_map/ppermute | solution.py:434
  61.8 0.3 collective-permute-done.18.refs_7_
  62.0 2.1 %shard_map.67 = f32[128,16,384]{2,1,0:T(8,128)} custom-call(s32[2]{0:T(128)S(1)} %pad_add_fusion.place_ref._, bf16[2,128,384]{2,1,0:T(8,128)(2,1)S(1)} %get-tuple-element.63.refs_0_, bf16[2,128,384]{2,1,0:T(8,128)(2,1)S(1)} %collective-permute-done.9.refs_1_, ...), custom_call_target="tpu_custom_call", output_to_operand_aliasing={{}: (9, {})} | custom-call | flops 1000 | bytes 1000 | tf_op jit(solution)/shard_map/pallas_call | solution.py:388
Async XLA Ops:
  0.0 5.1 %collective-permute-start = (bf16[64,2,16,384]{3,2,1,0:T(8,128)(2,1)}, bf16[64,2,16,384]{3,2,1,0:T(8,128)(2,1)S(1)}, u32[]{:S(2)}, u32[]{:S(2)}) collective-permute-start(bf16[64,2,16,384]{3,2,1,0:T(8,128)(2,1)} %own_ref.1), channel_id=1, source_target_pairs={{0,1},{1,0},{2,3},{3,2},{4,5},{5,4},{6,7},{7,6},{8,9},{9,8},{10,11... | collective-permute-start | bytes 4718600 | tf_op jit(solution)/shard_map/ppermute | solution.py:434
  9.8 12.7 %collective-permute-start.4 = (bf16[4,2,192,128]{3,2,1,0:T(8,128)(2,1)}, bf16[4,2,192,128]{3,2,1,0:T(8,128)(2,1)S(1)}, u32[]{:S(2)}, u32[]{:S(2)}) collective-permute-start(bf16[4,2,192,128]{3,2,1,0:T(8,128)(2,1)} %get-tuple-element.50), channel_id=1, source_target_pairs={{0,2},{1,3},{2,0},{3,1},{4,6},{5,7},{6,4},{7,5},{8,10},{9,11},{10,... | collective-permute-start | bytes 1179656 | tf_op jit(solution)/shard_map/ppermute | solution.py:435
  15.5 15.2 %collective-permute-start.1 = (bf16[4,2,192,128]{3,2,1,0:T(8,128)(2,1)}, bf16[4,2,192,128]{3,2,1,0:T(8,128)(2,1)S(1)}, u32[]{:S(2)}, u32[]{:S(2)}) collective-permute-start(bf16[4,2,192,128]{3,2,1,0:T(8,128)(2,1)} %get-tuple-element.46), channel_id=1, source_target_pairs={{0,2},{1,3},{2,0},{3,1},{4,6},{5,7},{6,4},{7,5},{8,10},{9,11},{10,... | collective-permute-start | bytes 1179656 | tf_op jit(solution)/shard_map/ppermute | solution.py:435
  15.6 13.8 %collective-permute-start.2 = (bf16[4,2,96,128]{3,2,1,0:T(8,128)(2,1)}, bf16[4,2,96,128]{3,2,1,0:T(8,128)(2,1)S(1)}, u32[]{:S(2)}, u32[]{:S(2)}) collective-permute-start(bf16[4,2,96,128]{3,2,1,0:T(8,128)(2,1)} %get-tuple-element.44), channel_id=1, source_target_pairs={{0,4},{4,0},{8,12},{12,8},{16,20},{20,16},{24,28},{28,24},{1,5},{5... | collective-permute-start | bytes 589832 | tf_op jit(solution)/shard_map/ppermute | solution.py:214
  17.7 11.7 %collective-permute-start.3 = (bf16[4,2,96,128]{3,2,1,0:T(8,128)(2,1)}, bf16[4,2,96,128]{3,2,1,0:T(8,128)(2,1)S(1)}, u32[]{:S(2)}, u32[]{:S(2)}) collective-permute-start(bf16[4,2,96,128]{3,2,1,0:T(8,128)(2,1)} %get-tuple-element.47), channel_id=1, source_target_pairs={{4,8},{8,4},{12,16},{16,12},{20,24},{24,20},{5,9},{9,5},{13,17},{1... | collective-permute-start | bytes 589832 | tf_op jit(solution)/shard_map/ppermute | solution.py:214
  24.1 10.6 %collective-permute-start.5 = (bf16[4,2,96,128]{3,2,1,0:T(8,128)(2,1)S(1)}, bf16[4,2,96,128]{3,2,1,0:T(8,128)(2,1)S(1)}, u32[]{:S(2)}, u32[]{:S(2)}) collective-permute-start(bf16[4,2,96,128]{3,2,1,0:T(8,128)(2,1)S(1)} %get-tuple-element.54), channel_id=1, source_target_pairs={{0,4},{4,0},{8,12},{12,8},{16,20},{20,16},{24,28},{28,24},{1,5},{5... | collective-permute-start | bytes 589832 | tf_op jit(solution)/shard_map/ppermute | solution.py:214
  26.2 8.6 %collective-permute-start.6 = (bf16[4,2,96,128]{3,2,1,0:T(8,128)(2,1)S(1)}, bf16[4,2,96,128]{3,2,1,0:T(8,128)(2,1)S(1)}, u32[]{:S(2)}, u32[]{:S(2)}) collective-permute-start(bf16[4,2,96,128]{3,2,1,0:T(8,128)(2,1)S(1)} %get-tuple-element.55), channel_id=1, source_target_pairs={{4,8},{8,4},{12,16},{16,12},{20,24},{24,20},{5,9},{9,5},{13,17},{1... | collective-permute-start | bytes 589832 | tf_op jit(solution)/shard_map/ppermute | solution.py:214
  27.0 7.8 %copy-start = (s32[4,3]{1,0:T(4,128)S(1)}, s32[4,3]{1,0:T(4,128)}, u32[]{:S(2)}) copy-start(s32[4,3]{1,0:T(4,128)} %columns_ref.9) | copy-start | bytes 148
  38.0 5.7 %collective-permute-start.7 = (bf16[2,128,384]{2,1,0:T(8,128)(2,1)S(1)}, bf16[2,128,384]{2,1,0:T(8,128)(2,1)S(1)}, u32[]{:S(2)}, u32[]{:S(2)}) collective-permute-start(bf16[2,128,384]{2,1,0:T(8,128)(2,1)S(1)} %get-tuple-element.57.refs_0_), channel_id=1, source_target_pairs={{0,1},{1,0},{2,3},{3,2},{4,5},{5,4},{6,7},{7,6},{8,9},{9,8},{10,11... | collective-permute-start | bytes 589832 | tf_op jit(solution)/shard_map/ppermute | solution.py:434
  38.1 9.0 %collective-permute-start.10 = (bf16[2,128,384]{2,1,0:T(8,128)(2,1)S(1)}, bf16[2,128,384]{2,1,0:T(8,128)(2,1)S(1)}, u32[]{:S(2)}, u32[]{:S(2)}) collective-permute-start(bf16[2,128,384]{2,1,0:T(8,128)(2,1)S(1)} %get-tuple-element.64), channel_id=1, source_target_pairs={{0,2},{1,3},{2,0},{3,1},{4,6},{5,7},{6,4},{7,5},{8,10},{9,11},{10,... | collective-permute-start | bytes 589832 | tf_op jit(solution)/shard_map/ppermute | solution.py:435
  42.9 4.2 %collective-permute-start.12 = (bf16[2,128,384]{2,1,0:T(8,128)(2,1)S(1)}, bf16[2,128,384]{2,1,0:T(8,128)(2,1)S(1)}, u32[]{:S(2)}, u32[]{:S(2)}) collective-permute-start(bf16[2,128,384]{2,1,0:T(8,128)(2,1)S(1)} %get-tuple-element.67.refs_4_), channel_id=1, source_target_pairs={{0,1},{1,0},{2,3},{3,2},{4,5},{5,4},{6,7},{7,6},{8,9},{9,8},{10,11... | collective-permute-start | bytes 589832 | tf_op jit(solution)/shard_map/ppermute | solution.py:434
  43.2 7.8 %collective-permute-start.11 = (bf16[2,128,384]{2,1,0:T(8,128)(2,1)S(1)}, bf16[2,128,384]{2,1,0:T(8,128)(2,1)S(1)}, u32[]{:S(2)}, u32[]{:S(2)}) collective-permute-start(bf16[2,128,384]{2,1,0:T(8,128)(2,1)S(1)} %get-tuple-element.65), channel_id=1, source_target_pairs={{0,2},{1,3},{2,0},{3,1},{4,6},{5,7},{6,4},{7,5},{8,10},{9,11},{10,... | collective-permute-start | bytes 589832 | tf_op jit(solution)/shard_map/ppermute | solution.py:435
  47.0 4.1 %collective-permute-start.9 = (bf16[2,128,384]{2,1,0:T(8,128)(2,1)S(1)}, bf16[2,128,384]{2,1,0:T(8,128)(2,1)S(1)}, u32[]{:S(2)}, u32[]{:S(2)}) collective-permute-start(bf16[2,128,384]{2,1,0:T(8,128)(2,1)S(1)} %get-tuple-element.63.refs_0_), channel_id=1, source_target_pairs={{0,1},{1,0},{2,3},{3,2},{4,5},{5,4},{6,7},{7,6},{8,9},{9,8},{10,11... | collective-permute-start | bytes 589832 | tf_op jit(solution)/shard_map/ppermute | solution.py:434
  47.1 7.4 %collective-permute-start.8 = (bf16[2,128,384]{2,1,0:T(8,128)(2,1)S(1)}, bf16[2,128,384]{2,1,0:T(8,128)(2,1)S(1)}, u32[]{:S(2)}, u32[]{:S(2)}) collective-permute-start(bf16[2,128,384]{2,1,0:T(8,128)(2,1)S(1)} %get-tuple-element.61), channel_id=1, source_target_pairs={{0,2},{1,3},{2,0},{3,1},{4,6},{5,7},{6,4},{7,5},{8,10},{9,11},{10,... | collective-permute-start | bytes 589832 | tf_op jit(solution)/shard_map/ppermute | solution.py:435
  52.8 1.7 %collective-permute-start.13 = (bf16[2,128,384]{2,1,0:T(8,128)(2,1)S(1)}, bf16[2,128,384]{2,1,0:T(8,128)(2,1)S(1)}, u32[]{:S(2)}, u32[]{:S(2)}) collective-permute-start(bf16[2,128,384]{2,1,0:T(8,128)(2,1)S(1)} %collective-permute-done.10.refs_2_), channel_id=1, source_target_pairs={{0,1},{1,0},{2,3},{3,2},{4,5},{5,4},{6,7},{7,6},{8,9},{9,8},{10,11... | collective-permute-start | bytes 589832 | tf_op jit(solution)/shard_map/ppermute | solution.py:434
  53.0 1.6 %collective-permute-start.14 = (bf16[2,128,384]{2,1,0:T(8,128)(2,1)S(1)}, bf16[2,128,384]{2,1,0:T(8,128)(2,1)S(1)}, u32[]{:S(2)}, u32[]{:S(2)}) collective-permute-start(bf16[2,128,384]{2,1,0:T(8,128)(2,1)S(1)} %collective-permute-done.11.refs_6_), channel_id=1, source_target_pairs={{0,1},{1,0},{2,3},{3,2},{4,5},{5,4},{6,7},{7,6},{8,9},{9,8},{10,11... | collective-permute-start | bytes 589832 | tf_op jit(solution)/shard_map/ppermute | solution.py:434
  53.4 7.0 %collective-permute-start.17 = (bf16[2,128,384]{2,1,0:T(8,128)(2,1)S(1)}, bf16[2,128,384]{2,1,0:T(8,128)(2,1)S(1)}, u32[]{:S(2)}, u32[]{:S(2)}) collective-permute-start(bf16[2,128,384]{2,1,0:T(8,128)(2,1)S(1)} %get-tuple-element.75), channel_id=1, source_target_pairs={{0,2},{1,3},{2,0},{3,1},{4,6},{5,7},{6,4},{7,5},{8,10},{9,11},{10,... | collective-permute-start | bytes 589832 | tf_op jit(solution)/shard_map/ppermute | solution.py:435
  53.9 6.9 %collective-permute-start.16 = (bf16[2,128,384]{2,1,0:T(8,128)(2,1)S(1)}, bf16[2,128,384]{2,1,0:T(8,128)(2,1)S(1)}, u32[]{:S(2)}, u32[]{:S(2)}) collective-permute-start(bf16[2,128,384]{2,1,0:T(8,128)(2,1)S(1)} %get-tuple-element.71.refs_4_), channel_id=1, source_target_pairs={{0,1},{1,0},{2,3},{3,2},{4,5},{5,4},{6,7},{7,6},{8,9},{9,8},{10,11... | collective-permute-start | bytes 589832 | tf_op jit(solution)/shard_map/ppermute | solution.py:434
  60.3 1.4 %collective-permute-start.15 = (bf16[2,128,384]{2,1,0:T(8,128)(2,1)S(1)}, bf16[2,128,384]{2,1,0:T(8,128)(2,1)S(1)}, u32[]{:S(2)}, u32[]{:S(2)}) collective-permute-start(bf16[2,128,384]{2,1,0:T(8,128)(2,1)S(1)} %collective-permute-done.8.refs_2_), channel_id=1, source_target_pairs={{0,1},{1,0},{2,3},{3,2},{4,5},{5,4},{6,7},{7,6},{8,9},{9,8},{10,11... | collective-permute-start | bytes 589832 | tf_op jit(solution)/shard_map/ppermute | solution.py:434
  60.3 1.7 %collective-permute-start.18 = (bf16[2,128,384]{2,1,0:T(8,128)(2,1)S(1)}, bf16[2,128,384]{2,1,0:T(8,128)(2,1)S(1)}, u32[]{:S(2)}, u32[]{:S(2)}) collective-permute-start(bf16[2,128,384]{2,1,0:T(8,128)(2,1)S(1)} %collective-permute-done.17.refs_6_), channel_id=1, source_target_pairs={{0,1},{1,0},{2,3},{3,2},{4,5},{5,4},{6,7},{7,6},{8,9},{9,8},{10,11... | collective-permute-start | bytes 589832 | tf_op jit(solution)/shard_map/ppermute | solution.py:434

commit v3 on v2

--- a/solution.py
+++ b/solution.py
@@ -434,14 +434,14 @@
     near = lambda v: lax.ppermute(v, "chaos", [(i, i ^ 1) for i in range(4)])
     across = lambda v: lax.ppermute(v, "chaos", [(i, i ^ 2) for i in range(4)])
     near_loads = near(load_vectors)
-    coupling = dense_coupling(place, chaos_index, chaos_value)
-    place = after(place, coupling)
+    tiles = wide_tiles(place, stiff_tiles)
+    place = after(place, tiles)
     send_outer, send_inner, outer, inner, even, odd = pack(place, load_vectors, near_loads)
     far_outer = across(send_outer)
     own_edges = swap(even, odd)
-    tiles = wide_tiles(after(place, even), stiff_tiles)
-    far_inner = across(after(send_inner, tiles))
-    field, even, odd = gather_outer(after(place, tiles), outer, far_outer)
+    coupling = dense_coupling(after(place, even), chaos_index, chaos_value)
+    far_inner = across(after(send_inner, coupling))
+    field, even, odd = gather_outer(after(place, coupling, *own_edges), outer, far_outer)
     far_edges = swap(even, odd)
     mixed = mix_outer(field, coupling, blocks)
     mixed, *own_edges = mix_inner(inner, far_inner, own_edges, coupling, mixed)

time: 64.6 us -> 63.3 us (0.980)
  waiting for transfers between devices: 11.6 us -> 9.24 us
  starting transfers between devices: 14.3 us -> 15.1 us
    ppermute x6, waiting for transfers between devices: 9.75 us -> 4.71 us  [body(): across = lambda v: lax.ppermute(v, 'chaos', [(i, i ^ 2) for i in range(4)])]
    ppermute x2, waiting for transfers between devices: 0.6 us -> 3.27 us  [swap(): lax.ppermute(even, 'space', even_pairs)]
    ppermute x6, starting transfers between devices: 6.77 us -> 7.64 us  [body(): across = lambda v: lax.ppermute(v, 'chaos', [(i, i ^ 2) for i in range(4)])]
  transfers between devices with their start and end apart: 19 -> 19, of which waited for: 8 -> 7; matrix products, arithmetic and copies ran while one was open for 0% -> 0% of each run, Pallas kernels for 43% -> 45%
where the time goes in v3:
time: 63.3 us; the launch traced here: 62.6 us
  Pallas kernels  37.9 us (60%)
  starting transfers between devices  15.1 us (24%)
  waiting for transfers between devices  9.24 us (15%)
    pallas_call x5, Pallas kernels, apply_tiles(): pl.pallas_call(functools.partial(tiles_apply_kernel, m, quarters), in_spe...  13.8 us
    ppermute x6, starting transfers between devices, body(): across = lambda v: lax.ppermute(v, 'chaos', [(i, i ^ 2) for i in range(4)])  7.64 us
    ppermute x6, waiting for transfers between devices, body(): across = lambda v: lax.ppermute(v, 'chaos', [(i, i ^ 2) for i in range(4)])  4.71 us
    pallas_call x1, Pallas kernels, pack(): pl.pallas_call(pack_kernel, in_specs=[SMEM, ANY, ANY], out_specs=[HBM] *...  4.62 us
    pallas_call x1, Pallas kernels, dense_coupling(): pl.pallas_call(coupling_kernel, in_specs=[SMEM, ANY, ANY], out_specs=VMEM...  4.59 us
    pallas_call x2, Pallas kernels, unpack(): pl.pallas_call(kernel, in_specs=specs, out_specs=ANY, scratch_shapes=[plt...  4.26 us
    ppermute x2, starting transfers between devices, swap(): lax.ppermute(even, 'space', even_pairs)  3.96 us
    pallas_call x1, Pallas kernels, mix_inner(): pl.pallas_call(mix_inner_kernel, in_specs=[ANY] * (2 + count) + [VMEM] *...  3.46 us
  transfers between devices with their start and end apart: 19, of which 7 were waited for; matrix products, arithmetic and copies ran while one was open for 0% of the time, Pallas kernels for 45%

profile of v3, /device:TPU:0, one launch (start us, length us, event | category | flops | bytes accessed | tf_op | source)
XLA Modules:
  0.0 62.6 jit_solution(17099814125847082714)
XLA Ops:
  0.0 0.5 collective-permute-start
  0.5 0.1 pad_add_fusion._.place_ref
  0.5 3.2 %shard_map.55.refs_5_ = bf16[4,3,192,768]{3,2,1,0:T(8,128)(2,1)S(1)} custom-call(s32[2]{0:T(128)S(1)} %pad_add_fusion._.place_ref, bf16[4,3,8,2,96,96]{5,4,3,2,1,0:T(8,128)(2,1)} %tiles_hbm_ref.1), custom_call_target="tpu_custom_call" | custom-call | flops 1000 | bytes 1000 | tf_op jit(solution)/shard_map/pallas_call | solution.py:100
  3.7 0.0 collective-permute-done.near_ref
  3.8 4.6 %shard_map.56 = (bf16[4,2,192,128]{3,2,1,0:T(8,128)(2,1)}, bf16[4,2,192,128]{3,2,1,0:T(8,128)(2,1)}, bf16[4,2,192,128]{3,2,1,0:T(8,128)(2,1)}, bf16[4,2,192,128]...) custom-call(s32[2]{0:T(128)S(1)} %pad_add_fusion._.place_ref, ...), custom_call_target="tpu_custom_call" | custom-call | flops 1000 | bytes 1000 | tf_op jit(solution)/shard_map/pallas_call | solution.py:162
  8.4 2.9 %collective-permute-start.4 = (bf16[4,2,192,128]{3,2,1,0:T(8,128)(2,1)}, bf16[4,2,192,128]{3,2,1,0:T(8,128)(2,1)S(1)}, u32[]{:S(2)}, u32[]{:S(2)}) collective-permute-start(bf16[4,2,192,128]{3,2,1,0:T(8,128)(2,1)} %get-tuple-element.50), channel_id=1, source_target_pairs={{0,2},{1,3},{2,0},{3,1},{4,6},{5,7},{6,4},{7,5},{8,10},{9,11},{10,... | collective-permute-start | bytes 1179656 | tf_op jit(solution)/shard_map/ppermute | solution.py:435
  11.3 1.5 %collective-permute-start.2 = (bf16[4,2,96,128]{3,2,1,0:T(8,128)(2,1)}, bf16[4,2,96,128]{3,2,1,0:T(8,128)(2,1)S(1)}, u32[]{:S(2)}, u32[]{:S(2)}) collective-permute-start(bf16[4,2,96,128]{3,2,1,0:T(8,128)(2,1)} %get-tuple-element.44), channel_id=1, source_target_pairs={{0,4},{4,0},{8,12},{12,8},{16,20},{20,16},{24,28},{28,24},{1,5},{5... | collective-permute-start | bytes 589832 | tf_op jit(solution)/shard_map/ppermute | solution.py:214
  12.8 0.7 %collective-permute-start.3 = (bf16[4,2,96,128]{3,2,1,0:T(8,128)(2,1)}, bf16[4,2,96,128]{3,2,1,0:T(8,128)(2,1)S(1)}, u32[]{:S(2)}, u32[]{:S(2)}) collective-permute-start(bf16[4,2,96,128]{3,2,1,0:T(8,128)(2,1)} %get-tuple-element.47), channel_id=1, source_target_pairs={{4,8},{8,4},{12,16},{16,12},{20,24},{24,20},{5,9},{9,5},{13,17},{1... | collective-permute-start | bytes 589832 | tf_op jit(solution)/shard_map/ppermute | solution.py:214
  13.4 4.6 %shard_map.57.coupling_ref.refs_2_.refs_4_ = bf16[8,256,256]{2,1,0:T(8,128)(2,1)S(1)} custom-call(s32[2]{0:T(128)S(1)} %pad_add_fusion._.place_ref, s32[8,32,256]{2,1,0:T(8,128)} %bitcast.5, bf16[8,32,256]{2,1,0:T(8,128)(2,1)} %bitcast.6), custom_call_target="tpu_custom_call" | custom-call | flops 1000 | bytes 1000 | tf_op jit(solution)/shard_map/pallas_call | solution.py:69
  18.0 0.6 collective-permute-start.1
  18.6 0.0 collective-permute-done.3.refs_1_
  18.6 2.9 %collective-permute-done.2.refs_0_ = bf16[4,2,96,128]{3,2,1,0:T(8,128)(2,1)S(1)} collective-permute-done((bf16[4,2,96,128]{3,2,1,0:T(8,128)(2,1)}, bf16[4,2,96,128]{3,2,1,0:T(8,128)(2,1)S(1)}, u32[]{:S(2)}, u32[]{:S(2)}) %collective-permute-start.2) | collective-permute-done | bytes 196640 | tf_op jit(solution)/shard_map/ppermute | solution.py:214
  21.5 0.0 collective-permute-done.4.far_ref
  21.5 1.6 %shard_map.58 = (bf16[4,2,192,256]{3,2,1,0:T(8,128)(2,1)S(1)}, bf16[4,2,96,128]{3,2,1,0:T(8,128)(2,1)S(1)}, bf16[4,2,96,128]{3,2,1,0:T(8,128)(2,1)S(1)}) custom-call(s32[2]{0:T(128)S(1)} %pad_add_fusion._.place_ref, bf16[4,2,192,128]{3,2,1,0:T(8,128)(2,1)} %get-tuple-element.49.own_ref, bf16[4,2,192,128]{3,2,1,0:T(8,128)(2,1)S(1)} %collective-permute-done.4.far_ref), custom_call_target="tpu_custom_call" | custom-call | flops 1000 | bytes 1000 | tf_op jit(solution)/shard_map/pallas_call | solution.py:199
  23.2 2.4 %collective-permute-start.5 = (bf16[4,2,96,128]{3,2,1,0:T(8,128)(2,1)S(1)}, bf16[4,2,96,128]{3,2,1,0:T(8,128)(2,1)S(1)}, u32[]{:S(2)}, u32[]{:S(2)}) collective-permute-start(bf16[4,2,96,128]{3,2,1,0:T(8,128)(2,1)S(1)} %get-tuple-element.54), channel_id=1, source_target_pairs={{0,4},{4,0},{8,12},{12,8},{16,20},{20,16},{24,28},{28,24},{1,5},{5... | collective-permute-start | bytes 589832 | tf_op jit(solution)/shard_map/ppermute | solution.py:214
  25.6 0.8 %collective-permute-start.6 = (bf16[4,2,96,128]{3,2,1,0:T(8,128)(2,1)S(1)}, bf16[4,2,96,128]{3,2,1,0:T(8,128)(2,1)S(1)}, u32[]{:S(2)}, u32[]{:S(2)}) collective-permute-start(bf16[4,2,96,128]{3,2,1,0:T(8,128)(2,1)S(1)} %get-tuple-element.55), channel_id=1, source_target_pairs={{4,8},{8,4},{12,16},{16,12},{20,24},{24,20},{5,9},{9,5},{13,17},{1... | collective-permute-start | bytes 589832 | tf_op jit(solution)/shard_map/ppermute | solution.py:214
  26.5 0.0 copy-start
  26.5 2.3 %shard_map.59.refs_3_ = bf16[4,6,768,512]{3,2,1,0:T(8,128)(2,1)S(1)} custom-call(bf16[4,2,192,256]{3,2,1,0:T(8,128)(2,1)S(1)} %get-tuple-element.51.field_ref, bf16[8,256,256]{2,1,0:T(8,128)(2,1)S(1)} %shard_map.57.coupling_ref.refs_2_.refs_4_), custom_call_target="tpu_custom_call" | custom-call | flops 1000 | bytes 1000 | tf_op jit(solution)/shard_map/pallas_call | solution.py:238
  28.8 0.6 collective-permute-done.1.far_ref
  29.4 3.5 %shard_map.60 = (bf16[4,6,768,512]{3,2,1,0:T(8,128)(2,1)S(1)}, bf16[4,2,96,128]{3,2,1,0:T(8,128)(2,1)S(1)}, bf16[4,2,96,128]{3,2,1,0:T(8,128)(2,1)S(1)}) custom-call(bf16[4,2,192,128]{3,2,1,0:T(8,128)(2,1)} %get-tuple-element.42.own_ref, bf16[4,2,192,128]{3,2,1,0:T(8,128)(2,1)S(1)} %collective-permute-done.1.far_ref, ...), custom_call_target="tpu_custom_call", output_to_operand_aliasing={{0}: (5, {})} | custom-call | flops 1000 | bytes 1000 | tf_op jit(solution)/shard_map/pallas_call | solution.py:276
  32.8 0.4 collective-permute-done.5.refs_2_
  33.2 0.0 collective-permute-done.6.refs_3_
  33.2 0.0 copy-done
  33.2 3.2 %shard_map.61 = (bf16[2,128,384]{2,1,0:T(8,128)(2,1)S(1)}, bf16[2,128,384]{2,1,0:T(8,128)(2,1)S(1)}, bf16[4,6,768,512]{3,2,1,0:T(8,128)(2,1)S(1)}) custom-call(s32[2]{0:T(128)S(1)} %pad_add_fusion._.place_ref, s32[4,3]{1,0:T(4,128)S(1)} %copy-done, bf16[4,2,96,128]{3,2,1,0:T(8,128)(2,1)S(1)} %get-tuple-element.52.refs_0_, ...), custom_call_target="tpu_custom_call", output_to_operand_aliasing={{2}: (8, {})} | custom-call | flops 1000 | bytes 1000 | tf_op jit(solution)/shard_map/pallas_call | solution.py:335
  36.5 0.1 collective-permute-start.7
  36.5 1.5 %collective-permute-start.10 = (bf16[2,128,384]{2,1,0:T(8,128)(2,1)S(1)}, bf16[2,128,384]{2,1,0:T(8,128)(2,1)S(1)}, u32[]{:S(2)}, u32[]{:S(2)}) collective-permute-start(bf16[2,128,384]{2,1,0:T(8,128)(2,1)S(1)} %get-tuple-element.64), channel_id=1, source_target_pairs={{0,2},{1,3},{2,0},{3,1},{4,6},{5,7},{6,4},{7,5},{8,10},{9,11},{10,... | collective-permute-start | bytes 589832 | tf_op jit(solution)/shard_map/ppermute | solution.py:435
  38.0 3.2 %shard_map.62 = (bf16[2,128,384]{2,1,0:T(8,128)(2,1)S(1)}, bf16[2,128,384]{2,1,0:T(8,128)(2,1)S(1)}, bf16[4,6,768,512]{3,2,1,0:T(8,128)(2,1)S(1)}) custom-call(s32[2]{0:T(128)S(1)} %pad_add_fusion._.place_ref, s32[4,3]{1,0:T(4,128)S(1)} %copy-done, bf16[4,2,96,128]{3,2,1,0:T(8,128)(2,1)S(1)} %get-tuple-element.52.refs_0_, ...), custom_call_target="tpu_custom_call", output_to_operand_aliasing={{2}: (8, {})} | custom-call | flops 1000 | bytes 1000 | tf_op jit(solution)/shard_map/pallas_call | solution.py:335
  41.2 0.2 collective-permute-start.12
  41.5 0.6 %collective-permute-start.11 = (bf16[2,128,384]{2,1,0:T(8,128)(2,1)S(1)}, bf16[2,128,384]{2,1,0:T(8,128)(2,1)S(1)}, u32[]{:S(2)}, u32[]{:S(2)}) collective-permute-start(bf16[2,128,384]{2,1,0:T(8,128)(2,1)S(1)} %get-tuple-element.65), channel_id=1, source_target_pairs={{0,2},{1,3},{2,0},{3,1},{4,6},{5,7},{6,4},{7,5},{8,10},{9,11},{10,... | collective-permute-start | bytes 589832 | tf_op jit(solution)/shard_map/ppermute | solution.py:435
  42.1 0.0 collective-permute-done.7.refs_1_
  42.1 3.2 %shard_map.63 = (bf16[2,128,384]{2,1,0:T(8,128)(2,1)S(1)}, bf16[2,128,384]{2,1,0:T(8,128)(2,1)S(1)}, bf16[4,6,768,512]{3,2,1,0:T(8,128)(2,1)S(1)}) custom-call(s32[2]{0:T(128)S(1)} %pad_add_fusion._.place_ref, s32[4,3]{1,0:T(4,128)S(1)} %copy-done, bf16[4,2,96,128]{3,2,1,0:T(8,128)(2,1)S(1)} %get-tuple-element.52.refs_0_, ...), custom_call_target="tpu_custom_call", output_to_operand_aliasing={{2}: (8, {})} | custom-call | flops 1000 | bytes 1000 | tf_op jit(solution)/shard_map/pallas_call | solution.py:335
  45.4 0.1 collective-permute-start.9
  45.5 0.0 collective-permute-done.10.refs_2_
  45.5 0.0 collective-permute-done.12.refs_5_
  45.5 1.4 %collective-permute-start.8 = (bf16[2,128,384]{2,1,0:T(8,128)(2,1)S(1)}, bf16[2,128,384]{2,1,0:T(8,128)(2,1)S(1)}, u32[]{:S(2)}, u32[]{:S(2)}) collective-permute-start(bf16[2,128,384]{2,1,0:T(8,128)(2,1)S(1)} %get-tuple-element.61), channel_id=1, source_target_pairs={{0,2},{1,3},{2,0},{3,1},{4,6},{5,7},{6,4},{7,5},{8,10},{9,11},{10,... | collective-permute-start | bytes 589832 | tf_op jit(solution)/shard_map/ppermute | solution.py:435
  46.9 2.4 %shard_map.64 = (bf16[2,128,384]{2,1,0:T(8,128)(2,1)S(1)}, bf16[4,6,768,512]{3,2,1,0:T(8,128)(2,1)S(1)}) custom-call(s32[2]{0:T(128)S(1)} %pad_add_fusion._.place_ref, s32[4,3]{1,0:T(4,128)S(1)} %copy-done, bf16[4,2,96,128]{3,2,1,0:T(8,128)(2,1)S(1)} %get-tuple-element.52.refs_0_, ...), custom_call_target="tpu_custom_call", output_to_operand_aliasing={{1}: (8, {})} | custom-call | flops 1000 | bytes 1000 | tf_op jit(solution)/shard_map/pallas_call | solution.py:335
  49.3 0.0 collective-permute-done.11.refs_6_
  49.3 0.0 collective-permute-done.9.refs_1_
  49.3 1.8 %shard_map.65 = (bf16[2,128,384]{2,1,0:T(8,128)(2,1)S(1)}, bf16[4,6,768,512]{3,2,1,0:T(8,128)(2,1)S(1)}) custom-call(s32[2]{0:T(128)S(1)} %pad_add_fusion._.place_ref, s32[4,3]{1,0:T(4,128)S(1)} %copy-done, bf16[4,2,96,128]{3,2,1,0:T(8,128)(2,1)S(1)} %get-tuple-element.52.refs_0_, ...), custom_call_target="tpu_custom_call", output_to_operand_aliasing={{1}: (8, {})} | custom-call | flops 1000 | bytes 1000 | tf_op jit(solution)/shard_map/pallas_call | solution.py:335
  51.1 0.2 collective-permute-start.13
  51.3 0.4 collective-permute-start.14
  51.7 0.6 %collective-permute-start.17 = (bf16[2,128,384]{2,1,0:T(8,128)(2,1)S(1)}, bf16[2,128,384]{2,1,0:T(8,128)(2,1)S(1)}, u32[]{:S(2)}, u32[]{:S(2)}) collective-permute-start(bf16[2,128,384]{2,1,0:T(8,128)(2,1)S(1)} %get-tuple-element.75), channel_id=1, source_target_pairs={{0,2},{1,3},{2,0},{3,1},{4,6},{5,7},{6,4},{7,5},{8,10},{9,11},{10,... | collective-permute-start | bytes 589832 | tf_op jit(solution)/shard_map/ppermute | solution.py:435
  52.3 0.0 collective-permute-start.16
  52.3 0.5 collective-permute-done.8.refs_2_
  52.8 0.0 collective-permute-done.13.refs_3_
  52.8 0.0 collective-permute-done.14.refs_7_
  52.9 2.1 %shard_map.66.refs_8_ = f32[128,16,384]{2,1,0:T(8,128)} custom-call(s32[2]{0:T(128)S(1)} %pad_add_fusion._.place_ref, bf16[2,128,384]{2,1,0:T(8,128)(2,1)S(1)} %get-tuple-element.57.refs_0_, bf16[2,128,384]{2,1,0:T(8,128)(2,1)S(1)} %collective-permute-done.7.refs_1_, bf16[2,128,384]{2,1,0:T(8,128)(2,1)S(1)} %collective-permute-done.10.refs_2_, ...), custom_call_target="tpu_custom_call" | custom-call | flops 1000 | bytes 1000 | tf_op jit(solution)/shard_map/pallas_call | solution.py:388
  55.0 3.6 %collective-permute-done.17.refs_6_ = bf16[2,128,384]{2,1,0:T(8,128)(2,1)S(1)} collective-permute-done((bf16[2,128,384]{2,1,0:T(8,128)(2,1)S(1)}, bf16[2,128,384]{2,1,0:T(8,128)(2,1)S(1)}, u32[]{:S(2)}, u32[]{:S(2)}) %collective-permute-start.17) | collective-permute-done | bytes 196640 | tf_op jit(solution)/shard_map/ppermute | solution.py:435
  58.6 0.0 collective-permute-start.15
  58.6 0.5 collective-permute-start.18
  59.1 0.0 collective-permute-done.16.refs_5_
  59.1 0.9 %collective-permute-done.15.refs_3_ = bf16[2,128,384]{2,1,0:T(8,128)(2,1)S(1)} collective-permute-done((bf16[2,128,384]{2,1,0:T(8,128)(2,1)S(1)}, bf16[2,128,384]{2,1,0:T(8,128)(2,1)S(1)}, u32[]{:S(2)}, u32[]{:S(2)}) %collective-permute-start.15) | collective-permute-done | bytes 196640 | tf_op jit(solution)/shard_map/ppermute | solution.py:434
  60.1 0.3 collective-permute-done.18.refs_7_
  60.3 2.1 %shard_map.67 = f32[128,16,384]{2,1,0:T(8,128)} custom-call(s32[2]{0:T(128)S(1)} %pad_add_fusion._.place_ref, bf16[2,128,384]{2,1,0:T(8,128)(2,1)S(1)} %get-tuple-element.63.refs_0_, bf16[2,128,384]{2,1,0:T(8,128)(2,1)S(1)} %collective-permute-done.9.refs_1_, ...), custom_call_target="tpu_custom_call", output_to_operand_aliasing={{}: (9, {})} | custom-call | flops 1000 | bytes 1000 | tf_op jit(solution)/shard_map/pallas_call | solution.py:388
Async XLA Ops:
  0.0 3.7 %collective-permute-start = (bf16[64,2,16,384]{3,2,1,0:T(8,128)(2,1)}, bf16[64,2,16,384]{3,2,1,0:T(8,128)(2,1)S(1)}, u32[]{:S(2)}, u32[]{:S(2)}) collective-permute-start(bf16[64,2,16,384]{3,2,1,0:T(8,128)(2,1)} %own_ref.1), channel_id=1, source_target_pairs={{0,1},{1,0},{2,3},{3,2},{4,5},{5,4},{6,7},{7,6},{8,9},{9,8},{10,11... | collective-permute-start | bytes 4718600 | tf_op jit(solution)/shard_map/ppermute | solution.py:434
  8.4 13.2 %collective-permute-start.4 = (bf16[4,2,192,128]{3,2,1,0:T(8,128)(2,1)}, bf16[4,2,192,128]{3,2,1,0:T(8,128)(2,1)S(1)}, u32[]{:S(2)}, u32[]{:S(2)}) collective-permute-start(bf16[4,2,192,128]{3,2,1,0:T(8,128)(2,1)} %get-tuple-element.50), channel_id=1, source_target_pairs={{0,2},{1,3},{2,0},{3,1},{4,6},{5,7},{6,4},{7,5},{8,10},{9,11},{10,... | collective-permute-start | bytes 1179656 | tf_op jit(solution)/shard_map/ppermute | solution.py:435
  11.3 10.3 %collective-permute-start.2 = (bf16[4,2,96,128]{3,2,1,0:T(8,128)(2,1)}, bf16[4,2,96,128]{3,2,1,0:T(8,128)(2,1)S(1)}, u32[]{:S(2)}, u32[]{:S(2)}) collective-permute-start(bf16[4,2,96,128]{3,2,1,0:T(8,128)(2,1)} %get-tuple-element.44), channel_id=1, source_target_pairs={{0,4},{4,0},{8,12},{12,8},{16,20},{20,16},{24,28},{28,24},{1,5},{5... | collective-permute-start | bytes 589832 | tf_op jit(solution)/shard_map/ppermute | solution.py:214
  12.8 5.9 %collective-permute-start.3 = (bf16[4,2,96,128]{3,2,1,0:T(8,128)(2,1)}, bf16[4,2,96,128]{3,2,1,0:T(8,128)(2,1)S(1)}, u32[]{:S(2)}, u32[]{:S(2)}) collective-permute-start(bf16[4,2,96,128]{3,2,1,0:T(8,128)(2,1)} %get-tuple-element.47), channel_id=1, source_target_pairs={{4,8},{8,4},{12,16},{16,12},{20,24},{24,20},{5,9},{9,5},{13,17},{1... | collective-permute-start | bytes 589832 | tf_op jit(solution)/shard_map/ppermute | solution.py:214
  18.0 11.3 %collective-permute-start.1 = (bf16[4,2,192,128]{3,2,1,0:T(8,128)(2,1)}, bf16[4,2,192,128]{3,2,1,0:T(8,128)(2,1)S(1)}, u32[]{:S(2)}, u32[]{:S(2)}) collective-permute-start(bf16[4,2,192,128]{3,2,1,0:T(8,128)(2,1)} %get-tuple-element.46), channel_id=1, source_target_pairs={{0,2},{1,3},{2,0},{3,1},{4,6},{5,7},{6,4},{7,5},{8,10},{9,11},{10,... | collective-permute-start | bytes 1179656 | tf_op jit(solution)/shard_map/ppermute | solution.py:435
  23.2 10.0 %collective-permute-start.5 = (bf16[4,2,96,128]{3,2,1,0:T(8,128)(2,1)S(1)}, bf16[4,2,96,128]{3,2,1,0:T(8,128)(2,1)S(1)}, u32[]{:S(2)}, u32[]{:S(2)}) collective-permute-start(bf16[4,2,96,128]{3,2,1,0:T(8,128)(2,1)S(1)} %get-tuple-element.54), channel_id=1, source_target_pairs={{0,4},{4,0},{8,12},{12,8},{16,20},{20,16},{24,28},{28,24},{1,5},{5... | collective-permute-start | bytes 589832 | tf_op jit(solution)/shard_map/ppermute | solution.py:214
  25.6 7.6 %collective-permute-start.6 = (bf16[4,2,96,128]{3,2,1,0:T(8,128)(2,1)S(1)}, bf16[4,2,96,128]{3,2,1,0:T(8,128)(2,1)S(1)}, u32[]{:S(2)}, u32[]{:S(2)}) collective-permute-start(bf16[4,2,96,128]{3,2,1,0:T(8,128)(2,1)S(1)} %get-tuple-element.55), channel_id=1, source_target_pairs={{4,8},{8,4},{12,16},{16,12},{20,24},{24,20},{5,9},{9,5},{13,17},{1... | collective-permute-start | bytes 589832 | tf_op jit(solution)/shard_map/ppermute | solution.py:214
  26.5 6.7 %copy-start = (s32[4,3]{1,0:T(4,128)S(1)}, s32[4,3]{1,0:T(4,128)}, u32[]{:S(2)}) copy-start(s32[4,3]{1,0:T(4,128)} %columns_ref.9) | copy-start | bytes 148
  36.5 5.7 %collective-permute-start.7 = (bf16[2,128,384]{2,1,0:T(8,128)(2,1)S(1)}, bf16[2,128,384]{2,1,0:T(8,128)(2,1)S(1)}, u32[]{:S(2)}, u32[]{:S(2)}) collective-permute-start(bf16[2,128,384]{2,1,0:T(8,128)(2,1)S(1)} %get-tuple-element.57.refs_0_), channel_id=1, source_target_pairs={{0,1},{1,0},{2,3},{3,2},{4,5},{5,4},{6,7},{7,6},{8,9},{9,8},{10,11... | collective-permute-start | bytes 589832 | tf_op jit(solution)/shard_map/ppermute | solution.py:434
  36.5 9.0 %collective-permute-start.10 = (bf16[2,128,384]{2,1,0:T(8,128)(2,1)S(1)}, bf16[2,128,384]{2,1,0:T(8,128)(2,1)S(1)}, u32[]{:S(2)}, u32[]{:S(2)}) collective-permute-start(bf16[2,128,384]{2,1,0:T(8,128)(2,1)S(1)} %get-tuple-element.64), channel_id=1, source_target_pairs={{0,2},{1,3},{2,0},{3,1},{4,6},{5,7},{6,4},{7,5},{8,10},{9,11},{10,... | collective-permute-start | bytes 589832 | tf_op jit(solution)/shard_map/ppermute | solution.py:435
  41.2 4.3 %collective-permute-start.12 = (bf16[2,128,384]{2,1,0:T(8,128)(2,1)S(1)}, bf16[2,128,384]{2,1,0:T(8,128)(2,1)S(1)}, u32[]{:S(2)}, u32[]{:S(2)}) collective-permute-start(bf16[2,128,384]{2,1,0:T(8,128)(2,1)S(1)} %get-tuple-element.67.refs_4_), channel_id=1, source_target_pairs={{0,1},{1,0},{2,3},{3,2},{4,5},{5,4},{6,7},{7,6},{8,9},{9,8},{10,11... | collective-permute-start | bytes 589832 | tf_op jit(solution)/shard_map/ppermute | solution.py:434
  41.5 7.8 %collective-permute-start.11 = (bf16[2,128,384]{2,1,0:T(8,128)(2,1)S(1)}, bf16[2,128,384]{2,1,0:T(8,128)(2,1)S(1)}, u32[]{:S(2)}, u32[]{:S(2)}) collective-permute-start(bf16[2,128,384]{2,1,0:T(8,128)(2,1)S(1)} %get-tuple-element.65), channel_id=1, source_target_pairs={{0,2},{1,3},{2,0},{3,1},{4,6},{5,7},{6,4},{7,5},{8,10},{9,11},{10,... | collective-permute-start | bytes 589832 | tf_op jit(solution)/shard_map/ppermute | solution.py:435
  45.4 3.9 %collective-permute-start.9 = (bf16[2,128,384]{2,1,0:T(8,128)(2,1)S(1)}, bf16[2,128,384]{2,1,0:T(8,128)(2,1)S(1)}, u32[]{:S(2)}, u32[]{:S(2)}) collective-permute-start(bf16[2,128,384]{2,1,0:T(8,128)(2,1)S(1)} %get-tuple-element.63.refs_0_), channel_id=1, source_target_pairs={{0,1},{1,0},{2,3},{3,2},{4,5},{5,4},{6,7},{7,6},{8,9},{9,8},{10,11... | collective-permute-start | bytes 589832 | tf_op jit(solution)/shard_map/ppermute | solution.py:434
  45.5 7.3 %collective-permute-start.8 = (bf16[2,128,384]{2,1,0:T(8,128)(2,1)S(1)}, bf16[2,128,384]{2,1,0:T(8,128)(2,1)S(1)}, u32[]{:S(2)}, u32[]{:S(2)}) collective-permute-start(bf16[2,128,384]{2,1,0:T(8,128)(2,1)S(1)} %get-tuple-element.61), channel_id=1, source_target_pairs={{0,2},{1,3},{2,0},{3,1},{4,6},{5,7},{6,4},{7,5},{8,10},{9,11},{10,... | collective-permute-start | bytes 589832 | tf_op jit(solution)/shard_map/ppermute | solution.py:435
  51.1 1.8 %collective-permute-start.13 = (bf16[2,128,384]{2,1,0:T(8,128)(2,1)S(1)}, bf16[2,128,384]{2,1,0:T(8,128)(2,1)S(1)}, u32[]{:S(2)}, u32[]{:S(2)}) collective-permute-start(bf16[2,128,384]{2,1,0:T(8,128)(2,1)S(1)} %collective-permute-done.10.refs_2_), channel_id=1, source_target_pairs={{0,1},{1,0},{2,3},{3,2},{4,5},{5,4},{6,7},{7,6},{8,9},{9,8},{10,11... | collective-permute-start | bytes 589832 | tf_op jit(solution)/shard_map/ppermute | solution.py:434
  51.3 1.6 %collective-permute-start.14 = (bf16[2,128,384]{2,1,0:T(8,128)(2,1)S(1)}, bf16[2,128,384]{2,1,0:T(8,128)(2,1)S(1)}, u32[]{:S(2)}, u32[]{:S(2)}) collective-permute-start(bf16[2,128,384]{2,1,0:T(8,128)(2,1)S(1)} %collective-permute-done.11.refs_6_), channel_id=1, source_target_pairs={{0,1},{1,0},{2,3},{3,2},{4,5},{5,4},{6,7},{7,6},{8,9},{9,8},{10,11... | collective-permute-start | bytes 589832 | tf_op jit(solution)/shard_map/ppermute | solution.py:434
  51.7 7.0 %collective-permute-start.17 = (bf16[2,128,384]{2,1,0:T(8,128)(2,1)S(1)}, bf16[2,128,384]{2,1,0:T(8,128)(2,1)S(1)}, u32[]{:S(2)}, u32[]{:S(2)}) collective-permute-start(bf16[2,128,384]{2,1,0:T(8,128)(2,1)S(1)} %get-tuple-element.75), channel_id=1, source_target_pairs={{0,2},{1,3},{2,0},{3,1},{4,6},{5,7},{6,4},{7,5},{8,10},{9,11},{10,... | collective-permute-start | bytes 589832 | tf_op jit(solution)/shard_map/ppermute | solution.py:435
  52.3 6.8 %collective-permute-start.16 = (bf16[2,128,384]{2,1,0:T(8,128)(2,1)S(1)}, bf16[2,128,384]{2,1,0:T(8,128)(2,1)S(1)}, u32[]{:S(2)}, u32[]{:S(2)}) collective-permute-start(bf16[2,128,384]{2,1,0:T(8,128)(2,1)S(1)} %get-tuple-element.71.refs_4_), channel_id=1, source_target_pairs={{0,1},{1,0},{2,3},{3,2},{4,5},{5,4},{6,7},{7,6},{8,9},{9,8},{10,11... | collective-permute-start | bytes 589832 | tf_op jit(solution)/shard_map/ppermute | solution.py:434
  58.6 1.4 %collective-permute-start.15 = (bf16[2,128,384]{2,1,0:T(8,128)(2,1)S(1)}, bf16[2,128,384]{2,1,0:T(8,128)(2,1)S(1)}, u32[]{:S(2)}, u32[]{:S(2)}) collective-permute-start(bf16[2,128,384]{2,1,0:T(8,128)(2,1)S(1)} %collective-permute-done.8.refs_2_), channel_id=1, source_target_pairs={{0,1},{1,0},{2,3},{3,2},{4,5},{5,4},{6,7},{7,6},{8,9},{9,8},{10,11... | collective-permute-start | bytes 589832 | tf_op jit(solution)/shard_map/ppermute | solution.py:434
  58.6 1.7 %collective-permute-start.18 = (bf16[2,128,384]{2,1,0:T(8,128)(2,1)S(1)}, bf16[2,128,384]{2,1,0:T(8,128)(2,1)S(1)}, u32[]{:S(2)}, u32[]{:S(2)}) collective-permute-start(bf16[2,128,384]{2,1,0:T(8,128)(2,1)S(1)} %collective-permute-done.17.refs_6_), channel_id=1, source_target_pairs={{0,1},{1,0},{2,3},{3,2},{4,5},{5,4},{6,7},{7,6},{8,9},{9,8},{10,11... | collective-permute-start | bytes 589832 | tf_op jit(solution)/shard_map/ppermute | solution.py:434

commit v4 on v3

--- a/solution.py
+++ b/solution.py
@@ -178,19 +178,19 @@
 def outer_kernel(place_ref, own_ref, far_ref, field_ref, even_ref, odd_ref, done):
     odd_place = place_ref[1] == 1
     cases, parts, _, half = own_ref.shape
+    own_copy = pltpu.make_async_copy(own_ref, field_ref.at[:, :, :, pl.ds(0, half)], done.at[cases])
     copies = [
-        pltpu.make_async_copy(ref, field_ref.at[:, :, :, pl.ds(q * half, half)], done.at[q])
-        for q, ref in ((1, far_ref), (0, own_ref))
+        pltpu.make_async_copy(far_ref.at[m], field_ref.at[m, :, :, pl.ds(half, half)], done.at[m]) for m in range(cases)
     ]
-    for copy in copies:
+    for copy in [*copies, own_copy]:
         copy.start()
-    copies[0].wait()
     for m in range(cases):
+        copies[m].wait()
         for c in range(parts):
             low, high = field_ref[m, c, :TILE, half:], field_ref[m, c, TILE:, half:]
             even_ref[m, c] = jnp.where(odd_place, low, high)
             odd_ref[m, c] = jnp.where(odd_place, high, low)
-    copies[1].wait()
+    own_copy.wait()
 
 
 def gather_outer(place, own, far):
@@ -200,7 +200,7 @@
         outer_kernel,
         in_specs=[SMEM, ANY, ANY],
         out_specs=[VMEM] * 3,
-        scratch_shapes=[pltpu.SemaphoreType.DMA((2,))],
+        scratch_shapes=[pltpu.SemaphoreType.DMA((cases + 1,))],
         out_shape=[pltpu.VMEM((cases, parts, height, 2 * half), jnp.bfloat16), edge, edge],
         compiler_params=params(4),
         cost_estimate=SHORT,
@@ -249,23 +249,32 @@
     edge_refs = refs[: (len(refs) - 5) // 2]
     coupling_ref, _, mixed, *staged_refs, field_ref, done = refs[len(edge_refs) :]
     half = own_ref.shape[3]
-    pairs = [
-        (far_ref, field_ref.at[:, :, :, pl.ds(half, half)]),
-        (own_ref, field_ref.at[:, :, :, pl.ds(0, half)]),
-        *zip(edge_refs, staged_refs),
+    cases = field_ref.shape[0]
+
+    def parts_of(m):
+        return [
+            pltpu.make_async_copy(ref.at[m], field_ref.at[m, :, :, pl.ds(q * half, half)], done.at[2 * m + q])
+            for q, ref in enumerate((own_ref, far_ref))
+        ]
+
+    for m in range(cases):
+        for copy in parts_of(m):
+            copy.start()
+    copies = [
+        pltpu.make_async_copy(source, target, done.at[2 * cases + i])
+        for i, (source, target) in enumerate(zip(edge_refs, staged_refs))
     ]
-    copies = [pltpu.make_async_copy(source, target, done.at[i]) for i, (source, target) in enumerate(pairs)]
     for copy in copies:
         copy.start()
-    for copy in copies[:2]:
-        copy.wait()
 
     def one_case(m, carry):
+        for copy in parts_of(m):
+            copy.wait()
         mix([field_ref[m, c] for c in range(2)], coupling_ref, range(1, mixed.shape[1] - 3), mixed.at[m])
         return carry
 
     lax.fori_loop(0, field_ref.shape[0], one_case, 0)
-    for copy in copies[2:]:
+    for copy in copies:
         copy.wait()
 
 
@@ -279,7 +288,7 @@
         out_specs=[VMEM] * (1 + count),
         scratch_shapes=[
             pltpu.VMEM((cases, parts, height, terms), jnp.bfloat16),
-            pltpu.SemaphoreType.DMA((2 + count,)),
+            pltpu.SemaphoreType.DMA((2 * cases + count,)),
         ],
         out_shape=[pltpu.VMEM(mixed.shape, mixed.dtype)] + [pltpu.VMEM(v.shape, v.dtype) for v in edges],
         input_output_aliases={3 + count: 0},

time: 63.3 us -> 63.2 us (level)
  no operation moved by 1% of the time
where the time goes in v4:
time: 63.2 us; the launch traced here: 62.5 us
  Pallas kernels  37.8 us (60%)
  starting transfers between devices  15 us (24%)
  waiting for transfers between devices  9.22 us (15%)
    pallas_call x5, Pallas kernels, apply_tiles(): pl.pallas_call(functools.partial(tiles_apply_kernel, m, quarters), in_spe...  13.9 us
    ppermute x6, starting transfers between devices, body(): across = lambda v: lax.ppermute(v, 'chaos', [(i, i ^ 2) for i in range(4)])  7.62 us
    pallas_call x1, Pallas kernels, pack(): pl.pallas_call(pack_kernel, in_specs=[SMEM, ANY, ANY], out_specs=[HBM] *...  4.62 us
    pallas_call x1, Pallas kernels, dense_coupling(): pl.pallas_call(coupling_kernel, in_specs=[SMEM, ANY, ANY], out_specs=VMEM...  4.59 us
    ppermute x6, waiting for transfers between devices, body(): across = lambda v: lax.ppermute(v, 'chaos', [(i, i ^ 2) for i in range(4)])  4.57 us
    pallas_call x2, Pallas kernels, unpack(): pl.pallas_call(kernel, in_specs=specs, out_specs=ANY, scratch_shapes=[plt...  4.26 us
    ppermute x2, starting transfers between devices, swap(): lax.ppermute(even, 'space', even_pairs)  3.96 us
    ppermute x2, waiting for transfers between devices, swap(): lax.ppermute(even, 'space', even_pairs)  3.42 us
  transfers between devices with their start and end apart: 19, of which 7 were waited for; matrix products, arithmetic and copies ran while one was open for 0% of the time, Pallas kernels for 45%

profile of v4, /device:TPU:0, one launch (start us, length us, event | category | flops | bytes accessed | tf_op | source)
XLA Modules:
  0.0 62.5 jit_solution(13244417687797866575)
XLA Ops:
  0.0 0.5 collective-permute-start
  0.5 0.1 pad_add_fusion._.place_ref
  0.5 3.2 %shard_map.55.refs_5_ = bf16[4,3,192,768]{3,2,1,0:T(8,128)(2,1)S(1)} custom-call(s32[2]{0:T(128)S(1)} %pad_add_fusion._.place_ref, bf16[4,3,8,2,96,96]{5,4,3,2,1,0:T(8,128)(2,1)} %tiles_hbm_ref.1), custom_call_target="tpu_custom_call" | custom-call | flops 1000 | bytes 1000 | tf_op jit(solution)/shard_map/pallas_call | solution.py:100
  3.7 0.0 collective-permute-done.near_ref
  3.8 4.6 %shard_map.56 = (bf16[4,2,192,128]{3,2,1,0:T(8,128)(2,1)}, bf16[4,2,192,128]{3,2,1,0:T(8,128)(2,1)}, bf16[4,2,192,128]{3,2,1,0:T(8,128)(2,1)}, bf16[4,2,192,128]...) custom-call(s32[2]{0:T(128)S(1)} %pad_add_fusion._.place_ref, ...), custom_call_target="tpu_custom_call" | custom-call | flops 1000 | bytes 1000 | tf_op jit(solution)/shard_map/pallas_call | solution.py:162
  8.4 2.9 %collective-permute-start.4 = (bf16[4,2,192,128]{3,2,1,0:T(8,128)(2,1)}, bf16[4,2,192,128]{3,2,1,0:T(8,128)(2,1)S(1)}, u32[]{:S(2)}, u32[]{:S(2)}) collective-permute-start(bf16[4,2,192,128]{3,2,1,0:T(8,128)(2,1)} %get-tuple-element.50), channel_id=1, source_target_pairs={{0,2},{1,3},{2,0},{3,1},{4,6},{5,7},{6,4},{7,5},{8,10},{9,11},{10,... | collective-permute-start | bytes 1179656 | tf_op jit(solution)/shard_map/ppermute | solution.py:444
  11.3 1.5 %collective-permute-start.2 = (bf16[4,2,96,128]{3,2,1,0:T(8,128)(2,1)}, bf16[4,2,96,128]{3,2,1,0:T(8,128)(2,1)S(1)}, u32[]{:S(2)}, u32[]{:S(2)}) collective-permute-start(bf16[4,2,96,128]{3,2,1,0:T(8,128)(2,1)} %get-tuple-element.44), channel_id=1, source_target_pairs={{0,4},{4,0},{8,12},{12,8},{16,20},{20,16},{24,28},{28,24},{1,5},{5... | collective-permute-start | bytes 589832 | tf_op jit(solution)/shard_map/ppermute | solution.py:214
  12.8 0.7 %collective-permute-start.3 = (bf16[4,2,96,128]{3,2,1,0:T(8,128)(2,1)}, bf16[4,2,96,128]{3,2,1,0:T(8,128)(2,1)S(1)}, u32[]{:S(2)}, u32[]{:S(2)}) collective-permute-start(bf16[4,2,96,128]{3,2,1,0:T(8,128)(2,1)} %get-tuple-element.47), channel_id=1, source_target_pairs={{4,8},{8,4},{12,16},{16,12},{20,24},{24,20},{5,9},{9,5},{13,17},{1... | collective-permute-start | bytes 589832 | tf_op jit(solution)/shard_map/ppermute | solution.py:214
  13.4 4.6 %shard_map.57.coupling_ref.refs_2_.refs_4_ = bf16[8,256,256]{2,1,0:T(8,128)(2,1)S(1)} custom-call(s32[2]{0:T(128)S(1)} %pad_add_fusion._.place_ref, s32[8,32,256]{2,1,0:T(8,128)} %bitcast.5, bf16[8,32,256]{2,1,0:T(8,128)(2,1)} %bitcast.6), custom_call_target="tpu_custom_call" | custom-call | flops 1000 | bytes 1000 | tf_op jit(solution)/shard_map/pallas_call | solution.py:69
  18.0 0.6 collective-permute-start.1
  18.6 0.0 collective-permute-done.3.refs_1_
  18.6 2.9 %collective-permute-done.2.refs_0_ = bf16[4,2,96,128]{3,2,1,0:T(8,128)(2,1)S(1)} collective-permute-done((bf16[4,2,96,128]{3,2,1,0:T(8,128)(2,1)}, bf16[4,2,96,128]{3,2,1,0:T(8,128)(2,1)S(1)}, u32[]{:S(2)}, u32[]{:S(2)}) %collective-permute-start.2) | collective-permute-done | bytes 196640 | tf_op jit(solution)/shard_map/ppermute | solution.py:214
  21.5 0.0 collective-permute-done.4.far_ref
  21.5 1.6 %shard_map.58 = (bf16[4,2,192,256]{3,2,1,0:T(8,128)(2,1)S(1)}, bf16[4,2,96,128]{3,2,1,0:T(8,128)(2,1)S(1)}, bf16[4,2,96,128]{3,2,1,0:T(8,128)(2,1)S(1)}) custom-call(s32[2]{0:T(128)S(1)} %pad_add_fusion._.place_ref, bf16[4,2,192,128]{3,2,1,0:T(8,128)(2,1)} %get-tuple-element.49.own_ref, bf16[4,2,192,128]{3,2,1,0:T(8,128)(2,1)S(1)} %collective-permute-done.4.far_ref), custom_call_target="tpu_custom_call" | custom-call | flops 1000 | bytes 1000 | tf_op jit(solution)/shard_map/pallas_call | solution.py:199
  23.2 2.4 %collective-permute-start.5 = (bf16[4,2,96,128]{3,2,1,0:T(8,128)(2,1)S(1)}, bf16[4,2,96,128]{3,2,1,0:T(8,128)(2,1)S(1)}, u32[]{:S(2)}, u32[]{:S(2)}) collective-permute-start(bf16[4,2,96,128]{3,2,1,0:T(8,128)(2,1)S(1)} %get-tuple-element.54), channel_id=1, source_target_pairs={{0,4},{4,0},{8,12},{12,8},{16,20},{20,16},{24,28},{28,24},{1,5},{5... | collective-permute-start | bytes 589832 | tf_op jit(solution)/shard_map/ppermute | solution.py:214
  25.6 0.8 %collective-permute-start.6 = (bf16[4,2,96,128]{3,2,1,0:T(8,128)(2,1)S(1)}, bf16[4,2,96,128]{3,2,1,0:T(8,128)(2,1)S(1)}, u32[]{:S(2)}, u32[]{:S(2)}) collective-permute-start(bf16[4,2,96,128]{3,2,1,0:T(8,128)(2,1)S(1)} %get-tuple-element.55), channel_id=1, source_target_pairs={{4,8},{8,4},{12,16},{16,12},{20,24},{24,20},{5,9},{9,5},{13,17},{1... | collective-permute-start | bytes 589832 | tf_op jit(solution)/shard_map/ppermute | solution.py:214
  26.5 0.0 copy-start
  26.5 2.3 %shard_map.59.refs_3_ = bf16[4,6,768,512]{3,2,1,0:T(8,128)(2,1)S(1)} custom-call(bf16[4,2,192,256]{3,2,1,0:T(8,128)(2,1)S(1)} %get-tuple-element.51.field_ref, bf16[8,256,256]{2,1,0:T(8,128)(2,1)S(1)} %shard_map.57.coupling_ref.refs_2_.refs_4_), custom_call_target="tpu_custom_call" | custom-call | flops 1000 | bytes 1000 | tf_op jit(solution)/shard_map/pallas_call | solution.py:238
  28.8 0.5 collective-permute-done.1.far_ref
  29.4 3.3 %shard_map.60 = (bf16[4,6,768,512]{3,2,1,0:T(8,128)(2,1)S(1)}, bf16[4,2,96,128]{3,2,1,0:T(8,128)(2,1)S(1)}, bf16[4,2,96,128]{3,2,1,0:T(8,128)(2,1)S(1)}) custom-call(bf16[4,2,192,128]{3,2,1,0:T(8,128)(2,1)} %get-tuple-element.42.own_ref, bf16[4,2,192,128]{3,2,1,0:T(8,128)(2,1)S(1)} %collective-permute-done.1.far_ref, ...), custom_call_target="tpu_custom_call", output_to_operand_aliasing={{0}: (5, {})} | custom-call | flops 1000 | bytes 1000 | tf_op jit(solution)/shard_map/pallas_call | solution.py:285
  32.7 0.5 collective-permute-done.5.refs_2_
  33.2 0.0 collective-permute-done.6.refs_3_
  33.2 0.0 copy-done
  33.2 3.2 %shard_map.61 = (bf16[2,128,384]{2,1,0:T(8,128)(2,1)S(1)}, bf16[2,128,384]{2,1,0:T(8,128)(2,1)S(1)}, bf16[4,6,768,512]{3,2,1,0:T(8,128)(2,1)S(1)}) custom-call(s32[2]{0:T(128)S(1)} %pad_add_fusion._.place_ref, s32[4,3]{1,0:T(4,128)S(1)} %copy-done, bf16[4,2,96,128]{3,2,1,0:T(8,128)(2,1)S(1)} %get-tuple-element.52.refs_0_, ...), custom_call_target="tpu_custom_call", output_to_operand_aliasing={{2}: (8, {})} | custom-call | flops 1000 | bytes 1000 | tf_op jit(solution)/shard_map/pallas_call | solution.py:344
  36.5 0.1 collective-permute-start.7
  36.6 1.3 %collective-permute-start.10 = (bf16[2,128,384]{2,1,0:T(8,128)(2,1)S(1)}, bf16[2,128,384]{2,1,0:T(8,128)(2,1)S(1)}, u32[]{:S(2)}, u32[]{:S(2)}) collective-permute-start(bf16[2,128,384]{2,1,0:T(8,128)(2,1)S(1)} %get-tuple-element.64), channel_id=1, source_target_pairs={{0,2},{1,3},{2,0},{3,1},{4,6},{5,7},{6,4},{7,5},{8,10},{9,11},{10,... | collective-permute-start | bytes 589832 | tf_op jit(solution)/shard_map/ppermute | solution.py:444
  37.9 3.2 %shard_map.62 = (bf16[2,128,384]{2,1,0:T(8,128)(2,1)S(1)}, bf16[2,128,384]{2,1,0:T(8,128)(2,1)S(1)}, bf16[4,6,768,512]{3,2,1,0:T(8,128)(2,1)S(1)}) custom-call(s32[2]{0:T(128)S(1)} %pad_add_fusion._.place_ref, s32[4,3]{1,0:T(4,128)S(1)} %copy-done, bf16[4,2,96,128]{3,2,1,0:T(8,128)(2,1)S(1)} %get-tuple-element.52.refs_0_, ...), custom_call_target="tpu_custom_call", output_to_operand_aliasing={{2}: (8, {})} | custom-call | flops 1000 | bytes 1000 | tf_op jit(solution)/shard_map/pallas_call | solution.py:344
  41.1 0.2 collective-permute-start.12
  41.4 0.8 %collective-permute-start.11 = (bf16[2,128,384]{2,1,0:T(8,128)(2,1)S(1)}, bf16[2,128,384]{2,1,0:T(8,128)(2,1)S(1)}, u32[]{:S(2)}, u32[]{:S(2)}) collective-permute-start(bf16[2,128,384]{2,1,0:T(8,128)(2,1)S(1)} %get-tuple-element.65), channel_id=1, source_target_pairs={{0,2},{1,3},{2,0},{3,1},{4,6},{5,7},{6,4},{7,5},{8,10},{9,11},{10,... | collective-permute-start | bytes 589832 | tf_op jit(solution)/shard_map/ppermute | solution.py:444
  42.1 0.0 collective-permute-done.7.refs_1_
  42.1 3.2 %shard_map.63 = (bf16[2,128,384]{2,1,0:T(8,128)(2,1)S(1)}, bf16[2,128,384]{2,1,0:T(8,128)(2,1)S(1)}, bf16[4,6,768,512]{3,2,1,0:T(8,128)(2,1)S(1)}) custom-call(s32[2]{0:T(128)S(1)} %pad_add_fusion._.place_ref, s32[4,3]{1,0:T(4,128)S(1)} %copy-done, bf16[4,2,96,128]{3,2,1,0:T(8,128)(2,1)S(1)} %get-tuple-element.52.refs_0_, ...), custom_call_target="tpu_custom_call", output_to_operand_aliasing={{2}: (8, {})} | custom-call | flops 1000 | bytes 1000 | tf_op jit(solution)/shard_map/pallas_call | solution.py:344
  45.4 0.1 collective-permute-start.9
  45.5 0.0 collective-permute-done.10.refs_2_
  45.5 0.0 collective-permute-done.12.refs_5_
  45.5 1.3 %collective-permute-start.8 = (bf16[2,128,384]{2,1,0:T(8,128)(2,1)S(1)}, bf16[2,128,384]{2,1,0:T(8,128)(2,1)S(1)}, u32[]{:S(2)}, u32[]{:S(2)}) collective-permute-start(bf16[2,128,384]{2,1,0:T(8,128)(2,1)S(1)} %get-tuple-element.61), channel_id=1, source_target_pairs={{0,2},{1,3},{2,0},{3,1},{4,6},{5,7},{6,4},{7,5},{8,10},{9,11},{10,... | collective-permute-start | bytes 589832 | tf_op jit(solution)/shard_map/ppermute | solution.py:444
  46.8 2.4 %shard_map.64 = (bf16[2,128,384]{2,1,0:T(8,128)(2,1)S(1)}, bf16[4,6,768,512]{3,2,1,0:T(8,128)(2,1)S(1)}) custom-call(s32[2]{0:T(128)S(1)} %pad_add_fusion._.place_ref, s32[4,3]{1,0:T(4,128)S(1)} %copy-done, bf16[4,2,96,128]{3,2,1,0:T(8,128)(2,1)S(1)} %get-tuple-element.52.refs_0_, ...), custom_call_target="tpu_custom_call", output_to_operand_aliasing={{1}: (8, {})} | custom-call | flops 1000 | bytes 1000 | tf_op jit(solution)/shard_map/pallas_call | solution.py:344
  49.2 0.0 collective-permute-done.11.refs_6_
  49.2 0.0 collective-permute-done.9.refs_1_
  49.2 1.8 %shard_map.65 = (bf16[2,128,384]{2,1,0:T(8,128)(2,1)S(1)}, bf16[4,6,768,512]{3,2,1,0:T(8,128)(2,1)S(1)}) custom-call(s32[2]{0:T(128)S(1)} %pad_add_fusion._.place_ref, s32[4,3]{1,0:T(4,128)S(1)} %copy-done, bf16[4,2,96,128]{3,2,1,0:T(8,128)(2,1)S(1)} %get-tuple-element.52.refs_0_, ...), custom_call_target="tpu_custom_call", output_to_operand_aliasing={{1}: (8, {})} | custom-call | flops 1000 | bytes 1000 | tf_op jit(solution)/shard_map/pallas_call | solution.py:344
  51.0 0.2 collective-permute-start.13
  51.2 0.4 collective-permute-start.14
  51.6 0.8 %collective-permute-start.17 = (bf16[2,128,384]{2,1,0:T(8,128)(2,1)S(1)}, bf16[2,128,384]{2,1,0:T(8,128)(2,1)S(1)}, u32[]{:S(2)}, u32[]{:S(2)}) collective-permute-start(bf16[2,128,384]{2,1,0:T(8,128)(2,1)S(1)} %get-tuple-element.75), channel_id=1, source_target_pairs={{0,2},{1,3},{2,0},{3,1},{4,6},{5,7},{6,4},{7,5},{8,10},{9,11},{10,... | collective-permute-start | bytes 589832 | tf_op jit(solution)/shard_map/ppermute | solution.py:444
  52.3 0.0 collective-permute-start.16
  52.3 0.5 collective-permute-done.8.refs_2_
  52.8 0.0 collective-permute-done.13.refs_3_
  52.8 0.0 collective-permute-done.14.refs_7_
  52.8 2.1 %shard_map.66.refs_8_ = f32[128,16,384]{2,1,0:T(8,128)} custom-call(s32[2]{0:T(128)S(1)} %pad_add_fusion._.place_ref, bf16[2,128,384]{2,1,0:T(8,128)(2,1)S(1)} %get-tuple-element.57.refs_0_, bf16[2,128,384]{2,1,0:T(8,128)(2,1)S(1)} %collective-permute-done.7.refs_1_, bf16[2,128,384]{2,1,0:T(8,128)(2,1)S(1)} %collective-permute-done.10.refs_2_, ...), custom_call_target="tpu_custom_call" | custom-call | flops 1000 | bytes 1000 | tf_op jit(solution)/shard_map/pallas_call | solution.py:397
  54.9 3.5 %collective-permute-done.17.refs_6_ = bf16[2,128,384]{2,1,0:T(8,128)(2,1)S(1)} collective-permute-done((bf16[2,128,384]{2,1,0:T(8,128)(2,1)S(1)}, bf16[2,128,384]{2,1,0:T(8,128)(2,1)S(1)}, u32[]{:S(2)}, u32[]{:S(2)}) %collective-permute-start.17) | collective-permute-done | bytes 196640 | tf_op jit(solution)/shard_map/ppermute | solution.py:444
  58.5 0.0 collective-permute-start.15
  58.5 0.5 collective-permute-start.18
  59.0 0.0 collective-permute-done.16.refs_5_
  59.0 0.9 %collective-permute-done.15.refs_3_ = bf16[2,128,384]{2,1,0:T(8,128)(2,1)S(1)} collective-permute-done((bf16[2,128,384]{2,1,0:T(8,128)(2,1)S(1)}, bf16[2,128,384]{2,1,0:T(8,128)(2,1)S(1)}, u32[]{:S(2)}, u32[]{:S(2)}) %collective-permute-start.15) | collective-permute-done | bytes 196640 | tf_op jit(solution)/shard_map/ppermute | solution.py:443
  59.9 0.3 collective-permute-done.18.refs_7_
  60.2 2.1 %shard_map.67 = f32[128,16,384]{2,1,0:T(8,128)} custom-call(s32[2]{0:T(128)S(1)} %pad_add_fusion._.place_ref, bf16[2,128,384]{2,1,0:T(8,128)(2,1)S(1)} %get-tuple-element.63.refs_0_, bf16[2,128,384]{2,1,0:T(8,128)(2,1)S(1)} %collective-permute-done.9.refs_1_, ...), custom_call_target="tpu_custom_call", output_to_operand_aliasing={{}: (9, {})} | custom-call | flops 1000 | bytes 1000 | tf_op jit(solution)/shard_map/pallas_call | solution.py:397
Async XLA Ops:
  0.0 3.7 %collective-permute-start = (bf16[64,2,16,384]{3,2,1,0:T(8,128)(2,1)}, bf16[64,2,16,384]{3,2,1,0:T(8,128)(2,1)S(1)}, u32[]{:S(2)}, u32[]{:S(2)}) collective-permute-start(bf16[64,2,16,384]{3,2,1,0:T(8,128)(2,1)} %own_ref.1), channel_id=1, source_target_pairs={{0,1},{1,0},{2,3},{3,2},{4,5},{5,4},{6,7},{7,6},{8,9},{9,8},{10,11... | collective-permute-start | bytes 4718600 | tf_op jit(solution)/shard_map/ppermute | solution.py:443
  8.4 13.2 %collective-permute-start.4 = (bf16[4,2,192,128]{3,2,1,0:T(8,128)(2,1)}, bf16[4,2,192,128]{3,2,1,0:T(8,128)(2,1)S(1)}, u32[]{:S(2)}, u32[]{:S(2)}) collective-permute-start(bf16[4,2,192,128]{3,2,1,0:T(8,128)(2,1)} %get-tuple-element.50), channel_id=1, source_target_pairs={{0,2},{1,3},{2,0},{3,1},{4,6},{5,7},{6,4},{7,5},{8,10},{9,11},{10,... | collective-permute-start | bytes 1179656 | tf_op jit(solution)/shard_map/ppermute | solution.py:444
  11.3 10.3 %collective-permute-start.2 = (bf16[4,2,96,128]{3,2,1,0:T(8,128)(2,1)}, bf16[4,2,96,128]{3,2,1,0:T(8,128)(2,1)S(1)}, u32[]{:S(2)}, u32[]{:S(2)}) collective-permute-start(bf16[4,2,96,128]{3,2,1,0:T(8,128)(2,1)} %get-tuple-element.44), channel_id=1, source_target_pairs={{0,4},{4,0},{8,12},{12,8},{16,20},{20,16},{24,28},{28,24},{1,5},{5... | collective-permute-start | bytes 589832 | tf_op jit(solution)/shard_map/ppermute | solution.py:214
  12.8 5.9 %collective-permute-start.3 = (bf16[4,2,96,128]{3,2,1,0:T(8,128)(2,1)}, bf16[4,2,96,128]{3,2,1,0:T(8,128)(2,1)S(1)}, u32[]{:S(2)}, u32[]{:S(2)}) collective-permute-start(bf16[4,2,96,128]{3,2,1,0:T(8,128)(2,1)} %get-tuple-element.47), channel_id=1, source_target_pairs={{4,8},{8,4},{12,16},{16,12},{20,24},{24,20},{5,9},{9,5},{13,17},{1... | collective-permute-start | bytes 589832 | tf_op jit(solution)/shard_map/ppermute | solution.py:214
  18.0 11.3 %collective-permute-start.1 = (bf16[4,2,192,128]{3,2,1,0:T(8,128)(2,1)}, bf16[4,2,192,128]{3,2,1,0:T(8,128)(2,1)S(1)}, u32[]{:S(2)}, u32[]{:S(2)}) collective-permute-start(bf16[4,2,192,128]{3,2,1,0:T(8,128)(2,1)} %get-tuple-element.46), channel_id=1, source_target_pairs={{0,2},{1,3},{2,0},{3,1},{4,6},{5,7},{6,4},{7,5},{8,10},{9,11},{10,... | collective-permute-start | bytes 1179656 | tf_op jit(solution)/shard_map/ppermute | solution.py:444
  23.2 10.0 %collective-permute-start.5 = (bf16[4,2,96,128]{3,2,1,0:T(8,128)(2,1)S(1)}, bf16[4,2,96,128]{3,2,1,0:T(8,128)(2,1)S(1)}, u32[]{:S(2)}, u32[]{:S(2)}) collective-permute-start(bf16[4,2,96,128]{3,2,1,0:T(8,128)(2,1)S(1)} %get-tuple-element.54), channel_id=1, source_target_pairs={{0,4},{4,0},{8,12},{12,8},{16,20},{20,16},{24,28},{28,24},{1,5},{5... | collective-permute-start | bytes 589832 | tf_op jit(solution)/shard_map/ppermute | solution.py:214
  25.6 7.6 %collective-permute-start.6 = (bf16[4,2,96,128]{3,2,1,0:T(8,128)(2,1)S(1)}, bf16[4,2,96,128]{3,2,1,0:T(8,128)(2,1)S(1)}, u32[]{:S(2)}, u32[]{:S(2)}) collective-permute-start(bf16[4,2,96,128]{3,2,1,0:T(8,128)(2,1)S(1)} %get-tuple-element.55), channel_id=1, source_target_pairs={{4,8},{8,4},{12,16},{16,12},{20,24},{24,20},{5,9},{9,5},{13,17},{1... | collective-permute-start | bytes 589832 | tf_op jit(solution)/shard_map/ppermute | solution.py:214
  26.5 6.7 %copy-start = (s32[4,3]{1,0:T(4,128)S(1)}, s32[4,3]{1,0:T(4,128)}, u32[]{:S(2)}) copy-start(s32[4,3]{1,0:T(4,128)} %columns_ref.9) | copy-start | bytes 148
  36.5 5.7 %collective-permute-start.7 = (bf16[2,128,384]{2,1,0:T(8,128)(2,1)S(1)}, bf16[2,128,384]{2,1,0:T(8,128)(2,1)S(1)}, u32[]{:S(2)}, u32[]{:S(2)}) collective-permute-start(bf16[2,128,384]{2,1,0:T(8,128)(2,1)S(1)} %get-tuple-element.57.refs_0_), channel_id=1, source_target_pairs={{0,1},{1,0},{2,3},{3,2},{4,5},{5,4},{6,7},{7,6},{8,9},{9,8},{10,11... | collective-permute-start | bytes 589832 | tf_op jit(solution)/shard_map/ppermute | solution.py:443
  36.6 9.0 %collective-permute-start.10 = (bf16[2,128,384]{2,1,0:T(8,128)(2,1)S(1)}, bf16[2,128,384]{2,1,0:T(8,128)(2,1)S(1)}, u32[]{:S(2)}, u32[]{:S(2)}) collective-permute-start(bf16[2,128,384]{2,1,0:T(8,128)(2,1)S(1)} %get-tuple-element.64), channel_id=1, source_target_pairs={{0,2},{1,3},{2,0},{3,1},{4,6},{5,7},{6,4},{7,5},{8,10},{9,11},{10,... | collective-permute-start | bytes 589832 | tf_op jit(solution)/shard_map/ppermute | solution.py:444
  41.1 4.4 %collective-permute-start.12 = (bf16[2,128,384]{2,1,0:T(8,128)(2,1)S(1)}, bf16[2,128,384]{2,1,0:T(8,128)(2,1)S(1)}, u32[]{:S(2)}, u32[]{:S(2)}) collective-permute-start(bf16[2,128,384]{2,1,0:T(8,128)(2,1)S(1)} %get-tuple-element.67.refs_4_), channel_id=1, source_target_pairs={{0,1},{1,0},{2,3},{3,2},{4,5},{5,4},{6,7},{7,6},{8,9},{9,8},{10,11... | collective-permute-start | bytes 589832 | tf_op jit(solution)/shard_map/ppermute | solution.py:443
  41.4 7.8 %collective-permute-start.11 = (bf16[2,128,384]{2,1,0:T(8,128)(2,1)S(1)}, bf16[2,128,384]{2,1,0:T(8,128)(2,1)S(1)}, u32[]{:S(2)}, u32[]{:S(2)}) collective-permute-start(bf16[2,128,384]{2,1,0:T(8,128)(2,1)S(1)} %get-tuple-element.65), channel_id=1, source_target_pairs={{0,2},{1,3},{2,0},{3,1},{4,6},{5,7},{6,4},{7,5},{8,10},{9,11},{10,... | collective-permute-start | bytes 589832 | tf_op jit(solution)/shard_map/ppermute | solution.py:444
  45.4 3.8 %collective-permute-start.9 = (bf16[2,128,384]{2,1,0:T(8,128)(2,1)S(1)}, bf16[2,128,384]{2,1,0:T(8,128)(2,1)S(1)}, u32[]{:S(2)}, u32[]{:S(2)}) collective-permute-start(bf16[2,128,384]{2,1,0:T(8,128)(2,1)S(1)} %get-tuple-element.63.refs_0_), channel_id=1, source_target_pairs={{0,1},{1,0},{2,3},{3,2},{4,5},{5,4},{6,7},{7,6},{8,9},{9,8},{10,11... | collective-permute-start | bytes 589832 | tf_op jit(solution)/shard_map/ppermute | solution.py:443
  45.5 7.3 %collective-permute-start.8 = (bf16[2,128,384]{2,1,0:T(8,128)(2,1)S(1)}, bf16[2,128,384]{2,1,0:T(8,128)(2,1)S(1)}, u32[]{:S(2)}, u32[]{:S(2)}) collective-permute-start(bf16[2,128,384]{2,1,0:T(8,128)(2,1)S(1)} %get-tuple-element.61), channel_id=1, source_target_pairs={{0,2},{1,3},{2,0},{3,1},{4,6},{5,7},{6,4},{7,5},{8,10},{9,11},{10,... | collective-permute-start | bytes 589832 | tf_op jit(solution)/shard_map/ppermute | solution.py:444
  51.0 1.8 %collective-permute-start.13 = (bf16[2,128,384]{2,1,0:T(8,128)(2,1)S(1)}, bf16[2,128,384]{2,1,0:T(8,128)(2,1)S(1)}, u32[]{:S(2)}, u32[]{:S(2)}) collective-permute-start(bf16[2,128,384]{2,1,0:T(8,128)(2,1)S(1)} %collective-permute-done.10.refs_2_), channel_id=1, source_target_pairs={{0,1},{1,0},{2,3},{3,2},{4,5},{5,4},{6,7},{7,6},{8,9},{9,8},{10,11... | collective-permute-start | bytes 589832 | tf_op jit(solution)/shard_map/ppermute | solution.py:443
  51.2 1.6 %collective-permute-start.14 = (bf16[2,128,384]{2,1,0:T(8,128)(2,1)S(1)}, bf16[2,128,384]{2,1,0:T(8,128)(2,1)S(1)}, u32[]{:S(2)}, u32[]{:S(2)}) collective-permute-start(bf16[2,128,384]{2,1,0:T(8,128)(2,1)S(1)} %collective-permute-done.11.refs_6_), channel_id=1, source_target_pairs={{0,1},{1,0},{2,3},{3,2},{4,5},{5,4},{6,7},{7,6},{8,9},{9,8},{10,11... | collective-permute-start | bytes 589832 | tf_op jit(solution)/shard_map/ppermute | solution.py:443
  51.6 6.9 %collective-permute-start.17 = (bf16[2,128,384]{2,1,0:T(8,128)(2,1)S(1)}, bf16[2,128,384]{2,1,0:T(8,128)(2,1)S(1)}, u32[]{:S(2)}, u32[]{:S(2)}) collective-permute-start(bf16[2,128,384]{2,1,0:T(8,128)(2,1)S(1)} %get-tuple-element.75), channel_id=1, source_target_pairs={{0,2},{1,3},{2,0},{3,1},{4,6},{5,7},{6,4},{7,5},{8,10},{9,11},{10,... | collective-permute-start | bytes 589832 | tf_op jit(solution)/shard_map/ppermute | solution.py:444
  52.3 6.7 %collective-permute-start.16 = (bf16[2,128,384]{2,1,0:T(8,128)(2,1)S(1)}, bf16[2,128,384]{2,1,0:T(8,128)(2,1)S(1)}, u32[]{:S(2)}, u32[]{:S(2)}) collective-permute-start(bf16[2,128,384]{2,1,0:T(8,128)(2,1)S(1)} %get-tuple-element.71.refs_4_), channel_id=1, source_target_pairs={{0,1},{1,0},{2,3},{3,2},{4,5},{5,4},{6,7},{7,6},{8,9},{9,8},{10,11... | collective-permute-start | bytes 589832 | tf_op jit(solution)/shard_map/ppermute | solution.py:443
  58.5 1.4 %collective-permute-start.15 = (bf16[2,128,384]{2,1,0:T(8,128)(2,1)S(1)}, bf16[2,128,384]{2,1,0:T(8,128)(2,1)S(1)}, u32[]{:S(2)}, u32[]{:S(2)}) collective-permute-start(bf16[2,128,384]{2,1,0:T(8,128)(2,1)S(1)} %collective-permute-done.8.refs_2_), channel_id=1, source_target_pairs={{0,1},{1,0},{2,3},{3,2},{4,5},{5,4},{6,7},{7,6},{8,9},{9,8},{10,11... | collective-permute-start | bytes 589832 | tf_op jit(solution)/shard_map/ppermute | solution.py:443
  58.5 1.7 %collective-permute-start.18 = (bf16[2,128,384]{2,1,0:T(8,128)(2,1)S(1)}, bf16[2,128,384]{2,1,0:T(8,128)(2,1)S(1)}, u32[]{:S(2)}, u32[]{:S(2)}) collective-permute-start(bf16[2,128,384]{2,1,0:T(8,128)(2,1)S(1)} %collective-permute-done.17.refs_6_), channel_id=1, source_target_pairs={{0,1},{1,0},{2,3},{3,2},{4,5},{5,4},{6,7},{7,6},{8,9},{9,8},{10,11... | collective-permute-start | bytes 589832 | tf_op jit(solution)/shard_map/ppermute | solution.py:443
